TPU v7x, 32 devices: a whole 2x2x4 slice. The times are simulated.
32 devices in a mesh: seq: 16 (over z, y, x), head: 2 (over core).
Axes of the slice: x: 2, y: 2, z: 4, core: 2. Of those that a mesh axis runs over, the one named last changes fastest.
Arguments:
- tokens: bfloat16 [2048, 2048], P('seq'), may hold values from -6 to 6
- norm1_gain: float32 [2048], replicated, may hold values from 0.1 to 1.9
- mix_weight: bfloat16 [4, 2048, 2048], P(None, 'seq', 'head'), may hold values from -0.125 to 0.125
- conv_weight: float32 [3, 4, 2048], P(None, None, 'head'), may hold values from -3 to 3
- decay_gap: float32 [2048], P('head'), may hold values from 0.00024414062 to 0.05
- group_gain: float32 [2048], P('head'), may hold values from 0.1 to 1.9
- out_weight: bfloat16 [2048, 2048], P('head', 'seq'), may hold values from -0.25 to 0.25
- norm2_gain: float32 [2048], replicated, may hold values from 0.1 to 1.9
- up_pair: bfloat16 [2, 2048, 5632], P(None, 'seq', 'head'), may hold values from -0.125 to 0.125
- down_weight: bfloat16 [5632, 2048], P('head', 'seq'), may hold values from -0.078125 to 0.078125
- cotangent: bfloat16 [2048, 2048], P('seq'), may hold values from -6 to 6
Outputs:
- block_out: float32 [2048, 2048], P('seq')
- grad_tokens: float32 [2048, 2048], P('seq')
- grad_norm1: float32 [2048], replicated
- grad_mix: float32 [4, 2048, 2048], P(None, 'seq', 'head')
- grad_conv: float32 [3, 4, 2048], P(None, None, 'head')
- grad_gap: float32 [2048], P('head')
- grad_group: float32 [2048], P('head')
- grad_out: float32 [2048, 2048], P('head', 'seq')
- grad_norm2: float32 [2048], replicated
- grad_up: float32 [2, 2048, 5632], P(None, 'seq', 'head')
- grad_down: float32 [5632, 2048], P('head', 'seq')
- inverse_rms: float32 [2, 2048], P(None, 'seq')
All inputs are finite; a program needn't handle non-finite values.
Results may differ from a plain program's by a relative error of at most 0.012.
Values may be sent and summed in bfloat16 or wider, within the bound.
No kernel may reach another device: no remote copies, remote signals or barrier semaphores. Data moves between devices by JAX's collectives and lax.ppermute only.
A program may use at most 320 MiB of HBM per device.

v0:
```python
import jax
import jax.numpy as jnp
from jax import lax
from jax.sharding import PartitionSpec as P

HEAD_DIM = 128
SPAN = 64


EPS_TOKEN = 1e-06
EPS_GROUP = 1e-05
HIGH = lax.Precision.HIGHEST


def from_behind(value, axis, steps):
    count = lax.axis_size(axis)
    first, last = (max(0, -steps), min(count, count - steps))
    return lax.ppermute(value, axis, [(source, source + steps) for source in range(first, last)])


def carried_in(array, axis, combine, identity, reverse):
    peers, here = (lax.axis_size(axis), lax.axis_index(axis))
    everything = jax.tree.map(lambda part: lax.all_gather(part, axis), array)
    start = jax.tree.map(
        lambda part, zero: jnp.broadcast_to(jnp.asarray(zero, part.dtype), part.shape),
        array,
        identity,
    )

    def turn(k, before):
        at = peers - 1 - k if reverse else k
        reached = at > here if reverse else at < here
        new = combine(before, jax.tree.map(lambda part: part[at], everything))
        return jax.tree.map(lambda a, b: jnp.where(reached, a, b), new, before)

    return lax.fori_loop(0, peers, turn, start)


def silu_grad(inputs_val):
    sigmoid_val = jax.nn.sigmoid(inputs_val)
    return sigmoid_val * (1.0 + inputs_val * (1.0 - sigmoid_val))


def token_norm(token_rows, gain_vec):
    inverse = lax.rsqrt(jnp.mean(token_rows * token_rows, axis=-1, keepdims=True) + EPS_TOKEN)
    return (token_rows * inverse * gain_vec, inverse)


def token_norm_back(token_rows, inverse, gain_vec, grad_in):
    scaled = grad_in * gain_vec
    dot_term = jnp.mean(scaled * token_rows, axis=-1, keepdims=True)
    grad_rows = inverse * scaled - token_rows * inverse * inverse * inverse * dot_term
    grad_gain = jnp.sum(grad_in * token_rows * inverse, axis=0)
    return (grad_rows, grad_gain)


def convolve(extended, conv_taps):
    length = extended.shape[1] - 3
    total = conv_taps[:, 0][:, None] * extended[:, 3:]
    for delay_step in range(1, 4):
        total = (
            total
            + conv_taps[:, delay_step][:, None]
            * extended[:, 3 - delay_step : 3 - delay_step + length]
        )
    return total


def gates(convolved, decay_gap):
    queries = jax.nn.silu(convolved[0])
    open_share = 1.0 - jax.nn.sigmoid(convolved[1])
    log_forget = jnp.log(1.0 - decay_gap * open_share)
    key_rows = decay_gap * open_share
    return (queries, log_forget, key_rows, convolved[2])


def span_step(carry_state, pieces):
    queries, log_forget, key_rows, values = pieces
    running = jnp.cumsum(log_forget, axis=0)
    decayed_query = queries * jnp.exp(running)
    lifted_key = key_rows * jnp.exp(-running)
    scores = jnp.einsum("thd,shd->hts", decayed_query, lifted_key, precision=HIGH)
    causal = jnp.arange(SPAN)[:, None] >= jnp.arange(SPAN)[None, :]
    scores = jnp.where(causal[None], scores, 0.0)
    mixed_out = jnp.einsum("hts,she->the", scores, values, precision=HIGH)
    mixed_out = mixed_out + jnp.einsum("thd,hde->the", decayed_query, carry_state, precision=HIGH)
    final_log = running[-1]
    carried = key_rows * jnp.exp(final_log[None] - running)
    carry_state = jnp.exp(final_log)[:, :, None] * carry_state + jnp.einsum(
        "thd,the->hde", carried, values, precision=HIGH
    )
    return (carry_state, mixed_out)


def local_mix(queries, log_forget, key_rows, values, state_in):
    length, heads_here, head_width = queries.shape
    blocks = length // SPAN

    def blocked(array):
        return array.reshape(blocks, SPAN, heads_here, head_width)

    state_out, mixed_out = lax.scan(
        jax.checkpoint(span_step),
        state_in,
        (blocked(queries), blocked(log_forget), blocked(key_rows), blocked(values)),
    )
    return (mixed_out.reshape(length, heads_here, head_width), state_out)


def running_log(log_forget):
    length = log_forget.shape[0]
    blocked = log_forget.reshape((length // SPAN, SPAN) + log_forget.shape[1:])
    inside = jnp.cumsum(blocked, axis=1)
    totals = inside[:, -1]
    before = jnp.cumsum(totals, axis=0) - totals
    return (inside + before[:, None]).reshape(log_forget.shape)


def group_gate(mixed_out, gate_rows, group_gain):
    inverse = lax.rsqrt(jnp.mean(mixed_out * mixed_out, axis=-1, keepdims=True) + EPS_GROUP)
    normed = (mixed_out * inverse).reshape(gate_rows.shape)
    return normed * group_gain * jax.nn.silu(gate_rows)


def split_heads(array):
    return array.reshape(array.shape[0], -1, HEAD_DIM)


def merge_heads(array):
    return array.reshape(array.shape[0], -1)


def combine_state(earlier, later):
    return (earlier[0] * later[0], later[0][..., None] * earlier[1] + later[1])


def head_total(partial_sum):
    share = lax.psum_scatter(partial_sum, "head", scatter_dimension=1, tiled=True)
    return lax.all_gather(share, "head", axis=1, tiled=True)


def shards(
    tokens,
    norm1_gain,
    mix_weight,
    conv_weight,
    decay_gap,
    group_gain,
    out_weight,
    norm2_gain,
    up_pair,
    down_weight,
    cotangent,
):
    mix_full, up_full, out_full, down_full = (
        lax.all_gather(mix_weight, "seq", axis=1, tiled=True),
        lax.all_gather(up_pair, "seq", axis=1, tiled=True),
        lax.all_gather(out_weight, "seq", axis=1, tiled=True),
        lax.all_gather(down_weight, "seq", axis=1, tiled=True),
    )
    token_rows = tokens.astype(jnp.float32)
    normed1, inverse1 = token_norm(token_rows, norm1_gain)
    normed1_low = normed1.astype(jnp.bfloat16)
    projected = jnp.einsum(
        "td,jdc->jtc", normed1_low, mix_full, preferred_element_type=jnp.float32
    ).astype(jnp.bfloat16)
    length = projected.shape[1]
    earlier_rows = from_behind(projected[:3, length - 3 :], "seq", 1)
    extended = jnp.concatenate([earlier_rows, projected[:3]], axis=1).astype(jnp.float32)
    convolved, conv_back = jax.vjp(convolve, extended, conv_weight)
    (queries, log_forget, key_rows, values), gate_back = jax.vjp(gates, convolved, decay_gap)
    query_heads = split_heads(queries)
    forget_heads = split_heads(log_forget)
    key_heads = split_heads(key_rows)
    value_heads = split_heads(values)
    log_total = running_log(forget_heads)
    last_log = log_total[-1]
    decay_dev = jnp.exp(last_log)
    own_state = jnp.einsum(
        "thd,the->hde", key_heads * jnp.exp(last_log[None] - log_total), value_heads, precision=HIGH
    )
    identity = (jnp.ones_like(decay_dev), jnp.zeros_like(own_state))
    prior_decay, state_in = carried_in(
        (decay_dev, own_state), "seq", combine_state, identity, False
    )
    (mixed_out, state_end), mix_back = jax.vjp(
        local_mix, query_heads, forget_heads, key_heads, value_heads, state_in
    )
    gate_rows = projected[3].astype(jnp.float32)
    gated, group_back = jax.vjp(group_gate, mixed_out, gate_rows, group_gain)
    gated_low = gated.astype(jnp.bfloat16)
    hidden = token_rows + head_total(
        jnp.dot(gated_low, out_full, preferred_element_type=jnp.float32)
    )
    normed2, inverse2 = token_norm(hidden, norm2_gain)
    normed2_low = normed2.astype(jnp.bfloat16)
    lifted = jnp.einsum("td,jdf->jtf", normed2_low, up_full, preferred_element_type=jnp.float32)
    gate_act = jax.nn.silu(lifted[0])
    inner_act = (gate_act * lifted[1]).astype(jnp.bfloat16)
    block_out = hidden + head_total(
        jnp.dot(inner_act, down_full, preferred_element_type=jnp.float32)
    )
    mix_again, up_again, out_again, down_again = (
        lax.all_gather(mix_weight, "seq", axis=1, tiled=True),
        lax.all_gather(up_pair, "seq", axis=1, tiled=True),
        lax.all_gather(out_weight, "seq", axis=1, tiled=True),
        lax.all_gather(down_weight, "seq", axis=1, tiled=True),
    )
    upstream = cotangent.astype(jnp.float32)
    grad_down = jnp.einsum("tf,td->fd", inner_act, cotangent, preferred_element_type=jnp.float32)
    grad_inner = jnp.einsum("td,fd->tf", cotangent, down_again, preferred_element_type=jnp.float32)
    grad_lifted = jnp.stack(
        [grad_inner * lifted[1] * silu_grad(lifted[0]), grad_inner * gate_act]
    ).astype(jnp.bfloat16)
    grad_up = jnp.einsum(
        "td,jtf->jdf", normed2_low, grad_lifted, preferred_element_type=jnp.float32
    )
    grad_normed2 = head_total(
        jnp.einsum("jtf,jdf->td", grad_lifted, up_again, preferred_element_type=jnp.float32)
    )
    grad_hidden_norm, grad_norm2 = token_norm_back(hidden, inverse2, norm2_gain, grad_normed2)
    grad_hidden = upstream + grad_hidden_norm
    grad_branch = grad_hidden.astype(jnp.bfloat16)
    grad_out = jnp.einsum("tc,td->cd", gated_low, grad_branch, preferred_element_type=jnp.float32)
    grad_gated = jnp.einsum("td,cd->tc", grad_branch, out_again, preferred_element_type=jnp.float32)
    grad_mixed, grad_gate_rows, grad_group = group_back(grad_gated)
    own_grad = jnp.einsum(
        "thd,the->hde", query_heads * jnp.exp(log_total), grad_mixed, precision=HIGH
    )
    later_decay, state_after = carried_in(
        (decay_dev, own_grad), "seq", combine_state, identity, True
    )
    grad_q, grad_f, grad_k, grad_v, grad_start = mix_back((grad_mixed, state_after))
    grad_convolved, grad_gap = gate_back(
        (merge_heads(grad_q), merge_heads(grad_f), merge_heads(grad_k), merge_heads(grad_v))
    )
    grad_extended, grad_conv = conv_back(grad_convolved)
    later_edge = from_behind(grad_extended[:, :3].astype(jnp.bfloat16), "seq", -1).astype(
        jnp.float32
    )
    edge_pad = jnp.concatenate(
        [jnp.zeros((3, length - 3, later_edge.shape[2]), jnp.float32), later_edge], axis=1
    )
    grad_conv_rows = grad_extended[:, 3:] + edge_pad
    grad_projected = jnp.concatenate([grad_conv_rows, grad_gate_rows[None]], axis=0).astype(
        jnp.bfloat16
    )
    grad_mix = jnp.einsum(
        "td,jtc->jdc", normed1_low, grad_projected, preferred_element_type=jnp.float32
    )
    grad_normed1 = head_total(
        jnp.einsum("jtc,jdc->td", grad_projected, mix_again, preferred_element_type=jnp.float32)
    )
    grad_rows1, grad_norm1 = token_norm_back(token_rows, inverse1, norm1_gain, grad_normed1)
    grad_tokens = grad_hidden + grad_rows1
    mix_part, up_part, out_part, down_part = (
        lax.psum_scatter(grad_mix, "seq", scatter_dimension=1, tiled=True),
        lax.psum_scatter(grad_up, "seq", scatter_dimension=1, tiled=True),
        lax.psum_scatter(grad_out, "seq", scatter_dimension=1, tiled=True),
        lax.psum_scatter(grad_down, "seq", scatter_dimension=1, tiled=True),
    )
    conv_total, gap_total, group_total, norm1_total, norm2_total = lax.psum(
        (grad_conv, grad_gap, grad_group, grad_norm1, grad_norm2), "seq"
    )
    inverse_rms = jnp.stack([inverse1[:, 0], inverse2[:, 0]])
    return (
        block_out,
        grad_tokens,
        norm1_total,
        mix_part,
        conv_total,
        gap_total,
        group_total,
        out_part,
        norm2_total,
        up_part,
        down_part,
        inverse_rms,
    )


def solution(mesh):
    in_specs = (
        P("seq", None),
        P(),
        P(None, "seq", "head"),
        P(None, None, "head"),
        P("head"),
        P("head"),
        P("head", "seq"),
        P(),
        P(None, "seq", "head"),
        P("head", "seq"),
        P("seq", None),
    )
    out_specs = (
        P("seq", None),
        P("seq", None),
        P(),
        P(None, "seq", "head"),
        P(None, None, "head"),
        P("head"),
        P("head"),
        P("head", "seq"),
        P(),
        P(None, "seq", "head"),
        P("head", "seq"),
        P(None, "seq"),
    )
    return jax.shard_map(shards, mesh=mesh, in_specs=in_specs, out_specs=out_specs, check_vma=False)
```

profile of v0, /device:TPU:18, one launch (start us, length us, event | category | flops | bytes accessed | tf_op | source)
XLA Modules:
  0.0 3646.0 jit_solution(11405974941305117379)
XLA Ops:
  9.8 192.6 %all-gather.13.cloned.1.call-done = bf16[4,2048,1024]{2,1,0:T(8,128)(2,1)} async-done(((bf16[4,128,1024]{2,1,0:T(8,128)(2,1)}), bf16[4,2048,1024]{2,1,0:T(8,128)(2,1)}) %all-gather.13.cloned.1.call-update) | async-done | bytes 16777232 | tf_op jit(solution)/shard_map/all_gather | solution.py:156
  219.6 12.9 fusion.119
  236.7 31.3 all_gather.47
  271.1 76.9 %all-gather.29.cloned.1.call-done = f32[128,128,128]{2,1,0:T(8,128)} async-done(((f32[8,128,128]{2,1,0:T(8,128)}), f32[128,128,128]{2,1,0:T(8,128)}) %all-gather.29.cloned.1.call-update) | async-done | bytes 8388624 | tf_op jit(solution)/shard_map/all_gather | solution.py:23
  348.0 22.8 while.70
  386.6 50.8 %all-gather.15.cloned.1.call-done = bf16[1024,2048]{1,0:T(8,128)(2,1)} async-done(((bf16[1024,128]{1,0:T(8,128)(2,1)}), bf16[1024,2048]{1,0:T(8,128)(2,1)}) %all-gather.15.cloned.1.call-update) | async-done | bytes 4194320 | tf_op jit(solution)/shard_map/all_gather | solution.py:158
  464.1 251.8 %all-gather.19.cloned.1.call-done = bf16[2,2048,2816]{2,1,0:T(8,128)(2,1)} async-done(((bf16[2,128,2816]{2,1,0:T(8,128)(2,1)}), bf16[2,2048,2816]{2,1,0:T(8,128)(2,1)}) %all-gather.19.cloned.1.call-update) | async-done | bytes 23068688 | tf_op jit(solution)/shard_map/all_gather | solution.py:157
  715.9 12.4 convolution_bitcast_fusion.6
  728.3 170.9 %all-gather.21.cloned.1.call-done = bf16[2816,2048]{1,0:T(8,128)(2,1)} async-done(((bf16[2816,128]{1,0:T(8,128)(2,1)}), bf16[2816,2048]{1,0:T(8,128)(2,1)}) %all-gather.21.cloned.1.call-update) | async-done | bytes 11534352 | tf_op jit(solution)/shard_map/all_gather | solution.py:159
  899.2 10.1 fusion.59
  910.4 12.9 convolution_bitcast_fusion.8
  932.3 12.5 reduce-scatter.11.cloned.1.call-done
  944.9 11.6 all-gather.25.cloned.1.call-done
  988.2 109.6 %all-gather.31.cloned.1.call-done = f32[128,128,128]{2,1,0:T(8,128)} async-done(((f32[8,128,128]{2,1,0:T(8,128)}), f32[128,128,128]{2,1,0:T(8,128)}) %all-gather.31.cloned.1.call-update) | async-done | bytes 8388624 | tf_op jit(solution)/shard_map/all_gather | solution.py:23
  1097.8 33.4 while.71
  1134.6 37.0 %while.68 = (s32[]{:T(128)}, f32[8,128,128]{2,1,0:T(8,128)S(1)}, f32[2,64,8,128]{3,2,1,0:T(8,128)}, f32[2,64,8,128]{3,2,1,0:T(8,128)}, f32[2,64,8,128]{3,2,1,0:T...) while((s32[]{:T(128)}, f32[8,128,128]{2,1,0:T(8,128)S(1)}, ...), condition=%wide.region_22.23_spmd, body=%wide.region_17.22_spmd.sunk | while | flops 665260032 | bytes 41624012 | solution.py:102
  1187.4 12.4 convolution_bitcast_fusion.7
  1222.8 13.4 convolution_bitcast_fusion.5
  1237.6 19.0 convolution_bitcast_fusion.4
  1275.7 57.5 %all-reduce.16.cloned.1.call-done = (f32[2048]{0:T(1024)}, f32[3,4,1024]{2,0,1:T(4,128)}, f32[1024]{0:T(1024)}, f32[1024]{0:T(1024)}, f32[2048]{0:T(1024)}) async-done(((f32[2048]{0:T(1024)}, f32[3,4,1024]{2,0,1:T(4,128)}, f32[1024]{0:T(1024)}, f32[1024]{0:T(1024)}, f32[2048]{0:T(1024)}), (f32[2048]{0:T(1024)}, f32[3,4,1024]{2,0,1:T(4,128)}, f32[1024]{0:T(1024)}, f32[1024]{0:T(1024)}, ...) | async-done | bytes 73744 | tf_op jit(solution)/shard_map/psum | solution.py:262
  1334.6 690.8 %reduce-scatter.17.cloned.1.call-done = f32[4,128,1024]{1,2,0:T(8,128)} async-done(((f32[4,2048,1024]{1,2,0:T(8,128)}), f32[4,128,1024]{1,2,0:T(8,128)}) %reduce-scatter.17.cloned.1.call-update) | async-done | bytes 2097168 | tf_op jit(solution)/shard_map/reduce_scatter | solution.py:257
  2028.3 942.6 %reduce-scatter.21.cloned.1.call-done = f32[2,128,2816]{1,2,0:T(8,128)} async-done(((f32[2,2048,2816]{1,2,0:T(8,128)}), f32[2,128,2816]{1,2,0:T(8,128)}) %reduce-scatter.21.cloned.1.call-update) | async-done | bytes 2883600 | tf_op jit(solution)/shard_map/reduce_scatter | solution.py:258
  2974.3 179.6 %reduce-scatter.19.cloned.1.call-done = f32[1024,128]{1,0:T(8,128)} async-done(((f32[1024,2048]{1,0:T(8,128)}), f32[1024,128]{1,0:T(8,128)}) %reduce-scatter.19.cloned.1.call-update) | async-done | bytes 524304 | tf_op jit(solution)/shard_map/reduce_scatter | solution.py:259
  3153.9 482.7 %reduce-scatter.23.cloned.1.call-done = f32[2816,128]{1,0:T(8,128)} async-done(((f32[2816,2048]{1,0:T(8,128)}), f32[2816,128]{1,0:T(8,128)}) %reduce-scatter.23.cloned.1.call-update) | async-done | bytes 1441808 | tf_op jit(solution)/shard_map/reduce_scatter | solution.py:260
  (449 shorter events, 283.1 us)
Async XLA Ops:
  7.2 195.2 %all-gather.13.cloned.1.call-start = ((), (), s32[]{:S(2)}) async-start(), calls=%async_computation.8 | async-start | bytes 17825792 | tf_op jit(solution)/shard_map/all_gather | solution.py:156
  7.9 340.0 %all-gather.29.cloned.1.call-start = ((), (), s32[]{:S(2)}) async-start(), calls=%async_computation.24 | async-start | bytes 8912896 | tf_op jit(solution)/shard_map/all_gather | solution.py:23
  210.7 5.7 collective-permute-start
  235.8 201.6 %all-gather.15.cloned.1.call-start = ((), (), s32[]{:S(2)}) async-start(), calls=%async_computation.9 | async-start | bytes 4456448 | tf_op jit(solution)/shard_map/all_gather | solution.py:158
  236.6 213.7 %reduce-scatter.9.cloned.1.call-start = ((), (), s32[]{:S(2)}) async-start(), calls=%async_computation.10 | async-start | bytes 1572864 | tf_op jit(solution)/shard_map/reduce_scatter | solution.py:138
  441.3 20.6 all-gather.17.cloned.1.call-start
  450.3 265.7 %all-gather.19.cloned.1.call-start = ((), (), s32[]{:S(2)}) async-start(), calls=%async_computation.12 | async-start | bytes 24510464 | tf_op jit(solution)/shard_map/all_gather | solution.py:157
  450.8 448.4 %all-gather.21.cloned.1.call-start = ((), (), s32[]{:S(2)}) async-start(), calls=%async_computation.13 | async-start | bytes 12255232 | tf_op jit(solution)/shard_map/all_gather | solution.py:159
  451.6 480.7 %reduce-scatter.13.cloned.1.call-start = ((), (), s32[]{:S(2)}) async-start(), calls=%async_computation.16 | async-start | bytes 1572864 | tf_op jit(solution)/shard_map/reduce_scatter | solution.py:138
  923.3 21.5 reduce-scatter.11.cloned.1.call-start
  930.5 26.0 all-gather.25.cloned.1.call-start
  932.3 36.1 all-gather.23.cloned.1.call-start
  944.8 153.0 %all-gather.31.cloned.1.call-start = ((), (), s32[]{:S(2)}) async-start(), calls=%async_computation.25 | async-start | bytes 8912896 | tf_op jit(solution)/shard_map/all_gather | solution.py:23
  985.0 223.9 %reduce-scatter.15.cloned.1.call-start = ((), (), s32[]{:S(2)}) async-start(), calls=%async_computation.18 | async-start | bytes 1572864 | tf_op jit(solution)/shard_map/reduce_scatter | solution.py:138
  1180.3 6.8 collective-permute-start.1
  1199.8 20.8 all-gather.27.cloned.1.call-start
  1209.0 124.2 %all-reduce.16.cloned.1.call-start = ((), (), s32[]{:S(2)}) async-start(), calls=%async_computation.26 | async-start | bytes 180224 | tf_op jit(solution)/shard_map/psum | solution.py:262
  1222.7 802.7 %reduce-scatter.17.cloned.1.call-start = ((), (), s32[]{:S(2)}) async-start(), calls=%async_computation.20 | async-start | bytes 35651584 | tf_op jit(solution)/shard_map/reduce_scatter | solution.py:257
  1236.2 1734.7 %reduce-scatter.21.cloned.1.call-start = ((), (), s32[]{:S(2)}) async-start(), calls=%async_computation.22 | async-start | bytes 49020928 | tf_op jit(solution)/shard_map/reduce_scatter | solution.py:258
  1256.6 1897.3 %reduce-scatter.19.cloned.1.call-start = ((), (), s32[]{:S(2)}) async-start(), calls=%async_computation.21 | async-start | bytes 8912896 | tf_op jit(solution)/shard_map/reduce_scatter | solution.py:259
  1262.4 2374.2 %reduce-scatter.23.cloned.1.call-start = ((), (), s32[]{:S(2)}) async-start(), calls=%async_computation.23 | async-start | bytes 24510464 | tf_op jit(solution)/shard_map/reduce_scatter | solution.py:260
  2028.3 1608.9 %copy-start.73 = (f32[1024]{0:T(1024)S(1)}, f32[1024]{0:T(1024)}, u32[]{:S(2)}) copy-start(f32[1024]{0:T(1024)} %get-tuple-element.1199) | copy-start | bytes 12292
  2028.3 1609.5 %copy-start.72 = (f32[1024]{0:T(1024)S(1)}, f32[1024]{0:T(1024)}, u32[]{:S(2)}) copy-start(f32[1024]{0:T(1024)} %get-tuple-element.1200) | copy-start | bytes 12292
  2028.3 1610.1 %copy-start.66 = (f32[2048]{0:T(1024)S(1)}, f32[2048]{0:T(1024)}, u32[]{:S(2)}) copy-start(f32[2048]{0:T(1024)} %get-tuple-element.1202) | copy-start | bytes 24580
  (87 other events, 3336.7 us)
Sparse Core Ops, SparseCore 0:
  10.8 191.5 all-gather.12
  235.9 111.9 all-gather.28
  350.7 86.6 all-gather.14
  441.4 8.7 reduce-scatter.8
  451.7 10.1 all-gather.16
  464.9 250.9 all-gather.18
  719.0 180.1 all-gather.20
  923.4 8.7 reduce-scatter.12
  935.1 9.6 reduce-scatter.10
  946.3 10.1 all-gather.24
  958.1 10.1 all-gather.22
  985.1 112.6 all-gather.30
  1199.9 8.9 reduce-scatter.14
  1210.3 10.1 all-gather.26
  1227.7 105.3 all-reduce.15
  1335.3 690.0 reduce-scatter.16
  2027.6 943.2 reduce-scatter.20
  2973.6 180.2 reduce-scatter.18
  3156.8 479.7 reduce-scatter.22
where the time goes:
time: 3660 us; the launch traced here: 3650 us
  waiting for transfers between devices  3290 us (90%)
  matrix products  140 us (4%)
  other arithmetic  105 us (3%)
  local copies, waits for them, and re-layouts  56.5 us (2%)
    reduce_scatter x1, waiting for transfers between devices, shards(): lax.psum_scatter(grad_up, 'seq', scatter_dimension=1, tiled=True)  943 us
    reduce_scatter x1, waiting for transfers between devices, shards(): lax.psum_scatter(grad_mix, 'seq', scatter_dimension=1, tiled=True)  691 us
    reduce_scatter x1, waiting for transfers between devices, shards(): lax.psum_scatter(grad_down, 'seq', scatter_dimension=1, tiled=True)  483 us
    all_gather x1, waiting for transfers between devices, shards(): lax.all_gather(up_pair, 'seq', axis=1, tiled=True)  252 us
    all_gather x1, waiting for transfers between devices, shards(): lax.all_gather(mix_weight, 'seq', axis=1, tiled=True)  193 us
    all_gather x2, waiting for transfers between devices, carried_in(): everything = jax.tree.map(lambda part: lax.all_gather(part, axis), array)  187 us
    reduce_scatter x1, waiting for transfers between devices, shards(): lax.psum_scatter(grad_out, 'seq', scatter_dimension=1, tiled=True)  180 us
    all_gather x1, waiting for transfers between devices, shards(): lax.all_gather(down_weight, 'seq', axis=1, tiled=True)  171 us
  transfers between devices with their start and end apart: 21, of which 21 were waited for; matrix products, arithmetic and copies ran while one was open for 3% of the time, Pallas kernels for 0%

commit v1 on v0

v1 whole, which is shorter than its diff:
```python
import functools

import jax
import jax.numpy as jnp
from jax import lax
from jax.experimental import pallas as pl
from jax.experimental.pallas import tpu as pltpu
from jax.sharding import PartitionSpec as P

HEAD_DIM = 128
CHUNK = 128
PAD = 8
EPS_TOKEN = 1e-06
EPS_GROUP = 1e-05
HIGH = lax.Precision.HIGHEST
F32 = jnp.float32
BF16 = jnp.bfloat16
VMEM_LIMIT = 48 * 1024 * 1024


def mul(a, b, ca, cb, precision=HIGH):
    return lax.dot_general(
        a, b, (((ca,), (cb,)), ((), ())), precision=precision, preferred_element_type=F32
    )


def dsilu(v):
    s = jax.nn.sigmoid(v)
    return s * (1.0 + v * (1.0 - s))


def triangle(lower):
    row = lax.broadcasted_iota(jnp.int32, (CHUNK, CHUNK), 0)
    col = lax.broadcasted_iota(jnp.int32, (CHUNK, CHUNK), 1)
    return (row >= col) if lower else (row <= col)


def forward_kernel(
    proj, halo, taps, gap, conv_out, query_out, key_out, total_out, state_out, local_out, last_out, rows
):
    length = proj.shape[0]
    rows[0:PAD, :] = halo[...].astype(F32)
    rows[PAD:, :] = proj[...].astype(F32)
    lower = triangle(True)
    ones = lower.astype(F32)
    state = jnp.zeros((HEAD_DIM, HEAD_DIM), F32)
    before = jnp.zeros((1, HEAD_DIM), F32)
    for c in range(length // CHUNK):
        at = c * CHUNK
        here = slice(at, at + CHUNK)
        conv = []
        for j in range(3):
            cols = slice(j * HEAD_DIM, (j + 1) * HEAD_DIM)
            total = taps[4 * j : 4 * j + 1, :] * rows[PAD + at : PAD + at + CHUNK, cols]
            for d in range(1, 4):
                total = total + taps[4 * j + d : 4 * j + d + 1, :] * rows[PAD + at - d : PAD + at - d + CHUNK, cols]
            conv.append(total)
            conv_out[here, cols] = total
        queries = conv[0] * jax.nn.sigmoid(conv[0])
        open_share = 1.0 - jax.nn.sigmoid(conv[1])
        keys = gap[...] * open_share
        log_forget = jnp.log(1.0 - keys)
        values = conv[2]
        running = mul(ones, log_forget, 1, 0)
        last = running[CHUNK - 1 : CHUNK, :]
        query = queries * jnp.exp(running)
        key = keys * jnp.exp(-running)
        carried = keys * jnp.exp(last - running)
        query_out[here, :] = query
        key_out[here, :] = key
        total_out[c : c + 1, :] = before
        state_out[c] = state
        scores = jnp.where(lower, mul(query, key, 1, 1), 0.0)
        local_out[here, :] = mul(scores, values, 1, 0) + mul(query, state, 1, 1)
        state = state * jnp.exp(last) + mul(values, carried, 0, 0)
        before = before + last
    last_out[0:HEAD_DIM, :] = state
    last_out[HEAD_DIM:, :] = jnp.broadcast_to(jnp.exp(before), (PAD, HEAD_DIM))


def gate_kernel(local, query, total, state, carry, gate, gain, mixed_out, state_out, gated_out):
    length = local.shape[0]
    start = carry[...]
    for c in range(length // CHUNK):
        here = slice(c * CHUNK, (c + 1) * CHUNK)
        grown = start * jnp.exp(total[c : c + 1, :])
        state_out[c] = state[c] + grown
        mixed = local[here, :] + mul(query[here, :], grown, 1, 1)
        mixed_out[here, :] = mixed
        inverse = lax.rsqrt(jnp.mean(mixed * mixed, axis=-1, keepdims=True) + EPS_GROUP)
        g = gate[here, :].astype(F32)
        gated_out[here, :] = (mixed * inverse * gain[...] * (g * jax.nn.sigmoid(g))).astype(BF16)


def gate_back_kernel(
    grad_gated, mixed, gate, gain, query, decay, grad_mixed_out, grad_gate_out, grad_gain_out, start_out
):
    length = mixed.shape[0]
    count = length // CHUNK
    grad_gain = jnp.zeros((1, HEAD_DIM), F32)
    state = jnp.zeros((HEAD_DIM, HEAD_DIM), F32)
    for c in reversed(range(count)):
        here = slice(c * CHUNK, (c + 1) * CHUNK)
        grad = grad_gated[here, :].astype(F32)
        mix = mixed[here, :]
        inverse = lax.rsqrt(jnp.mean(mix * mix, axis=-1, keepdims=True) + EPS_GROUP)
        g = gate[here, :].astype(F32)
        s = jax.nn.sigmoid(g)
        unit = mix * inverse
        w = grad * gain[...] * (g * s)
        grad_gain = grad_gain + jnp.sum(grad * unit * (g * s), axis=0, keepdims=True)
        grad_gate_out[here, :] = (grad * unit * gain[...] * (s * (1.0 + g * (1.0 - s)))).astype(BF16)
        grad_mixed = inverse * w - mix * (inverse * inverse * inverse) * jnp.mean(w * mix, axis=-1, keepdims=True)
        grad_mixed_out[here, :] = grad_mixed
        state = state * decay[c : c + 1, :] + mul(grad_mixed, query[here, :], 0, 0)
    start_out[...] = state
    grad_gain_out[...] = jnp.broadcast_to(grad_gain, (PAD, HEAD_DIM))


def backward_kernel(
    grad_mixed, conv, query, key, states, carry, halo, proj, taps, gap, grad_out, edge_out, small_out, rows, grads
):
    length = grad_mixed.shape[0]
    count = length // CHUNK
    rows[0:PAD, :] = halo[...].astype(F32)
    rows[PAD:, :] = proj[...].astype(F32)
    grads[0:PAD, :] = jnp.zeros((PAD, 3 * HEAD_DIM), F32)
    grads[PAD + length :, :] = jnp.zeros((PAD, 3 * HEAD_DIM), F32)
    lower = triangle(True)
    ones = lower.astype(F32)
    upper = triangle(False).astype(F32)
    last_row = lax.broadcasted_iota(jnp.int32, (CHUNK, HEAD_DIM), 0) == CHUNK - 1
    back = carry[...]
    grad_gap = jnp.zeros((1, HEAD_DIM), F32)
    sums = [jnp.zeros((1, HEAD_DIM), F32) for _ in range(12)]
    for c in reversed(range(count)):
        at = c * CHUNK
        here = slice(at, at + CHUNK)
        c0, c1, values = (conv[here, j * HEAD_DIM : (j + 1) * HEAD_DIM] for j in range(3))
        s1 = jax.nn.sigmoid(c1)
        open_share = 1.0 - s1
        keys = gap[...] * open_share
        forget = 1.0 - keys
        running = mul(ones, jnp.log(forget), 1, 0)
        last = running[CHUNK - 1 : CHUNK, :]
        grown, shrunk, rest = jnp.exp(running), jnp.exp(-running), jnp.exp(last - running)
        q, k, g = query[here, :], key[here, :], grad_mixed[here, :]
        carried = keys * rest
        state = states[c]
        scores = jnp.where(lower, mul(q, k, 1, 1), 0.0)
        grad_scores = jnp.where(lower, mul(g, values, 1, 1), 0.0)
        grad_values = mul(scores, g, 0, 0) + mul(carried, back, 1, 1)
        grad_query = mul(grad_scores, k, 1, 0) + mul(g, state, 1, 0)
        grad_key = mul(grad_scores, q, 0, 0)
        grad_carried = mul(values, back, 1, 0)
        grad_last = jnp.exp(last) * jnp.sum(back * state, axis=0, keepdims=True) + jnp.sum(
            grad_carried * carried, axis=0, keepdims=True
        )
        grad_running = grad_query * q - grad_key * k - grad_carried * carried
        grad_running = grad_running + jnp.where(last_row, grad_last, 0.0)
        grad_keys = grad_key * shrunk + grad_carried * rest
        grad_forget = mul(upper, grad_running, 1, 0) / forget
        inner = grad_forget - grad_keys
        grad_gap = grad_gap - jnp.sum(open_share * inner, axis=0, keepdims=True)
        sigmoid0 = jax.nn.sigmoid(c0)
        new = (
            grad_query * grown * (sigmoid0 * (1.0 + c0 * (1.0 - sigmoid0))),
            gap[...] * s1 * open_share * inner,
            grad_values,
        )
        back = back * jnp.exp(last) + mul(g, q, 0, 0)
        for j in range(3):
            cols = slice(j * HEAD_DIM, (j + 1) * HEAD_DIM)
            grads[PAD + at : PAD + at + CHUNK, cols] = new[j]
            for d in range(4):
                sums[4 * j + d] = sums[4 * j + d] + jnp.sum(
                    new[j] * rows[PAD + at - d : PAD + at - d + CHUNK, cols], axis=0, keepdims=True
                )
            total = taps[4 * j : 4 * j + 1, :] * new[j]
            for d in range(1, 4):
                total = total + taps[4 * j + d : 4 * j + d + 1, :] * grads[PAD + at + d : PAD + at + d + CHUNK, cols]
            grad_out[here, cols] = total
    for j in range(3):
        cols = slice(j * HEAD_DIM, (j + 1) * HEAD_DIM)
        total = taps[4 * j + 1 : 4 * j + 2, :] * grads[1 : 1 + PAD, cols]
        for d in range(2, 4):
            total = total + taps[4 * j + d : 4 * j + d + 1, :] * grads[d : d + PAD, cols]
        edge_out[:, cols] = total
    for i in range(12):
        small_out[i : i + 1, :] = sums[i]
    small_out[12:13, :] = grad_gap
    small_out[13:16, :] = jnp.zeros((3, HEAD_DIM), F32)


def call(kernel, outs, args, scratch=()):
    return pl.pallas_call(
        kernel,
        out_shape=[jax.ShapeDtypeStruct(s, d) for s, d in outs],
        in_specs=[pl.BlockSpec(memory_space=pltpu.VMEM)] * len(args),
        out_specs=[pl.BlockSpec(memory_space=pltpu.VMEM)] * len(outs),
        scratch_shapes=list(scratch),
        compiler_params=pltpu.CompilerParams(vmem_limit_bytes=VMEM_LIMIT),
    )(*args)


class Group:
    def __init__(self, heads):
        self.size = heads
        self.peers = lax.axis_size("seq")
        self.count = self.peers // heads
        self.member = lax.rem(lax.axis_index("seq"), heads)
        self.core = lax.axis_index("head")
        self.lists = [list(range(g * heads, (g + 1) * heads)) for g in range(self.count)]

    def swap(self, value, bits):
        return lax.ppermute(value, "seq", [(s, s ^ bits) for s in range(self.peers)])

    def other_core(self, value):
        return lax.ppermute(value, "head", [(0, 1), (1, 0)])

    def shift(self, value, groups):
        step = groups * self.size
        pairs = [(s, s + step) for s in range(self.peers) if 0 <= s + step < self.peers]
        return lax.ppermute(value, "seq", pairs)

    def carry(self, state, decay, sign):
        total = None
        for k in reversed(range(1, self.count)):
            new = self.shift(state, sign * k)
            total = new if total is None else new + total * self.shift(decay, sign * k)
        return jnp.zeros_like(state) if total is None else total

    def gather(self, half):
        got = {0: half}
        for bits in (1, 2, 4):
            got[bits] = self.swap(half, bits)
        got[3] = self.swap(got[2], 1)
        got[6] = self.swap(got[4], 2)
        got[5] = self.swap(got[4], 1)
        got[7] = self.swap(got[5], 2)
        own = jnp.zeros((self.size,) + half.shape, half.dtype)
        for bits in range(self.size):
            own = lax.dynamic_update_index_in_dim(own, got[bits], self.member ^ bits, 0)
        other = self.other_core(own)
        pair = jnp.where(self.core == 0, jnp.stack([own, other], 1), jnp.stack([other, own], 1))
        return pair.reshape((-1,) + half.shape[1:])

    def scatter(self, partial):
        rows = partial.reshape(self.size, 2, -1, partial.shape[-1])
        other = lax.dynamic_index_in_dim(rows, 1 - self.core, 1, False).astype(BF16)
        mine = lax.dynamic_index_in_dim(rows, self.core, 1, False)
        total = mine + self.other_core(other).astype(F32)
        part = [lax.dynamic_index_in_dim(total, self.member ^ bits, 0, False) for bits in range(self.size)]

        def add(to, source, bits):
            part[to] = part[to] + self.swap(part[source].astype(BF16), bits).astype(F32)

        add(5, 7, 2)
        add(2, 3, 1)
        add(4, 6, 2)
        add(0, 1, 1)
        add(4, 5, 1)
        add(0, 2, 2)
        add(0, 4, 4)
        return part[0]


def to_owners(group, blocks):
    return lax.all_to_all(jnp.concatenate([blocks] * group.count, 0), "seq", 0, 0, tiled=True)


def to_shards(group, blocks):
    got = lax.all_to_all(blocks, "seq", 0, 0, tiled=True)
    return jnp.sum(got.reshape((group.count, group.size) + got.shape[1:]).astype(F32), axis=0)


def inverse_of(rows):
    return lax.rsqrt(jnp.mean(rows * rows, axis=-1, keepdims=True) + EPS_TOKEN)


def norm_back(rows, inverse, gain, grad):
    scaled = grad * gain
    dot_term = jnp.mean(scaled * rows, axis=-1, keepdims=True)
    grad_rows = inverse * scaled - rows * (inverse * inverse * inverse) * dot_term
    return grad_rows, jnp.sum(grad * rows * inverse, axis=0)


def shards(
    tokens,
    norm1_gain,
    mix_weight,
    conv_weight,
    decay_gap,
    group_gain,
    out_weight,
    norm2_gain,
    up_pair,
    down_weight,
    cotangent,
):
    depth = mix_weight.shape[1]
    heads = mix_weight.shape[2] // HEAD_DIM
    units = down_weight.shape[0] // heads
    local, width = tokens.shape
    half = local // 2
    group = Group(heads)
    peers, member, core = group.peers, group.member, group.core
    length = heads * local
    count = length // CHUNK

    def my_half(rows):
        return lax.dynamic_slice_in_dim(rows, core * half, half, 0)

    def own_head(array):
        return lax.dynamic_slice_in_dim(array, member * HEAD_DIM, HEAD_DIM, array.ndim - 1)

    mix_blocks = mix_weight.reshape(4, depth, heads, HEAD_DIM).transpose(2, 1, 0, 3)
    mix_own = to_owners(group, mix_blocks.reshape(heads, depth, 4 * HEAD_DIM)).reshape(width, 4 * HEAD_DIM)
    up_blocks = up_pair.transpose(0, 2, 1).reshape(2, heads, units, depth).transpose(1, 0, 2, 3)
    up_own = to_owners(group, up_blocks.reshape(heads, 2 * units, depth))
    up_own = up_own.transpose(1, 0, 2).reshape(2 * units, width)
    down_own = to_owners(group, down_weight.reshape(heads, units, depth))
    down_own = down_own.transpose(1, 0, 2).reshape(units, width)
    out_all = lax.all_gather(out_weight, "seq", axis=0)
    out_all = out_all.transpose(1, 0, 2).reshape(heads * HEAD_DIM, width)

    taps = own_head(conv_weight).reshape(12, HEAD_DIM)
    gap = own_head(decay_gap).reshape(1, HEAD_DIM)
    gain = own_head(group_gain).reshape(1, HEAD_DIM)

    token_rows = tokens.astype(F32)
    inverse1 = inverse_of(token_rows)
    half_tokens = my_half(token_rows)
    half_inverse1 = my_half(inverse1)
    normed1 = group.gather((half_tokens * half_inverse1 * norm1_gain).astype(BF16))
    projected = mul(normed1, mix_own, 1, 0, None).astype(BF16)
    rows3, gate_rows = projected[:, : 3 * HEAD_DIM], projected[:, 3 * HEAD_DIM :]
    halo = jnp.concatenate(
        [jnp.zeros((PAD - 3, 3 * HEAD_DIM), BF16), group.shift(rows3[length - 3 :], 1)], axis=0
    )

    def wide(n, dtype=F32):
        return ((length, n * HEAD_DIM), dtype)

    square = ((HEAD_DIM, HEAD_DIM), F32)
    conv, query, key, totals, states, mixed_here, last = call(
        forward_kernel,
        [
            wide(3),
            wide(1),
            wide(1),
            ((count, HEAD_DIM), F32),
            ((count, HEAD_DIM, HEAD_DIM), F32),
            wide(1),
            ((HEAD_DIM + PAD, HEAD_DIM), F32),
        ],
        (rows3, halo, taps, gap),
        [pltpu.VMEM((length + PAD, 3 * HEAD_DIM), F32)],
    )
    own_decay = last[HEAD_DIM : HEAD_DIM + 1]
    carry = group.carry(last[:HEAD_DIM], own_decay, 1)
    mixed, states, gated = call(
        gate_kernel,
        [wide(1), ((count, HEAD_DIM, HEAD_DIM), F32), wide(1, BF16)],
        (mixed_here, query, totals, states, carry, gate_rows, gain),
    )

    def by_head(rows):
        got = lax.all_to_all(rows.reshape(heads, local, HEAD_DIM), "seq", 0, 0, axis_index_groups=group.lists, tiled=True)
        return got.transpose(1, 0, 2).reshape(local, heads * HEAD_DIM)

    def by_token(rows):
        blocks = rows.reshape(local, heads, HEAD_DIM).transpose(1, 0, 2)
        got = lax.all_to_all(blocks, "seq", 0, 0, axis_index_groups=group.lists, tiled=True)
        return got.reshape(length, HEAD_DIM)

    branch = mul(by_head(gated), out_all, 1, 0, None)
    away = lax.dynamic_slice_in_dim(branch, (1 - core) * half, half, 0)
    hidden = half_tokens + my_half(branch) + group.other_core(away)

    inverse2 = inverse_of(hidden)
    normed2 = group.gather((hidden * inverse2 * norm2_gain).astype(BF16))
    cot_half = my_half(cotangent)
    cot_all = group.gather(cot_half)

    lifted = mul(normed2, up_own, 1, 1, None)
    gate_in, up_in = lifted[:, :units], lifted[:, units:]
    gate_act = gate_in * jax.nn.sigmoid(gate_in)
    inner = (gate_act * up_in).astype(BF16)
    grad_inner = mul(cot_all, down_own, 1, 1, None)
    grad_lifted = jnp.concatenate(
        [grad_inner * up_in * dsilu(gate_in), grad_inner * gate_act], axis=1
    ).astype(BF16)
    grad_normed2 = group.scatter(mul(grad_lifted, up_own, 1, 0, None))
    grad_hidden_norm, grad_norm2 = norm_back(hidden, inverse2, norm2_gain, grad_normed2)
    grad_hidden = cot_half.astype(F32) + grad_hidden_norm
    grad_branch_half = grad_hidden.astype(BF16)

    other_branch = group.other_core(grad_branch_half)
    grad_branch = jnp.where(
        core == 0,
        jnp.concatenate([grad_branch_half, other_branch], 0),
        jnp.concatenate([other_branch, grad_branch_half], 0),
    )
    grad_gated = by_token(mul(grad_branch, out_all, 1, 1, None).astype(BF16))
    decays = jnp.exp(jnp.concatenate([totals[1:] - totals[:-1], jnp.log(own_decay) - totals[-1:]], axis=0))
    grad_mixed, grad_gate_rows, grad_group, start_grad = call(
        gate_back_kernel,
        [wide(1), wide(1, BF16), ((PAD, HEAD_DIM), F32), square],
        (grad_gated, mixed, gate_rows, gain, query, decays),
    )
    back_carry = group.carry(start_grad, own_decay, -1)
    grad_rows3, edge, small = call(
        backward_kernel,
        [wide(3), ((PAD, 3 * HEAD_DIM), F32), ((16, HEAD_DIM), F32)],
        (grad_mixed, conv, query, key, states, back_carry, halo, rows3, taps, gap),
        [
            pltpu.VMEM((length + PAD, 3 * HEAD_DIM), F32),
            pltpu.VMEM((length + 2 * PAD, 3 * HEAD_DIM), F32),
        ],
    )
    later = group.shift(edge, -1)
    grad_rows3 = jnp.concatenate([grad_rows3[: length - PAD], grad_rows3[length - PAD :] + later], axis=0)
    grad_projected = jnp.concatenate([grad_rows3.astype(BF16), grad_gate_rows], axis=1)

    grad_mix = mul(normed1, grad_projected, 0, 0, None).astype(BF16)
    mix_total = to_shards(group, grad_mix.reshape(peers, depth, 4 * HEAD_DIM))
    mix_total = mix_total.reshape(heads, depth, 4, HEAD_DIM).transpose(2, 1, 0, 3).reshape(4, depth, heads * HEAD_DIM)

    grad_normed1 = group.scatter(mul(grad_projected, mix_own, 1, 1, None))
    grad_rows1, grad_norm1 = norm_back(half_tokens, half_inverse1, norm1_gain, grad_normed1)
    grad_tokens = grad_hidden + grad_rows1

    def columns(rows):
        return rows.astype(BF16).reshape(-1, peers, depth).transpose(1, 0, 2)

    up_total = to_shards(group, columns(mul(grad_lifted, normed2, 0, 0, None)))
    up_total = up_total.reshape(heads, 2, units, depth).transpose(1, 3, 0, 2).reshape(2, depth, heads * units)
    down_total = to_shards(group, columns(mul(inner, cot_all, 0, 0, None)))
    down_total = down_total.reshape(heads * units, depth)
    branch_all = group.gather(grad_branch_half)
    out_total = to_shards(group, columns(mul(gated, branch_all, 0, 0, None))).reshape(heads * HEAD_DIM, depth)

    block_half = hidden + group.scatter(mul(inner, down_own, 1, 0, None))

    def both_halves(rows):
        other = group.other_core(rows)
        return jnp.where(core == 0, jnp.concatenate([rows, other], 0), jnp.concatenate([other, rows], 0))

    block_out = both_halves(block_half)
    grad_tokens = both_halves(grad_tokens)
    inverse2 = both_halves(inverse2)

    own_small = jnp.concatenate([small[:13], grad_group[:1]], axis=0)
    placed = lax.dynamic_update_slice(jnp.zeros((14, heads * HEAD_DIM), F32), own_small, (0, member * HEAD_DIM))
    small_total, norms = lax.psum((placed, jnp.stack([grad_norm1, grad_norm2])), "seq")
    norms = norms + group.other_core(norms)
    inverse_rms = jnp.stack([inverse1[:, 0], inverse2[:, 0]])
    return (
        block_out,
        grad_tokens,
        norms[0],
        mix_total,
        small_total[:12].reshape(3, 4, heads * HEAD_DIM),
        small_total[12],
        small_total[13],
        out_total,
        norms[1],
        up_total,
        down_total,
        inverse_rms,
    )


def solution(mesh):
    in_specs = (
        P("seq", None),
        P(),
        P(None, "seq", "head"),
        P(None, None, "head"),
        P("head"),
        P("head"),
        P("head", "seq"),
        P(),
        P(None, "seq", "head"),
        P("head", "seq"),
        P("seq", None),
    )
    out_specs = (
        P("seq", None),
        P("seq", None),
        P(),
        P(None, "seq", "head"),
        P(None, None, "head"),
        P("head"),
        P("head"),
        P("head", "seq"),
        P(),
        P(None, "seq", "head"),
        P("head", "seq"),
        P(None, "seq"),
    )
    return jax.shard_map(shards, mesh=mesh, in_specs=in_specs, out_specs=out_specs, check_vma=False)
```

time: 3660 us -> 709 us (0.19)
  waiting for transfers between devices: 3290 us -> 309 us
  starting transfers between devices: 7.93 us -> 132 us
  matrix products: 140 us -> 47.4 us
  local copies, waits for them, and re-layouts: 56.5 us -> 118 us
  other arithmetic: 105 us -> 56.6 us
    reduce_scatter x8 -> x0, waiting for transfers between devices: 2330 us -> none  [the longest x1 943 us: shards(): lax.psum_scatter(grad_up, 'seq', scatter_dimension=1, tiled=True)]
    all_gather x10 -> x1, waiting for transfers between devices: 894 us -> 0.01 us  [shards(): out_all = lax.all_gather(out_weight, 'seq', axis=0)]
    ppermute x2 -> x66, waiting for transfers between devices: 5.94 us -> 168 us  [the longest x49 106 us: swap(): lax.ppermute(value, 'seq', [(s, s ^ bits) for s in range(self.peers)])]
    dot_general x40 -> x12, matrix products: 140 us -> 47.4 us  [mul(): lax.dot_general(a, b, (((ca,), (cb,)), ((), ())), precision=precision, pr...]
    ppermute x2 -> x66, starting transfers between devices: 6.41 us -> 75.6 us  [the longest x49 63.4 us: swap(): lax.ppermute(value, 'seq', [(s, s ^ bits) for s in range(self.peers)])]
    all_to_all x0 -> x9, starting transfers between devices: none -> 56.1 us  [the longest x4 25 us: to_shards(): got = lax.all_to_all(blocks, 'seq', 0, 0, tiled=True)]
    psum x1, waiting for transfers between devices: 57.5 us -> 103 us  [shards(): lax.psum((placed, jnp.stack([grad_norm1, grad_norm2])), 'seq')]
    all_to_all x0 -> x9, waiting for transfers between devices: none -> 37.1 us  [the longest x3 26.9 us: to_owners(): lax.all_to_all(jnp.concatenate([blocks] * group.count, 0), 'seq', 0, 0, t...]
  transfers between devices with their start and end apart: 21 -> 77, of which waited for: 21 -> 31; matrix products, arithmetic and copies ran while one was open for 3% -> 25% of each run, Pallas kernels for 0% -> 2%
where the time goes in v1:
time: 709 us; the launch traced here: 695 us
  waiting for transfers between devices  309 us (44%)
  starting transfers between devices  132 us (19%)
  local copies, waits for them, and re-layouts  118 us (17%)
  other arithmetic  56.6 us (8%)
  matrix products  47.4 us (7%)
  Pallas kernels  16.7 us (2%)
  between operations  15.5 us (2%)
    ppermute x49, waiting for transfers between devices, swap(): lax.ppermute(value, 'seq', [(s, s ^ bits) for s in range(self.peers)])  106 us
    psum x1, waiting for transfers between devices, shards(): lax.psum((placed, jnp.stack([grad_norm1, grad_norm2])), 'seq')  103 us
    ppermute x49, starting transfers between devices, swap(): lax.ppermute(value, 'seq', [(s, s ^ bits) for s in range(self.peers)])  63.4 us
    ppermute x4, waiting for transfers between devices, shift(): return lax.ppermute(value, 'seq', pairs)  58.4 us
    dot_general x12, matrix products, mul(): lax.dot_general(a, b, (((ca,), (cb,)), ((), ())), precision=precision, pr...  47.4 us
    dynamic_update_slice x29, local copies, waits for them, and re-layouts, gather(): own = lax.dynamic_update_index_in_dim(own, got[bits], self.member ^ bits, 0)  33.4 us
    all_to_all x3, waiting for transfers between devices, to_owners(): lax.all_to_all(jnp.concatenate([blocks] * group.count, 0), 'seq', 0, 0, t...  26.9 us
    all_to_all x4, starting transfers between devices, to_shards(): got = lax.all_to_all(blocks, 'seq', 0, 0, tiled=True)  25 us
  transfers between devices with their start and end apart: 77, of which 31 were waited for; matrix products, arithmetic and copies ran while one was open for 25% of the time, Pallas kernels for 2%

profile of v1, /device:TPU:18, one launch (start us, length us, event | category | flops | bytes accessed | tf_op | source)
XLA Modules:
  0.0 694.8 jit_solution(12619929281387987009)
XLA Ops:
  32.5 7.3 %collective-permute-done.4 = bf16[64,2048]{1,0:T(8,128)(2,1)S(1)} collective-permute-done((bf16[64,2048]{1,0:T(8,128)(2,1)}, bf16[64,2048]{1,0:T(8,128)(2,1)S(1)}, u32[]{:S(2)}, u32[]{:S(2)}) %collective-permute-start.4) | collective-permute-done | bytes 262176 | tf_op jit(solution)/shard_map/ppermute | solution.py:216
  48.2 6.6 collective-permute-done.6
  72.7 7.0 %collective-permute-done.31 = bf16[64,2048]{1,0:T(8,128)(2,1)} collective-permute-done((bf16[64,2048]{1,0:T(8,128)(2,1)S(1)}, bf16[64,2048]{1,0:T(8,128)(2,1)}, u32[]{:S(2)}, u32[]{:S(2)}) %collective-permute-start.31) | collective-permute-done | bytes 262176 | tf_op jit(solution)/shard_map/ppermute | solution.py:216
  118.1 9.3 %all-to-all-start.1 = ((bf16[8,128,128]{1,2,0:T(8,128)(2,1)}), bf16[8,128,128]{1,2,0:T(8,128)(2,1)}, u32[]{:S(2)}, u32[]{:S(2)}) async-start(bf16[8,128,128]{1,2,0:T(8,128)(2,1)} %copy.107), calls=%async_computation.1 | async-start | bytes 524288 | tf_op jit(solution)/shard_map/all_to_all | solution.py:369
  132.3 5.8 all-to-all-start.3
  139.8 6.4 copy.108
  160.2 5.8 all-to-all-done.3
  166.0 6.0 all-to-all-start.2
  193.9 6.1 collective-permute-done.17
  213.3 20.4 %all-to-all-done.2 = bf16[16,704,128]{2,1,0:T(8,128)(2,1)} async-done(((bf16[16,704,128]{2,1,0:T(8,128)(2,1)}), bf16[16,704,128]{2,1,0:T(8,128)(2,1)}, u32[]{:S(2)}, u32[]{:S(2)}) %all-to-all-start.2) | async-done | bytes 2883616 | tf_op jit(solution)/shard_map/all_to_all | solution.py:269
  249.8 6.6 fusion
  277.0 5.7 fusion.3
  293.6 5.9 all-to-all-start.8
  318.1 15.5 %collective-permute-done.38 = bf16[64,2048]{1,0:T(8,128)(2,1)S(1)} collective-permute-done((bf16[64,2048]{1,0:T(8,128)(2,1)S(1)}, bf16[64,2048]{1,0:T(8,128)(2,1)S(1)}, u32[]{:S(2)}, u32[]{:S(2)}) %collective-permute-start.38) | collective-permute-done | bytes 262176 | tf_op jit(solution)/shard_map/ppermute | solution.py:216
  337.3 8.8 %collective-permute-done.25 = bf16[64,2048]{1,0:T(8,128)(2,1)S(1)} collective-permute-done((bf16[64,2048]{1,0:T(8,128)(2,1)S(1)}, bf16[64,2048]{1,0:T(8,128)(2,1)S(1)}, u32[]{:S(2)}, u32[]{:S(2)}) %collective-permute-start.25) | collective-permute-done | bytes 262176 | tf_op jit(solution)/shard_map/ppermute | solution.py:216
  354.7 6.8 collective-permute-done.26
  401.2 6.5 all-to-all-start.7
  420.4 49.9 %collective-permute-done.45.carry = f32[128,128]{1,0:T(8,128)S(1)} collective-permute-done((f32[128,128]{1,0:T(8,128)S(1)}, f32[128,128]{1,0:T(8,128)S(1)}, u32[]{:S(2)}, u32[]{:S(2)}) %collective-permute-start.45) | collective-permute-done | bytes 65568 | tf_op jit(solution)/shard_map/ppermute | solution.py:224
  470.2 8.2 %shard_map.205 = (f32[1024,384]{1,0:T(8,128)S(1)}, f32[8,384]{1,0:T(8,128)S(1)}, f32[16,128]{1,0:T(8,128)S(1)}) custom-call(f32[1024,128]{1,0:T(8,128)S(1)} %get-tuple-element.36.grad_mixed, f32[1024,384]{1,0:T(8,128)S(1)} %get-tuple-element.37.conv, f32[1024,128]{1,0:T(8,128)S(1)} %get-tuple-element.30.query, f32[1024,128]{1,0:T(8,128)S(1)} %copy-done.3, ...), custom_call_target="tpu_custom_call" | custom-call | tf_op jit(solution)/shard_map/pallas_call | solution.py:196
  501.5 6.5 all-to-all-start.6
  521.6 6.1 all-to-all-start.5
  543.2 6.9 collective-permute-start.54
  555.3 12.8 %collective-permute-done.54 = bf16[64,2048]{1,0:T(8,128)(2,1)} collective-permute-done((bf16[64,2048]{1,0:T(8,128)(2,1)}, bf16[64,2048]{1,0:T(8,128)(2,1)}, u32[]{:S(2)}, u32[]{:S(2)}) %collective-permute-start.54) | collective-permute-done | bytes 262176 | tf_op jit(solution)/shard_map/ppermute | solution.py:216
  570.8 103.0 %all-reduce.4.cloned.1.call-done = (f32[2,2048]{1,0:T(2,128)}, f32[14,1024]{1,0:T(8,128)}) async-done(((f32[2,2048]{1,0:T(2,128)}, f32[14,1024]{1,0:T(8,128)}), (f32[2,2048]{1,0:T(2,128)}, f32[14,1024]{1,0:T(8,128)})) %all-reduce.4.cloned.1.call-update) | async-done | bytes 73744 | tf_op jit(solution)/shard_map/psum | solution.py:456
  (352 shorter events, 349.6 us)
Async XLA Ops:
  20.7 69.3 %all-to-all-start = ((bf16[16,128,512]{2,1,0:T(8,128)(2,1)}), bf16[16,128,512]{2,1,0:T(8,128)(2,1)}, u32[]{:S(2)}, u32[]{:S(2)}) async-start(bf16[16,128,512]{2,1,0:T(8,128)(2,1)} %pad_maximum_fusion.1), calls=%async_computation | async-start | bytes 4194304 | tf_op jit(solution)/shard_map/all_to_all | solution.py:269
  26.2 113.6 %all-gather.3.cloned.1.call-start = ((), (), s32[]{:S(2)}) async-start(), calls=%async_computation.9 | async-start | bytes 4456448 | tf_op jit(solution)/shard_map/all_gather | solution.py:324
  54.8 29.9 %collective-permute-start.7 = (bf16[8,64,2048]{2,1,0:T(8,128)(2,1)S(1)}, bf16[8,64,2048]{2,1,0:T(8,128)(2,1)}, u32[]{:S(2)}, u32[]{:S(2)}) collective-permute-start(bf16[8,64,2048]{2,1,0:T(8,128)(2,1)S(1)} %bitcast_dynamic-update-slice_fusion.24), channel_id=1, source_target_pairs={{0,1},{1,0},{2,3},{3,2},{4,5},{5,4},{6,7},{7,6},{8,9},{9,8},{10,11... | collective-permute-start | bytes 6291464 | tf_op jit(solution)/shard_map/ppermute | solution.py:219
  57.2 39.3 %collective-permute-start.28 = (bf16[64,2048]{1,0:T(8,128)(2,1)S(1)}, bf16[64,2048]{1,0:T(8,128)(2,1)S(1)}, u32[]{:S(2)}, u32[]{:S(2)}) collective-permute-start(bf16[64,2048]{1,0:T(8,128)(2,1)S(1)} %get-tuple-element.110), channel_id=1, source_target_pairs={{0,2},{2,0},{4,6},{6,4},{8,10},{10,8},{12,14},{14,12},{16,18},{18,... | collective-permute-start | bytes 786440 | tf_op jit(solution)/shard_map/ppermute | solution.py:216
  79.7 30.7 %collective-permute-start.32 = (bf16[64,2048]{1,0:T(8,128)(2,1)}, bf16[64,2048]{1,0:T(8,128)(2,1)}, u32[]{:S(2)}, u32[]{:S(2)}) collective-permute-start(bf16[64,2048]{1,0:T(8,128)(2,1)} %collective-permute-done.31), channel_id=1, source_target_pairs={{0,2},{2,0},{4,6},{6,4},{8,10},{10,8},{12,14},{14,12},{16,18},{18,... | collective-permute-start | bytes 786440 | tf_op jit(solution)/shard_map/ppermute | solution.py:216
  81.9 70.0 %collective-permute-start.33 = (bf16[64,2048]{1,0:T(8,128)(2,1)}, bf16[64,2048]{1,0:T(8,128)(2,1)}, u32[]{:S(2)}, u32[]{:S(2)}) collective-permute-start(bf16[64,2048]{1,0:T(8,128)(2,1)} %collective-permute-done.31), channel_id=1, source_target_pairs={{0,4},{2,6},{4,0},{6,2},{8,12},{10,14},{12,8},{14,10},{16,20},{18,... | collective-permute-start | bytes 786440 | tf_op jit(solution)/shard_map/ppermute | solution.py:216
  84.8 42.6 %collective-permute-start.30 = (bf16[64,2048]{1,0:T(8,128)(2,1)}, bf16[64,2048]{1,0:T(8,128)(2,1)}, u32[]{:S(2)}, u32[]{:S(2)}) collective-permute-start(bf16[64,2048]{1,0:T(8,128)(2,1)} %collective-permute-done.29), channel_id=1, source_target_pairs={{0,2},{2,0},{4,6},{6,4},{8,10},{10,8},{12,14},{14,12},{16,18},{18,... | collective-permute-start | bytes 786440 | tf_op jit(solution)/shard_map/ppermute | solution.py:216
  110.4 61.7 %collective-permute-start.34 = (bf16[64,2048]{1,0:T(8,128)(2,1)}, bf16[64,2048]{1,0:T(8,128)(2,1)}, u32[]{:S(2)}, u32[]{:S(2)}) collective-permute-start(bf16[64,2048]{1,0:T(8,128)(2,1)} %collective-permute-done.32), channel_id=1, source_target_pairs={{0,4},{2,6},{4,0},{6,2},{8,12},{10,14},{12,8},{14,10},{16,20},{18,... | collective-permute-start | bytes 786440 | tf_op jit(solution)/shard_map/ppermute | solution.py:216
  132.3 33.7 %all-to-all-start.3 = ((bf16[16,352,128]{2,1,0:T(8,128)(2,1)}), bf16[16,352,128]{2,1,0:T(8,128)(2,1)}, u32[]{:S(2)}, u32[]{:S(2)}) async-start(bf16[16,352,128]{2,1,0:T(8,128)(2,1)} %pad_maximum_fusion.2), calls=%async_computation.3 | async-start | bytes 2883584 | tf_op jit(solution)/shard_map/all_to_all | solution.py:269
  166.0 67.7 %all-to-all-start.2 = ((bf16[16,704,128]{2,1,0:T(8,128)(2,1)}), bf16[16,704,128]{2,1,0:T(8,128)(2,1)}, u32[]{:S(2)}, u32[]{:S(2)}) async-start(bf16[16,704,128]{2,1,0:T(8,128)(2,1)} %pad_maximum_fusion), calls=%async_computation.2 | async-start | bytes 5767168 | tf_op jit(solution)/shard_map/all_to_all | solution.py:269
  173.7 33.5 %collective-permute-start.35 = (bf16[8,64,2048]{2,1,0:T(8,128)(2,1)}, bf16[8,64,2048]{2,1,0:T(8,128)(2,1)}, u32[]{:S(2)}, u32[]{:S(2)}) collective-permute-start(bf16[8,64,2048]{2,1,0:T(8,128)(2,1)} %bitcast_dynamic-update-slice_fusion.8), channel_id=1, source_target_pairs={{0,1},{1,0},{2,3},{3,2},{4,5},{5,4},{6,7},{7,6},{8,9},{9,8},{10,11... | collective-permute-start | bytes 6291464 | tf_op jit(solution)/shard_map/ppermute | solution.py:219
  200.7 43.8 %collective-permute-start.18 = (bf16[8,64,2048]{2,1,0:T(8,128)(2,1)}, bf16[8,64,2048]{2,1,0:T(8,128)(2,1)}, u32[]{:S(2)}, u32[]{:S(2)}) collective-permute-start(bf16[8,64,2048]{2,1,0:T(8,128)(2,1)} %bitcast_dynamic-update-slice_fusion.16), channel_id=1, source_target_pairs={{0,1},{1,0},{2,3},{3,2},{4,5},{5,4},{6,7},{7,6},{8,9},{9,8},{10,11... | collective-permute-start | bytes 6291464 | tf_op jit(solution)/shard_map/ppermute | solution.py:219
  293.6 95.9 %all-to-all-start.8 = ((bf16[16,352,128]{2,1,0:T(8,128)(2,1)}), bf16[16,352,128]{2,1,0:T(8,128)(2,1)}, u32[]{:S(2)}, u32[]{:S(2)}) async-start(bf16[16,352,128]{2,1,0:T(8,128)(2,1)} %bitcast.346), calls=%async_computation.8 | async-start | bytes 2883584 | tf_op jit(solution)/shard_map/all_to_all | solution.py:273
  305.2 30.6 %collective-permute-start.23 = (bf16[64,2048]{1,0:T(8,128)(2,1)S(1)}, bf16[64,2048]{1,0:T(8,128)(2,1)S(1)}, u32[]{:S(2)}, u32[]{:S(2)}) collective-permute-start(bf16[64,2048]{1,0:T(8,128)(2,1)S(1)} %get-tuple-element.133), channel_id=1, source_target_pairs={{0,4},{2,6},{4,0},{6,2},{8,12},{10,14},{12,8},{14,10},{16,20},{18,... | collective-permute-start | bytes 786440 | tf_op jit(solution)/shard_map/ppermute | solution.py:216
  305.7 48.8 %collective-permute-start.20 = (bf16[64,2048]{1,0:T(8,128)(2,1)S(1)}, bf16[64,2048]{1,0:T(8,128)(2,1)S(1)}, u32[]{:S(2)}, u32[]{:S(2)}) collective-permute-start(bf16[64,2048]{1,0:T(8,128)(2,1)S(1)} %get-tuple-element.131), channel_id=1, source_target_pairs={{0,2},{2,0},{4,6},{6,4},{8,10},{10,8},{12,14},{14,12},{16,18},{18,... | collective-permute-start | bytes 786440 | tf_op jit(solution)/shard_map/ppermute | solution.py:216
  318.0 28.9 %collective-permute-start.40 = (bf16[64,2048]{1,0:T(8,128)(2,1)S(1)}, bf16[64,2048]{1,0:T(8,128)(2,1)S(1)}, u32[]{:S(2)}, u32[]{:S(2)}) collective-permute-start(bf16[64,2048]{1,0:T(8,128)(2,1)S(1)} %get-tuple-element.127), channel_id=1, source_target_pairs={{0,4},{2,6},{4,0},{6,2},{8,12},{10,14},{12,8},{14,10},{16,20},{18,... | collective-permute-start | bytes 786440 | tf_op jit(solution)/shard_map/ppermute | solution.py:216
  385.2 33.4 %collective-permute-start.62 = (bf16[64,2048]{1,0:T(8,128)(2,1)}, bf16[64,2048]{1,0:T(8,128)(2,1)}, u32[]{:S(2)}, u32[]{:S(2)}) collective-permute-start(bf16[64,2048]{1,0:T(8,128)(2,1)} %collective-permute-done.60), channel_id=1, source_target_pairs={{0,4},{2,6},{4,0},{6,2},{8,12},{10,14},{12,8},{14,10},{16,20},{18,... | collective-permute-start | bytes 786440 | tf_op jit(solution)/shard_map/ppermute | solution.py:216
  395.6 88.3 %collective-permute-start.63 = (bf16[64,2048]{1,0:T(8,128)(2,1)}, bf16[64,2048]{1,0:T(8,128)(2,1)}, u32[]{:S(2)}, u32[]{:S(2)}) collective-permute-start(bf16[64,2048]{1,0:T(8,128)(2,1)} %collective-permute-done.61), channel_id=1, source_target_pairs={{0,4},{2,6},{4,0},{6,2},{8,12},{10,14},{12,8},{14,10},{16,20},{18,... | collective-permute-start | bytes 786440 | tf_op jit(solution)/shard_map/ppermute | solution.py:216
  401.2 100.2 %all-to-all-start.7 = ((bf16[16,704,128]{2,1,0:T(8,128)(2,1)}), bf16[16,704,128]{2,1,0:T(8,128)(2,1)}, u32[]{:S(2)}, u32[]{:S(2)}) async-start(bf16[16,704,128]{2,1,0:T(8,128)(2,1)} %bitcast.339), calls=%async_computation.7 | async-start | bytes 5767168 | tf_op jit(solution)/shard_map/all_to_all | solution.py:273
  416.0 54.2 %collective-permute-start.45 = (f32[128,128]{1,0:T(8,128)S(1)}, f32[128,128]{1,0:T(8,128)S(1)}, u32[]{:S(2)}, u32[]{:S(2)}) collective-permute-start(f32[128,128]{1,0:T(8,128)S(1)} %get-tuple-element.40), channel_id=1, source_target_pairs={{16,0},{18,2},{20,4},{22,6},{24,8},{26,10},{28,12},{30,14},{17,1},... | collective-permute-start | bytes 196616 | tf_op jit(solution)/shard_map/ppermute | solution.py:224
  496.1 37.2 %collective-permute-start.27 = (f32[64,2048]{1,0:T(8,128)S(1)}, f32[64,2048]{1,0:T(8,128)S(1)}, u32[]{:S(2)}, u32[]{:S(2)}) collective-permute-start(f32[64,2048]{1,0:T(8,128)S(1)} %copy-done.26), channel_id=1, source_target_pairs={{0,1},{1,0},{2,3},{3,2},{4,5},{5,4},{6,7},{7,6},{8,9},{9,8},{10,11... | collective-permute-start | bytes 1572872 | tf_op jit(solution)/shard_map/ppermute | solution.py:219
  521.6 158.4 %all-to-all-start.5 = ((bf16[16,128,512]{2,1,0:T(8,128)(2,1)}), bf16[16,128,512]{2,1,0:T(8,128)(2,1)}, u32[]{:S(2)}, u32[]{:S(2)}) async-start(bf16[16,128,512]{2,1,0:T(8,128)(2,1)} %bitcast.358), calls=%async_computation.5 | async-start | bytes 4194304 | tf_op jit(solution)/shard_map/all_to_all | solution.py:273
  527.8 146.0 %all-reduce.4.cloned.1.call-start = ((), (), s32[]{:S(2)}) async-start(), calls=%async_computation.10 | async-start | bytes 163840 | tf_op jit(solution)/shard_map/psum | solution.py:456
  570.7 108.2 %collective-permute-start.55 = (f32[64,2048]{1,0:T(8,128)S(1)}, f32[64,2048]{1,0:T(8,128)S(1)}, u32[]{:S(2)}, u32[]{:S(2)}) collective-permute-start(f32[64,2048]{1,0:T(8,128)S(1)} %subtract_add_fusion), channel_id=1, source_target_pairs={{0,1},{1,0},{2,3},{3,2},{4,5},{5,4},{6,7},{7,6},{8,9},{9,8},{10,11... | collective-permute-start | bytes 1572872 | tf_op jit(solution)/shard_map/ppermute | solution.py:219
  (91 other events, 1224.4 us)
Sparse Core Ops, SparseCore 0:
  29.8 95.1 all-gather.2
  570.6 103.1 all-reduce.3

commit v2 on v1

v2 whole, which is shorter than its diff:
```python
import functools

import jax
import jax.numpy as jnp
from jax import lax
from jax.experimental import pallas as pl
from jax.experimental.pallas import tpu as pltpu
from jax.sharding import PartitionSpec as P

HEAD_DIM = 128
CHUNK = 128
PAD = 8
STEP = 4
EPS_TOKEN = 1e-06
EPS_GROUP = 1e-05
HIGH = lax.Precision.HIGHEST
F32 = jnp.float32
BF16 = jnp.bfloat16
VMEM_LIMIT = 48 * 1024 * 1024


def mul(a, b, ca, cb, precision=HIGH):
    return lax.dot_general(
        a, b, (((ca,), (cb,)), ((), ())), precision=precision, preferred_element_type=F32
    )


def dsilu(v):
    s = jax.nn.sigmoid(v)
    return s * (1.0 + v * (1.0 - s))


def triangle(lower):
    row = lax.broadcasted_iota(jnp.int32, (CHUNK, CHUNK), 0)
    col = lax.broadcasted_iota(jnp.int32, (CHUNK, CHUNK), 1)
    return (row >= col) if lower else (row <= col)


def forward_kernel(
    proj, halo, taps, gap, conv_out, query_out, key_out, total_out, state_out, local_out, last_out, rows
):
    length = proj.shape[0]
    rows[0:16, :] = halo[...].astype(F32)
    rows[16:, :] = proj[:, : 3 * HEAD_DIM].astype(F32)
    lower = triangle(True)
    ones = lower.astype(F32)
    state = jnp.zeros((HEAD_DIM, HEAD_DIM), F32)
    before = jnp.zeros((1, HEAD_DIM), F32)
    for c in range(length // CHUNK):
        at = c * CHUNK
        here = slice(at, at + CHUNK)
        conv = []
        for j in range(3):
            cols = slice(j * HEAD_DIM, (j + 1) * HEAD_DIM)
            total = taps[4 * j : 4 * j + 1, :] * rows[16 + at : 16 + at + CHUNK, cols]
            for d in range(1, 4):
                total = total + taps[4 * j + d : 4 * j + d + 1, :] * rows[16 + at - d : 16 + at - d + CHUNK, cols]
            conv.append(total)
            conv_out[here, cols] = total
        queries = conv[0] * jax.nn.sigmoid(conv[0])
        open_share = 1.0 - jax.nn.sigmoid(conv[1])
        keys = gap[...] * open_share
        log_forget = jnp.log(1.0 - keys)
        values = conv[2]
        running = mul(ones, log_forget, 1, 0)
        last = running[CHUNK - 1 : CHUNK, :]
        query = queries * jnp.exp(running)
        key = keys * jnp.exp(-running)
        carried = keys * jnp.exp(last - running)
        query_out[here, :] = query
        key_out[here, :] = key
        total_out[c : c + 1, :] = before
        state_out[c] = state
        scores = jnp.where(lower, mul(query, key, 1, 1), 0.0)
        local_out[here, :] = mul(scores, values, 1, 0) + mul(query, state, 1, 1)
        state = state * jnp.exp(last) + mul(values, carried, 0, 0)
        before = before + last
    last_out[0:HEAD_DIM, :] = state
    last_out[HEAD_DIM:, :] = jnp.broadcast_to(jnp.exp(before), (PAD, HEAD_DIM))


def gate_kernel(
    ids, local, query, total, state, carry, gate, gain, weights, mixed_out, state_out, turned_out, mine, away, gated
):
    length = local.shape[0]
    members, half, _ = mine.shape
    start = carry[...]
    for c in range(length // CHUNK):
        here = slice(c * CHUNK, (c + 1) * CHUNK)
        grown = start * jnp.exp(total[c : c + 1, :])
        state_out[c] = state[c] + grown
        mixed = local[here, :] + mul(query[here, :], grown, 1, 1)
        mixed_out[here, :] = mixed
        inverse = lax.rsqrt(jnp.mean(mixed * mixed, axis=-1, keepdims=True) + EPS_GROUP)
        g = gate[here, 3 * HEAD_DIM :].astype(F32)
        gated[here, :] = (mixed * inverse * gain[...] * (g * jax.nn.sigmoid(g))).astype(BF16)
    parts = []
    for k, b, block in blocks_of(ids, members):
        parts.append(gated[pl.ds(pl.multiple_of(block * half, half), half), :])
        if len(parts) == STEP:
            x = jnp.concatenate(parts, axis=0)
            at = (k * members + b + 1 - STEP) * half
            turned_out[:, at : at + STEP * half] = x.astype(F32).T.astype(BF16)
            result = mul(x, weights[:, 4 * HEAD_DIM :], 1, 1, None).astype(BF16)
            (mine, away)[k][b + 1 - STEP : b + 1] = result.reshape(STEP, half, -1)
            parts = []


def gate_back_kernel(
    ids, *refs, members
):
    own, other = refs[:members], refs[members : 2 * members]
    weights, mixed, gate, gain, query, decay = refs[2 * members : 2 * members + 6]
    grad_mixed_out, grad_gate_out, grad_gain_out, start_out, grad_gated = refs[2 * members + 6 :]
    half = own[0].shape[0]
    at = 0
    blocks = list(blocks_of(ids, members))
    for at in range(0, len(blocks), STEP):
        k, b, _ = blocks[at]
        result = mul(rows_of((own, other)[k], b), weights[:, 4 * HEAD_DIM :], 1, 0, None)
        for i in range(STEP):
            to = pl.multiple_of(blocks[at + i][2] * half, half)
            grad_gated[pl.ds(to, half), :] = result[i * half : (i + 1) * half]
    length = mixed.shape[0]
    count = length // CHUNK
    grad_gain = jnp.zeros((1, HEAD_DIM), F32)
    state = jnp.zeros((HEAD_DIM, HEAD_DIM), F32)
    for c in reversed(range(count)):
        here = slice(c * CHUNK, (c + 1) * CHUNK)
        grad = grad_gated[here, :]
        mix = mixed[here, :]
        inverse = lax.rsqrt(jnp.mean(mix * mix, axis=-1, keepdims=True) + EPS_GROUP)
        g = gate[here, 3 * HEAD_DIM :].astype(F32)
        s = jax.nn.sigmoid(g)
        unit = mix * inverse
        w = grad * gain[...] * (g * s)
        grad_gain = grad_gain + jnp.sum(grad * unit * (g * s), axis=0, keepdims=True)
        grad_gate_out[here, :] = (grad * unit * gain[...] * (s * (1.0 + g * (1.0 - s)))).astype(BF16)
        grad_mixed = inverse * w - mix * (inverse * inverse * inverse) * jnp.mean(w * mix, axis=-1, keepdims=True)
        grad_mixed_out[here, :] = grad_mixed
        state = state * decay[c : c + 1, :] + mul(grad_mixed, query[here, :], 0, 0)
    start_out[...] = state
    grad_gain_out[...] = jnp.broadcast_to(grad_gain, (PAD, HEAD_DIM))


def backward_kernel(
    grad_mixed,
    conv,
    query,
    key,
    states,
    carry,
    halo,
    proj,
    taps,
    gap,
    grad_out,
    tail_out,
    edge_out,
    small_out,
    rows,
    grads,
):
    length = grad_mixed.shape[0]
    count = length // CHUNK
    rows[0:16, :] = halo[...].astype(F32)
    rows[16:, :] = proj[:, : 3 * HEAD_DIM].astype(F32)
    grads[0:PAD, :] = jnp.zeros((PAD, 3 * HEAD_DIM), F32)
    grads[PAD + length :, :] = jnp.zeros((PAD, 3 * HEAD_DIM), F32)
    lower = triangle(True)
    ones = lower.astype(F32)
    upper = triangle(False).astype(F32)
    last_row = lax.broadcasted_iota(jnp.int32, (CHUNK, HEAD_DIM), 0) == CHUNK - 1
    back = carry[...]
    grad_gap = jnp.zeros((1, HEAD_DIM), F32)
    sums = [jnp.zeros((1, HEAD_DIM), F32) for _ in range(12)]
    for c in reversed(range(count)):
        at = c * CHUNK
        here = slice(at, at + CHUNK)
        c0, c1, values = (conv[here, j * HEAD_DIM : (j + 1) * HEAD_DIM] for j in range(3))
        s1 = jax.nn.sigmoid(c1)
        open_share = 1.0 - s1
        keys = gap[...] * open_share
        forget = 1.0 - keys
        running = mul(ones, jnp.log(forget), 1, 0)
        last = running[CHUNK - 1 : CHUNK, :]
        grown, shrunk, rest = jnp.exp(running), jnp.exp(-running), jnp.exp(last - running)
        q, k, g = query[here, :], key[here, :], grad_mixed[here, :]
        carried = keys * rest
        state = states[c]
        scores = jnp.where(lower, mul(q, k, 1, 1), 0.0)
        grad_scores = jnp.where(lower, mul(g, values, 1, 1), 0.0)
        grad_values = mul(scores, g, 0, 0) + mul(carried, back, 1, 1)
        grad_query = mul(grad_scores, k, 1, 0) + mul(g, state, 1, 0)
        grad_key = mul(grad_scores, q, 0, 0)
        grad_carried = mul(values, back, 1, 0)
        grad_last = jnp.exp(last) * jnp.sum(back * state, axis=0, keepdims=True) + jnp.sum(
            grad_carried * carried, axis=0, keepdims=True
        )
        grad_running = grad_query * q - grad_key * k - grad_carried * carried
        grad_running = grad_running + jnp.where(last_row, grad_last, 0.0)
        grad_keys = grad_key * shrunk + grad_carried * rest
        grad_forget = mul(upper, grad_running, 1, 0) / forget
        inner = grad_forget - grad_keys
        grad_gap = grad_gap - jnp.sum(open_share * inner, axis=0, keepdims=True)
        sigmoid0 = jax.nn.sigmoid(c0)
        new = (
            grad_query * grown * (sigmoid0 * (1.0 + c0 * (1.0 - sigmoid0))),
            gap[...] * s1 * open_share * inner,
            grad_values,
        )
        back = back * jnp.exp(last) + mul(g, q, 0, 0)
        for j in range(3):
            cols = slice(j * HEAD_DIM, (j + 1) * HEAD_DIM)
            grads[PAD + at : PAD + at + CHUNK, cols] = new[j]
            for d in range(4):
                sums[4 * j + d] = sums[4 * j + d] + jnp.sum(
                    new[j] * rows[16 + at - d : 16 + at - d + CHUNK, cols], axis=0, keepdims=True
                )
            total = taps[4 * j : 4 * j + 1, :] * new[j]
            for d in range(1, 4):
                total = total + taps[4 * j + d : 4 * j + d + 1, :] * grads[PAD + at + d : PAD + at + d + CHUNK, cols]
            grad_out[here, cols] = total.astype(BF16)
            if c == count - 1:
                tail_out[:, cols] = total[CHUNK - 16 :]
    for j in range(3):
        cols = slice(j * HEAD_DIM, (j + 1) * HEAD_DIM)
        total = taps[4 * j + 1 : 4 * j + 2, :] * grads[1 : 1 + PAD, cols]
        for d in range(2, 4):
            total = total + taps[4 * j + d : 4 * j + d + 1, :] * grads[d : d + PAD, cols]
        edge_out[:, cols] = total
    for i in range(12):
        small_out[i : i + 1, :] = sums[i]
    small_out[12:13, :] = grad_gap
    small_out[13:16, :] = jnp.zeros((3, HEAD_DIM), F32)


def blocks_of(ids, count):
    member, core = ids[0], ids[1]
    for k in range(2):
        for b in range(count):
            yield k, b, (member ^ b) * 2 + (core ^ k)


def rows_of(blocks, first, count=STEP, cols=slice(None)):
    if isinstance(blocks, (tuple, list)):
        return jnp.concatenate([blocks[first + i][:, cols] for i in range(count)], axis=0)
    part = blocks[first : first + count, :, cols]
    return part.reshape(-1, part.shape[-1])


def fill_columns(weights, source, first, target, rows):
    groups, members, _, depth = source.shape
    per = max(1, 128 // depth)
    for at in range(0, groups * members, per):
        parts = [source[(at + i) // members, (at + i) % members, first : first + rows, :] for i in range(per)]
        part = parts[0] if per == 1 else jnp.concatenate(parts, axis=1)
        weights[target : target + rows, at * depth : (at + per) * depth] = part


def mix_blocks_kernel(mix, out_weight, out):
    groups, heads, depth, _ = out.shape
    for m in range(heads):
        cols = slice(m * HEAD_DIM, (m + 1) * HEAD_DIM)
        turned = out_weight[cols, :].astype(F32).T.astype(BF16)
        for g in range(groups):
            for j in range(4):
                out[g, m, :, j * HEAD_DIM : (j + 1) * HEAD_DIM] = mix[j, :, cols]
            out[g, m, :, 4 * HEAD_DIM :] = turned


def up_blocks_kernel(up, out, turned):
    _, _, units = up.shape
    groups, heads, rows, _ = out.shape
    rows = rows // 2
    for j in range(2):
        for t in range(units // 128):
            block = up[j, :, t * 128 : (t + 1) * 128].astype(F32)
            turned[t * 128 : (t + 1) * 128, :] = block.T.astype(BF16)
        for g in range(groups):
            for m in range(heads):
                out[g, m, j * rows : (j + 1) * rows, :] = turned[m * rows : (m + 1) * rows, :]


def project_kernel(ids, *refs, members):
    own, other = refs[:members], refs[members : 2 * members]
    weights, out, tail = refs[2 * members :]
    half = own[0].shape[0]
    blocks = list(blocks_of(ids, members))
    for at in range(0, len(blocks), STEP):
        k, b, _ = blocks[at]
        result = mul(rows_of((own, other)[k], b), weights[:, : 4 * HEAD_DIM], 1, 0, None).astype(BF16)
        for i in range(STEP):
            to = pl.multiple_of(blocks[at + i][2] * half, half)
            out[pl.ds(to, half), :] = result[i * half : (i + 1) * half]
    tail[...] = out[out.shape[0] - 16 :, : tail.shape[1]]


def feed_kernel(*refs, members):
    own, other, cot_own, cot_other = (refs[i * members : (i + 1) * members] for i in range(4))
    up, down, turned, inner_out, mine, away, weights = refs[4 * members :]
    half, width = own[0].shape
    units = down.shape[2]
    wide = turned.shape[0] // 3
    for j in range(3):
        weights[j * wide + units : (j + 1) * wide, :] = jnp.zeros((wide - units, width), BF16)
        fill_columns(weights, *((up, 0), (up, units), (down, 0))[j], j * wide, units)
    for k in range(2):
        for b in range(0, members, STEP):
            x = rows_of((own, other)[k], b)
            c = rows_of((cot_own, cot_other)[k], b)
            lifted = mul(x, weights[: 2 * wide], 1, 1, None)
            gate, up_in = lifted[:, :wide], lifted[:, wide:]
            grad = mul(c, weights[2 * wide :], 1, 1, None)
            s = jax.nn.sigmoid(gate)
            act = gate * s
            inner = act * up_in
            grad_gate = grad * up_in * (s * (1.0 + gate * (1.0 - s)))
            grad_up = grad * act
            at = (k * members + b) * half
            cols = slice(at, at + STEP * half)
            turned[0:wide, cols] = grad_gate.T.astype(BF16)
            turned[wide : 2 * wide, cols] = grad_up.T.astype(BF16)
            turned[2 * wide :, cols] = inner.T.astype(BF16)
            inner_out[cols, :] = inner.astype(BF16)
            lift = jnp.concatenate([grad_gate.astype(BF16), grad_up.astype(BF16)], axis=1)
            (mine, away)[k][b : b + STEP] = (
                mul(lift, weights[: 2 * wide], 1, 0, None).astype(BF16).reshape(STEP, half, width)
            )


def block_kernel(ids, inner, down, mine, away, weights):
    members, half, width = mine.shape
    units, wide = down.shape[2], inner.shape[1]
    weights[units:, :] = jnp.zeros((wide - units, width), BF16)
    fill_columns(weights, down, 0, 0, units)
    for k in range(2):
        for b in range(0, members, STEP):
            at = (k * members + b) * half
            result = mul(inner[at : at + STEP * half, :], weights[...], 1, 0, None).astype(BF16)
            for i in range(STEP):
                (mine, away)[k][ids[0] ^ (b + i)] = result[i * half : (i + 1) * half]


def store_shards(out, at, first, result):
    depth = out.shape[3]
    for i in range(result.shape[1] // depth):
        part = result[:, i * depth : (i + 1) * depth].astype(BF16)
        out[(at + i) // out.shape[1], (at + i) % out.shape[1], first : first + part.shape[0], :] = part


def product_into(out, first, turned, spans, own, other, members):
    rows = turned.shape[1] // 2
    width = out.shape[0] * out.shape[1] * out.shape[3]
    low, high = spans[0][0], spans[-1][1]
    for at in range(0, width, 256):
        cols = slice(at, at + 256)
        result = mul(turned[low:high, :rows], rows_of(own, 0, members, cols), 1, 0, None)
        result += mul(turned[low:high, rows:], rows_of(other, 0, members, cols), 1, 0, None)
        to = first
        for start, stop in spans:
            store_shards(out, at // out.shape[3], to, result[start - low : stop - low])
            to += stop - start


def feed_grad_kernel(*refs, members):
    own, other, cot_own, cot_other = (refs[i * members : (i + 1) * members] for i in range(4))
    turned, out = refs[4 * members :]
    units, wide = out.shape[2] // 3, turned.shape[0] // 3
    product_into(out, 0, turned, [(0, units), (wide, wide + units)], own, other, members)
    product_into(out, 2 * units, turned, [(2 * wide, 2 * wide + units)], cot_own, cot_other, members)


def mix_grad_kernel(*refs, members):
    own, other, branch_own, branch_other = (refs[i * members : (i + 1) * members] for i in range(4))
    turned, turned_gated, sums, out = refs[4 * members :]
    groups, heads, rows, _ = out.shape
    for g in range(groups):
        for m in range(heads):
            out[g, m, 5 * HEAD_DIM :, :] = sums[...]
    product_into(out, 0, turned, [(0, 4 * HEAD_DIM)], own, other, members)
    product_into(out, 4 * HEAD_DIM, turned_gated, [(0, HEAD_DIM)], branch_own, branch_other, members)


def project_back_kernel(ids, *refs, members):
    own, other = refs[:members], refs[members : 2 * members]
    grad3, tail, later, grad_gate, weights, norm_gain, turned, mine_out, away_out, norm_out, grads = refs[2 * members :]
    length = grad3.shape[0]
    members, half, width = mine_out.shape
    three = grad3.shape[1]
    grads[:, :three] = grad3[...]
    end = tail.shape[0]
    edge = jnp.concatenate([jnp.zeros((end - later.shape[0], three), F32), later[...]], axis=0)
    grads[length - end :, :three] = (tail[...] + edge).astype(BF16)
    grads[:, three:] = grad_gate[...]
    grad_norm = jnp.zeros((1, width), F32)
    parts = []
    for k, b, block in blocks_of(ids, members):
        parts.append(grads[pl.ds(pl.multiple_of(block * half, half), half), :])
        if len(parts) == STEP:
            x = jnp.concatenate(parts, axis=0)
            at = (k * members + b + 1 - STEP) * half
            turned[:, at : at + STEP * half] = x.astype(F32).T.astype(BF16)
            result = mul(x, weights[:, : 4 * HEAD_DIM], 1, 1, None)
            normed = rows_of((own, other)[k], b + 1 - STEP).astype(F32)
            grad_norm = grad_norm + jnp.sum(result * normed, axis=0, keepdims=True)
            (mine_out, away_out)[k][b + 1 - STEP : b + 1] = result.astype(BF16).reshape(STEP, half, width)
            parts = []
    norm_out[...] = jnp.broadcast_to(grad_norm / norm_gain[...], norm_out.shape)


def add_kernel(ids, blocks, got, out):
    for m in range(out.shape[0]):
        out[m] = (blocks[ids[0], m].astype(F32) + got[ids[1], m].astype(F32)).astype(BF16)


def mix_total_kernel(got, mix_out, out_out):
    groups, heads, _, depth = got.shape

    def total(i, rows):
        result = got[0, i, rows, :].astype(F32)
        for g in range(1, groups):
            result = result + got[g, i, rows, :].astype(F32)
        return result

    for i in range(heads):
        cols = slice(i * HEAD_DIM, (i + 1) * HEAD_DIM)
        for j in range(4):
            mix_out[j, :, cols] = total(i, slice(j * HEAD_DIM, (j + 1) * HEAD_DIM)).T
        out_out[cols, :] = total(i, slice(4 * HEAD_DIM, 5 * HEAD_DIM))


def feed_total_kernel(got, up_out, down_out, rows):
    heads, three, depth = got.shape
    units = three // 3
    for j in range(2):
        for i in range(heads):
            rows[i * units : (i + 1) * units, :] = got[i, j * units : (j + 1) * units, :].astype(F32)
        for t in range(heads * units // 128):
            up_out[j, :, t * 128 : (t + 1) * 128] = rows[t * 128 : (t + 1) * 128, :].T
    for i in range(heads):
        down_out[i * units : (i + 1) * units, :] = got[i, 2 * units :, :].astype(F32)


def call(kernel, outs, args, scratch=(), ids=None, behind=(), us=5):
    specs = [pl.BlockSpec(memory_space=pltpu.VMEM)] * len(args)
    if ids is not None:
        specs = [pl.BlockSpec(memory_space=pltpu.SMEM)] + specs
        args = (ids,) + tuple(args)
    real = len(args)

    def body(*refs):
        kernel(*refs[:real], *refs[real + len(behind) :])

    return pl.pallas_call(
        body,
        out_shape=[jax.ShapeDtypeStruct(s, d) for s, d in outs],
        in_specs=specs + [pl.BlockSpec(memory_space=pl.ANY)] * len(behind),
        out_specs=[pl.BlockSpec(memory_space=pltpu.VMEM)] * len(outs),
        scratch_shapes=list(scratch),
        compiler_params=pltpu.CompilerParams(vmem_limit_bytes=VMEM_LIMIT),
        cost_estimate=pl.CostEstimate(flops=0, bytes_accessed=us * 3000000, transcendentals=0),
    )(*args, *behind)


class Group:
    def __init__(self, heads):
        self.size = heads
        self.peers = lax.axis_size("seq")
        self.count = self.peers // heads
        self.member = lax.rem(lax.axis_index("seq"), heads)
        self.index = lax.div(lax.axis_index("seq"), heads)
        self.core = lax.axis_index("head")
        self.ids = jnp.stack([self.member, self.core]).astype(jnp.int32)
        self.lists = [list(range(g * heads, (g + 1) * heads)) for g in range(self.count)]
        self.columns = [list(range(m, self.peers, heads)) for m in range(heads)]

    def swap(self, value, bits):
        return lax.ppermute(value, "seq", [(s, s ^ bits) for s in range(self.peers)])

    def other_core(self, value):
        return lax.ppermute(value, "head", [(0, 1), (1, 0)])

    def shift(self, value, groups):
        step = groups * self.size
        pairs = [(s, s + step) for s in range(self.peers) if 0 <= s + step < self.peers]
        return lax.ppermute(value, "seq", pairs)

    def carry(self, state, decay, sign):
        total = None
        for k in reversed(range(1, self.count)):
            new = self.shift(state, sign * k)
            total = new if total is None else new + total * self.shift(decay, sign * k)
        return jnp.zeros_like(state) if total is None else total

    def gather(self, half):
        got = {0: half}
        for bits in (4, 1, 2):
            got[bits] = self.swap(half, bits)
        got[6] = self.swap(got[4], 2)
        got[5] = self.swap(got[4], 1)
        got[3] = self.swap(got[2], 1)
        got[7] = self.swap(got[5], 2)
        own = [got[bits] for bits in range(self.size)]
        return own, [self.other_core(block) for block in own]

    def scatter(self, mine, away, meanwhile=None):
        other = self.other_core(away)
        part = [mine[b].astype(F32) + other[b].astype(F32) for b in range(self.size)]

        def add(to, source, bits):
            part[to] = part[to] + self.swap(part[source].astype(BF16), bits).astype(F32)

        add(5, 7, 2)
        add(2, 3, 1)
        add(4, 6, 2)
        add(0, 1, 1)
        if meanwhile is not None:
            part[5] = after(part[5], meanwhile)
        add(4, 5, 1)
        add(0, 2, 2)
        add(0, 4, 4)
        return part[0]

    def spread(self, blocks):
        return lax.all_to_all(blocks, "seq", 0, 0, axis_index_groups=self.lists, tiled=True)

    def all_groups(self, value):
        return lax.all_gather(value, "seq", axis_index_groups=self.columns)

    def over_groups(self, blocks, behind):
        if self.count == 2:
            away = lax.dynamic_index_in_dim(blocks, 1 - self.index, 0, False)
            (total,) = call(
                add_kernel,
                [(away.shape, BF16)],
                (blocks, self.all_groups(away)),
                (),
                jnp.stack([self.index, 1 - self.index]).astype(jnp.int32),
                behind,
            )
            return total
        return lax.psum_scatter(blocks, "seq", axis_index_groups=self.columns)


def inverse_of(rows):
    return lax.rsqrt(jnp.mean(rows * rows, axis=-1, keepdims=True) + EPS_TOKEN)


def norm_back(rows, inverse, gain, grad):
    scaled = grad * gain
    dot_term = jnp.mean(scaled * rows, axis=-1, keepdims=True)
    grad_rows = inverse * scaled - rows * (inverse * inverse * inverse) * dot_term
    return grad_rows, jnp.sum(grad * rows * inverse, axis=0)


def after(value, *earlier):
    return lax.optimization_barrier((value,) + earlier)[0]


def shards(
    tokens,
    norm1_gain,
    mix_weight,
    conv_weight,
    decay_gap,
    group_gain,
    out_weight,
    norm2_gain,
    up_pair,
    down_weight,
    cotangent,
):
    depth = mix_weight.shape[1]
    heads = mix_weight.shape[2] // HEAD_DIM
    units = down_weight.shape[0] // heads
    wide = -(-units // 128) * 128
    local, width = tokens.shape
    half = local // 2
    group = Group(heads)
    ids, member, core = group.ids, group.member, group.core
    length = heads * local
    count = length // CHUNK
    groups, peers = group.count, group.peers

    def my_half(rows):
        return lax.dynamic_slice_in_dim(rows, core * half, half, 0)

    def own_head(array):
        return lax.dynamic_slice_in_dim(array, member * HEAD_DIM, HEAD_DIM, array.ndim - 1)

    taps = own_head(conv_weight).reshape(12, HEAD_DIM)
    gap = own_head(decay_gap).reshape(1, HEAD_DIM)
    gain = own_head(group_gain).reshape(1, HEAD_DIM)

    token_rows = tokens.astype(F32)
    inverse1 = inverse_of(token_rows)
    half_tokens = my_half(token_rows)
    half_inverse1 = my_half(inverse1)
    cot_half = my_half(cotangent)
    down_here = group.spread(down_weight.reshape(heads, units, depth))
    normed1, normed1_other = group.gather((half_tokens * half_inverse1 * norm1_gain).astype(BF16))
    cot, cot_other = group.gather(cot_half)
    (mix_blocks,) = call(
        mix_blocks_kernel,
        [((groups, heads, depth, 5 * HEAD_DIM), BF16)],
        (mix_weight, out_weight),
        (),
        None,
        (normed1[5], cot[5], down_here),
    )
    mix_own = lax.all_to_all(mix_blocks.reshape(peers, depth, 5 * HEAD_DIM), "seq", 0, 0, tiled=True)
    mix_own = mix_own.reshape(width, 5 * HEAD_DIM)
    (up_blocks,) = call(
        up_blocks_kernel,
        [((groups, heads, 2 * units, depth), BF16)],
        (up_pair,),
        [pltpu.VMEM((heads * units, depth), BF16)],
        None,
        (mix_blocks,),
        3,
    )
    down_own = group.all_groups(down_here)
    projected, tail = call(
        functools.partial(project_kernel, members=heads),
        [((length, 4 * HEAD_DIM), BF16), ((16, 3 * HEAD_DIM), BF16)],
        (*normed1, *normed1_other, mix_own),
        (),
        ids,
    )
    halo = group.shift(tail, 1)

    def many(n, dtype=F32):
        return ((length, n * HEAD_DIM), dtype)

    square = ((HEAD_DIM, HEAD_DIM), F32)
    all_rows = ((heads, half, width), BF16)
    conv, query, key, totals, states, mixed_here, last = call(
        forward_kernel,
        [
            many(3),
            many(1),
            many(1),
            ((count, HEAD_DIM), F32),
            ((count, HEAD_DIM, HEAD_DIM), F32),
            many(1),
            ((HEAD_DIM + PAD, HEAD_DIM), F32),
        ],
        (projected, halo, taps, gap),
        [pltpu.VMEM((length + 16, 3 * HEAD_DIM), F32)],
        None,
        cot_other,
    )
    own_decay = last[HEAD_DIM : HEAD_DIM + 1]
    carry = group.carry(last[:HEAD_DIM], own_decay, 1)
    up_own = lax.all_to_all(
        after(up_blocks.reshape(peers, 2 * units, depth), carry), "seq", 0, 0, tiled=True
    )
    up_own = up_own.reshape(groups, heads, 2 * units, depth)
    mixed, states, turned_gated, mine, away = call(
        gate_kernel,
        [many(1), ((count, HEAD_DIM, HEAD_DIM), F32), ((HEAD_DIM, length), BF16), all_rows, all_rows],
        (mixed_here, query, totals, states, carry, projected, gain, mix_own),
        [pltpu.VMEM((length, HEAD_DIM), BF16)],
        ids,
    )
    hidden = half_tokens + group.scatter(mine, away, up_own)
    inverse2 = inverse_of(hidden)
    normed2, normed2_other = group.gather((hidden * inverse2 * norm2_gain).astype(BF16))

    turned, inner, mine, away = call(
        functools.partial(feed_kernel, members=heads),
        [((3 * wide, length), BF16), ((length, wide), BF16), all_rows, all_rows],
        (*normed2, *normed2_other, *cot, *cot_other, up_own, down_own),
        [pltpu.VMEM((3 * wide, width), BF16)],
        us=17,
    )
    (grad_feed,) = call(
        functools.partial(feed_grad_kernel, members=heads),
        [((groups, heads, 3 * units, depth), BF16)],
        (*normed2, *normed2_other, *cot, *cot_other, turned),
        us=10,
    )
    grad_normed2 = group.scatter(mine, away, grad_feed)
    grad_hidden_norm, grad_norm2 = norm_back(hidden, inverse2, norm2_gain, grad_normed2)
    grad_hidden = cot_half.astype(F32) + grad_hidden_norm
    branch, branch_other = group.gather(grad_hidden.astype(BF16))

    decays = jnp.exp(jnp.concatenate([totals[1:] - totals[:-1], jnp.log(own_decay) - totals[-1:]], axis=0))
    grad_mixed, grad_gate_rows, grad_group, start_grad = call(
        functools.partial(gate_back_kernel, members=heads),
        [many(1), many(1, BF16), ((PAD, HEAD_DIM), F32), square],
        (*branch, *branch_other, mix_own, mixed, projected, gain, query, decays),
        [pltpu.VMEM((length, HEAD_DIM), F32)],
        ids,
    )
    back_carry = group.carry(start_grad, own_decay, -1)
    grad_rows3, grad_tail, edge, small = call(
        backward_kernel,
        [many(3, BF16), ((16, 3 * HEAD_DIM), F32), ((PAD, 3 * HEAD_DIM), F32), ((16, HEAD_DIM), F32)],
        (grad_mixed, conv, query, key, states, back_carry, halo, projected, taps, gap),
        [
            pltpu.VMEM((length + 16, 3 * HEAD_DIM), F32),
            pltpu.VMEM((length + 2 * PAD, 3 * HEAD_DIM), F32),
        ],
    )
    later = group.shift(edge, -1)
    turned_mix, mine, away, grad_norm1 = call(
        functools.partial(project_back_kernel, members=heads),
        [((4 * HEAD_DIM, length), BF16), all_rows, all_rows, ((PAD, width), F32)],
        (
            *normed1,
            *normed1_other,
            grad_rows3,
            grad_tail,
            later,
            grad_gate_rows,
            mix_own,
            norm1_gain.reshape(1, width),
        ),
        [pltpu.VMEM((length, 4 * HEAD_DIM), BF16)],
        ids,
    )
    sums = jnp.concatenate([small[:13].reshape(-1), grad_group[0], grad_norm1[0], grad_norm2]).astype(BF16)
    extra = -(-sums.shape[0] // (16 * depth)) * 16
    sums = jnp.pad(sums, (0, extra * depth - sums.shape[0])).reshape(extra, depth)
    (grad_mix,) = call(
        functools.partial(mix_grad_kernel, members=heads),
        [((groups, heads, 5 * HEAD_DIM + extra, depth), BF16)],
        (*normed1, *normed1_other, *branch, *branch_other, turned_mix, turned_gated, sums),
        us=7,
    )
    feed_total = group.over_groups(grad_feed, (grad_mix,))
    grad_mix = after(grad_mix.reshape(peers, 5 * HEAD_DIM + extra, depth), feed_total)
    mix_got = lax.all_to_all(grad_mix, "seq", 0, 0, tiled=True)
    grad_normed1 = group.scatter(mine, after(away, grad_mix))
    feed_got = group.spread(after(feed_total, mix_got))
    mix_total, out_total = call(
        mix_total_kernel,
        [((4, depth, heads * HEAD_DIM), F32), ((heads * HEAD_DIM, depth), F32)],
        (mix_got.reshape(groups, heads, 5 * HEAD_DIM + extra, depth),),
    )
    grad_rows1 = norm_back(half_tokens, half_inverse1, norm1_gain, grad_normed1)[0]
    grad_tokens = grad_hidden + grad_rows1

    up_total, down_total = call(
        feed_total_kernel,
        [((2, depth, heads * units), F32), ((heads * units, depth), F32)],
        (feed_got,),
        [pltpu.VMEM((heads * units, depth), F32)],
    )
    (block_mine, block_away) = call(
        block_kernel, [all_rows, all_rows], (inner, down_own), [pltpu.VMEM((wide, width), BF16)], ids, (grad_mix,)
    )
    block = (block_mine.astype(F32) + group.other_core(block_away).astype(F32)).astype(BF16)
    block_half = hidden + lax.psum_scatter(block, "seq", axis_index_groups=group.lists).astype(F32)

    def both_halves(rows):
        other = group.other_core(rows)
        return jnp.where(core == 0, jnp.concatenate([rows, other], 0), jnp.concatenate([other, rows], 0))

    block_out = both_halves(block_half)
    grad_tokens = both_halves(grad_tokens)
    inverse2 = both_halves(inverse2)

    sums = mix_got[:, 5 * HEAD_DIM :].reshape(groups, heads, -1).astype(F32).sum(0)
    own_sums = sums[:, : 14 * HEAD_DIM].reshape(heads, 14, HEAD_DIM).transpose(1, 0, 2).reshape(14, heads * HEAD_DIM)
    norms = sums[:, 14 * HEAD_DIM : 14 * HEAD_DIM + 2 * width].sum(0).reshape(2, width)
    norms = norms + group.other_core(norms)
    inverse_rms = jnp.stack([inverse1[:, 0], inverse2[:, 0]])
    return (
        block_out,
        grad_tokens,
        norms[0],
        mix_total,
        own_sums[:12].reshape(3, 4, heads * HEAD_DIM),
        own_sums[12],
        own_sums[13],
        out_total,
        norms[1],
        up_total,
        down_total,
        inverse_rms,
    )


def solution(mesh):
    in_specs = (
        P("seq", None),
        P(),
        P(None, "seq", "head"),
        P(None, None, "head"),
        P("head"),
        P("head"),
        P("head", "seq"),
        P(),
        P(None, "seq", "head"),
        P("head", "seq"),
        P("seq", None),
    )
    out_specs = (
        P("seq", None),
        P("seq", None),
        P(),
        P(None, "seq", "head"),
        P(None, None, "head"),
        P("head"),
        P("head"),
        P("head", "seq"),
        P(),
        P(None, "seq", "head"),
        P("head", "seq"),
        P(None, "seq"),
    )
    return jax.shard_map(shards, mesh=mesh, in_specs=in_specs, out_specs=out_specs, check_vma=False)
```

time: 709 us -> 609 us (0.86)
  Pallas kernels: 16.7 us -> 88 us
  local copies, waits for them, and re-layouts: 118 us -> 54.4 us
  matrix products: 47.4 us -> 0 us
  starting transfers between devices: 132 us -> 106 us
  other arithmetic: 56.6 us -> 36.4 us
  waiting for transfers between devices: 309 us -> 297 us
    ppermute x49, waiting for transfers between devices: 106 us -> 236 us  [swap(): lax.ppermute(value, 'seq', [(s, s ^ bits) for s in range(self.peers)])]
    psum x1 -> x0, waiting for transfers between devices: 103 us -> none  [shards(): lax.psum((placed, jnp.stack([grad_norm1, grad_norm2])), 'seq')]
    pallas_call x4 -> x15, Pallas kernels: 16.7 us -> 88 us  [call(): pl.pallas_call(body, out_shape=[jax.ShapeDtypeStruct(s, d) for s, d in ou...]
    dot_general x12 -> x0, matrix products: 47.4 us -> none  [mul(): lax.dot_general(a, b, (((ca,), (cb,)), ((), ())), precision=precision, pr...]
    ppermute x4, waiting for transfers between devices: 58.4 us -> 12.9 us  [shift(): return lax.ppermute(value, 'seq', pairs)]
    dynamic_update_slice x29 -> x0, local copies, waits for them, and re-layouts: 33.4 us -> none  [gather(): own = lax.dynamic_update_index_in_dim(own, got[bits], self.member ^ bits, 0)]
    all_to_all x9 -> x5, starting transfers between devices: 56.1 us -> 29.6 us  [the longest x2 10.4 us: spread(): lax.all_to_all(blocks, 'seq', 0, 0, axis_index_groups=self.lists, tiled=T...]
    unnamed x80 -> x200, local copies, waits for them, and re-layouts: 20 us -> 44.3 us
  transfers between devices with their start and end apart: 77 -> 101, of which waited for: 31 -> 45; matrix products, arithmetic and copies ran while one was open for 25% -> 8% of each run, Pallas kernels for 2% -> 9%
where the time goes in v2:
time: 609 us; the launch traced here: 597 us
  waiting for transfers between devices  297 us (49%)
  starting transfers between devices  106 us (17%)
  Pallas kernels  88 us (14%)
  local copies, waits for them, and re-layouts  54.4 us (9%)
  other arithmetic  36.4 us (6%)
  between operations  15 us (2%)
    ppermute x49, waiting for transfers between devices, swap(): lax.ppermute(value, 'seq', [(s, s ^ bits) for s in range(self.peers)])  236 us
    pallas_call x15, Pallas kernels, call(): pl.pallas_call(body, out_shape=[jax.ShapeDtypeStruct(s, d) for s, d in ou...  88 us
    ppermute x49, starting transfers between devices, swap(): lax.ppermute(value, 'seq', [(s, s ^ bits) for s in range(self.peers)])  48.2 us
    unnamed x200, local copies, waits for them, and re-layouts  44.3 us
    all_to_all x1, waiting for transfers between devices, shards(): lax.all_to_all(after(up_blocks.reshape(peers, 2 * units, depth), carry),...  23.6 us
    ppermute x40, waiting for transfers between devices, other_core(): return lax.ppermute(value, 'head', [(0, 1), (1, 0)])  13.8 us
    ppermute x4, waiting for transfers between devices, shift(): return lax.ppermute(value, 'seq', pairs)  12.9 us
    convert_element_type x7, other arithmetic, add(): part[to] = part[to] + self.swap(part[source].astype(BF16), bits).astype(F32)  12.2 us
  transfers between devices with their start and end apart: 101, of which 45 were waited for; matrix products, arithmetic and copies ran while one was open for 8% of the time, Pallas kernels for 9%

profile of v2, /device:TPU:18, one launch (start us, length us, event | category | flops | bytes accessed | tf_op | source)
XLA Modules:
  0.0 596.9 jit_solution(14377822551526059789)
XLA Ops:
  16.3 13.1 %collective-permute-done.15.refs_20_ = bf16[64,2048]{1,0:T(8,128)(2,1)} collective-permute-done((bf16[64,2048]{1,0:T(8,128)(2,1)S(1)}, bf16[64,2048]{1,0:T(8,128)(2,1)}, u32[]{:S(2)}, u32[]{:S(2)}) %collective-permute-start.15) | collective-permute-done | bytes 262176 | tf_op jit(solution)/shard_map/ppermute | solution.py:479
  44.9 6.0 %all-to-all-start.1 = ((bf16[16,128,640]{2,1,0:T(8,128)(2,1)}), bf16[16,128,640]{2,1,0:T(8,128)(2,1)}, u32[]{:S(2)}, u32[]{:S(2)}) async-start(bf16[16,128,640]{2,1,0:T(8,128)(2,1)} %bitcast.3), calls=%async_computation.1 | async-start | bytes 5242880 | tf_op jit(solution)/shard_map/all_to_all | solution.py:612
  54.0 20.8 %collective-permute-done.21.refs_18_ = bf16[64,2048]{1,0:T(8,128)(2,1)S(1)} collective-permute-done((bf16[64,2048]{1,0:T(8,128)(2,1)S(1)}, bf16[64,2048]{1,0:T(8,128)(2,1)S(1)}, u32[]{:S(2)}, u32[]{:S(2)}) %collective-permute-start.21) | collective-permute-done | bytes 262176 | tf_op jit(solution)/shard_map/ppermute | solution.py:479
  82.1 19.0 %collective-permute-done.refs_2_.refs_1_ = bf16[64,2048]{1,0:T(8,128)(2,1)S(1)} collective-permute-done((bf16[64,2048]{1,0:T(8,128)(2,1)S(1)}, bf16[64,2048]{1,0:T(8,128)(2,1)S(1)}, u32[]{:S(2)}, u32[]{:S(2)}) %collective-permute-start) | collective-permute-done | bytes 262176 | tf_op jit(solution)/shard_map/ppermute | solution.py:479
  169.2 6.0 %all-to-all-start.2 = ((bf16[16,704,128]{2,1,0:T(8,128)(2,1)}), bf16[16,704,128]{2,1,0:T(8,128)(2,1)}, u32[]{:S(2)}, u32[]{:S(2)}) async-start(bf16[16,704,128]{2,1,0:T(8,128)(2,1)} %bitcast.139), calls=%async_computation.2 | async-start | bytes 5767168 | tf_op jit(solution)/shard_map/all_to_all | solution.py:656
  175.3 11.2 %all-gather.6.cloned.1.call-start = ((), (), s32[]{:S(2)}) async-start(), calls=%async_computation.8 | async-start | bytes 2162688 | tf_op jit(solution)/shard_map/all_gather | solution.py:529
  203.6 10.4 %collective-permute-done.37 = bf16[64,2048]{1,0:T(8,128)(2,1)S(1)} collective-permute-done((bf16[64,2048]{1,0:T(8,128)(2,1)S(1)}, bf16[64,2048]{1,0:T(8,128)(2,1)S(1)}, u32[]{:S(2)}, u32[]{:S(2)}) %collective-permute-start.37) | collective-permute-done | bytes 262176 | tf_op jit(solution)/shard_map/ppermute | solution.py:479
  214.8 23.6 %all-to-all-done.2 = bf16[16,704,128]{2,1,0:T(8,128)(2,1)} async-done(((bf16[16,704,128]{2,1,0:T(8,128)(2,1)}), bf16[16,704,128]{2,1,0:T(8,128)(2,1)}, u32[]{:S(2)}, u32[]{:S(2)}) %all-to-all-start.2) | async-done | bytes 2883616 | tf_op jit(solution)/shard_map/all_to_all | solution.py:656
  240.5 6.9 %collective-permute-done.38 = bf16[64,2048]{1,0:T(8,128)(2,1)S(1)} collective-permute-done((bf16[64,2048]{1,0:T(8,128)(2,1)}, bf16[64,2048]{1,0:T(8,128)(2,1)S(1)}, u32[]{:S(2)}, u32[]{:S(2)}) %collective-permute-start.38) | collective-permute-done | bytes 262176 | tf_op jit(solution)/shard_map/ppermute | solution.py:479
  250.2 6.0 %collective-permute-done.35 = bf16[64,2048]{1,0:T(8,128)(2,1)S(1)} collective-permute-done((bf16[64,2048]{1,0:T(8,128)(2,1)}, bf16[64,2048]{1,0:T(8,128)(2,1)S(1)}, u32[]{:S(2)}, u32[]{:S(2)}) %collective-permute-start.35) | collective-permute-done | bytes 262176 | tf_op jit(solution)/shard_map/ppermute | solution.py:479
  262.8 8.5 %collective-permute-done.43.refs_4_ = bf16[64,2048]{1,0:T(8,128)(2,1)S(1)} collective-permute-done((bf16[64,2048]{1,0:T(8,128)(2,1)S(1)}, bf16[64,2048]{1,0:T(8,128)(2,1)S(1)}, u32[]{:S(2)}, u32[]{:S(2)}) %collective-permute-start.43) | collective-permute-done | bytes 262176 | tf_op jit(solution)/shard_map/ppermute | solution.py:479
  292.9 16.8 %shard_map.207 = (bf16[1152,1024]{1,0:T(8,128)(2,1)}, bf16[1024,384]{1,0:T(8,128)(2,1)}, bf16[8,64,2048]{2,1,0:T(8,128)(2,1)}, bf16[8,64,2048]{2,1,0:T(8,128)(2,1)}) custom-call(bf16[64,2048]{1,0:T(8,128)(2,1)S(1)} %multiply_convert_fusion.refs_0_, bf16[64,2048]{1,0:T(8,128)(2,1)} %collective-permute-done.40.refs_1_, ...), custom_call_target="tpu_custom_call" | custom-call | bytes 51000000 | tf_op jit(solution)/shard_map/pallas_call | solution.py:455
  311.7 10.5 %shard_map.208.refs_1_ = bf16[2,8,1056,128]{3,2,1,0:T(8,128)(2,1)} custom-call(bf16[64,2048]{1,0:T(8,128)(2,1)S(1)} %multiply_convert_fusion.refs_0_, bf16[64,2048]{1,0:T(8,128)(2,1)} %collective-permute-done.40.refs_1_, bf16[64,2048]{1,0:T(8,128)(2,1)S(1)} %collective-permute-done.41.refs_2_, bf16[64,2048]{1,0:T(8,128)(2,1)} %collective-permute-done.42.refs_3_, ...), custom_call_target="tpu_custom_call" | custom-call | bytes 30000000 | tf_op jit(solution)/shard_map/pallas_call | solution.py:455
  352.0 9.3 %collective-permute-done.62 = bf16[64,2048]{1,0:T(8,128)(2,1)S(1)} collective-permute-done((bf16[64,2048]{1,0:T(8,128)(2,1)S(1)}, bf16[64,2048]{1,0:T(8,128)(2,1)S(1)}, u32[]{:S(2)}, u32[]{:S(2)}) %collective-permute-start.62) | collective-permute-done | bytes 262176 | tf_op jit(solution)/shard_map/ppermute | solution.py:479
  364.7 12.6 %collective-permute-done.66.refs_5_.refs_20_ = bf16[64,2048]{1,0:T(8,128)(2,1)S(1)} collective-permute-done((bf16[64,2048]{1,0:T(8,128)(2,1)S(1)}, bf16[64,2048]{1,0:T(8,128)(2,1)S(1)}, u32[]{:S(2)}, u32[]{:S(2)}) %collective-permute-start.66) | collective-permute-done | bytes 262176 | tf_op jit(solution)/shard_map/ppermute | solution.py:479
  405.8 8.2 %shard_map.210 = (bf16[1024,384]{1,0:T(8,128)(2,1)S(1)}, f32[16,384]{1,0:T(8,128)S(1)}, f32[8,384]{1,0:T(8,128)S(1)}, f32[16,128]{1,0:T(8,128)S(1)}) custom-call(f32[1024,128]{1,0:T(8,128)S(1)} %get-tuple-element.71.refs_0_, f32[1024,384]{1,0:T(8,128)S(1)} %copy-done.52, f32[1024,128]{1,0:T(8,128)S(1)} %get-tuple-element.57.refs_2_.refs_21_, ...), custom_call_target="tpu_custom_call" | custom-call | bytes 15000000 | tf_op jit(solution)/shard_map/pallas_call | solution.py:455
  420.9 6.8 %shard_map.211 = (bf16[512,1024]{1,0:T(8,128)(2,1)}, bf16[8,64,2048]{2,1,0:T(8,128)(2,1)}, bf16[8,64,2048]{2,1,0:T(8,128)(2,1)}, f32[8,2048]{1,0:T(8,128)S(1)}) custom-call(s32[2]{0:T(128)S(1)} %pad_add_fusion.refs_0_, bf16[64,2048]{1,0:T(8,128)(2,1)S(1)} %multiply_convert_fusion.1.refs_1_.refs_0_, bf16[64,2048]{1,0:T(8,128)(2,1)S(1)} %copy-done.26, ...), custom_call_target="tpu_custom_call" | custom-call | bytes 15000000 | tf_op jit(solution)/shard_map/pallas_call | solution.py:455
  427.7 6.6 %shard_map.212.refs_3_ = bf16[2,8,688,128]{3,2,1,0:T(8,128)(2,1)} custom-call(bf16[64,2048]{1,0:T(8,128)(2,1)S(1)} %multiply_convert_fusion.1.refs_1_.refs_0_, bf16[64,2048]{1,0:T(8,128)(2,1)S(1)} %copy-done.26, bf16[64,2048]{1,0:T(8,128)(2,1)S(1)} %copy-done.23, bf16[64,2048]{1,0:T(8,128)(2,1)} %collective-permute-done.2.refs_4_.refs_3_, ...), custom_call_target="tpu_custom_call" | custom-call | bytes 21000000 | tf_op jit(solution)/shard_map/pallas_call | solution.py:455
  441.0 7.2 %all-to-all-start.3 = ((bf16[16,688,128]{2,1,0:T(8,128)(2,1)}), bf16[16,688,128]{2,1,0:T(8,128)(2,1)S(1)}, u32[]{:S(2)}, u32[]{:S(2)}) async-start(bf16[16,688,128]{2,1,0:T(8,128)(2,1)} %bitcast.30.refs_3_), calls=%async_computation.4 | async-start | bytes 5636096 | tf_op jit(solution)/shard_map/all_to_all | solution.py:735
  455.7 6.8 %collective-permute-done.80 = bf16[8,64,2048]{2,1,0:T(8,128)(2,1)S(1)} collective-permute-done((bf16[8,64,2048]{2,1,0:T(8,128)(2,1)}, bf16[8,64,2048]{2,1,0:T(8,128)(2,1)S(1)}, u32[]{:S(2)}, u32[]{:S(2)}) %collective-permute-start.80) | collective-permute-done | bytes 2097184 | tf_op jit(solution)/shard_map/ppermute | solution.py:482
  470.1 11.2 %collective-permute-done.87 = bf16[64,2048]{1,0:T(8,128)(2,1)S(1)} collective-permute-done((bf16[64,2048]{1,0:T(8,128)(2,1)S(1)}, bf16[64,2048]{1,0:T(8,128)(2,1)S(1)}, u32[]{:S(2)}, u32[]{:S(2)}) %collective-permute-start.87) | collective-permute-done | bytes 262176 | tf_op jit(solution)/shard_map/ppermute | solution.py:479
  481.3 30.5 %collective-permute-done.84 = bf16[64,2048]{1,0:T(8,128)(2,1)S(1)} collective-permute-done((bf16[64,2048]{1,0:T(8,128)(2,1)S(1)}, bf16[64,2048]{1,0:T(8,128)(2,1)S(1)}, u32[]{:S(2)}, u32[]{:S(2)}) %collective-permute-start.84) | collective-permute-done | bytes 262176 | tf_op jit(solution)/shard_map/ppermute | solution.py:479
  516.0 17.4 %collective-permute-done.88 = bf16[64,2048]{1,0:T(8,128)(2,1)S(1)} collective-permute-done((bf16[64,2048]{1,0:T(8,128)(2,1)S(1)}, bf16[64,2048]{1,0:T(8,128)(2,1)S(1)}, u32[]{:S(2)}, u32[]{:S(2)}) %collective-permute-start.88) | collective-permute-done | bytes 262176 | tf_op jit(solution)/shard_map/ppermute | solution.py:479
  540.3 16.5 %collective-permute-done.83 = bf16[64,2048]{1,0:T(8,128)(2,1)} collective-permute-done((bf16[64,2048]{1,0:T(8,128)(2,1)}, bf16[64,2048]{1,0:T(8,128)(2,1)}, u32[]{:S(2)}, u32[]{:S(2)}) %collective-permute-start.83) | collective-permute-done | bytes 262176 | tf_op jit(solution)/shard_map/ppermute | solution.py:479
  (453 shorter events, 289.9 us)
Async XLA Ops:
  7.2 34.3 %all-to-all-start = ((bf16[8,352,128]{2,1,0:T(8,128)(2,1)}), bf16[8,352,128]{2,1,0:T(8,128)(2,1)S(1)}, u32[]{:S(2)}, u32[]{:S(2)}) async-start(bf16[8,352,128]{2,1,0:T(8,128)(2,1)} %bitcast.140), calls=%async_computation | async-start | bytes 1441792 | tf_op jit(solution)/shard_map/all_to_all | solution.py:526
  44.9 83.2 %all-to-all-start.1 = ((bf16[16,128,640]{2,1,0:T(8,128)(2,1)}), bf16[16,128,640]{2,1,0:T(8,128)(2,1)}, u32[]{:S(2)}, u32[]{:S(2)}) async-start(bf16[16,128,640]{2,1,0:T(8,128)(2,1)} %bitcast.3), calls=%async_computation.1 | async-start | bytes 5242880 | tf_op jit(solution)/shard_map/all_to_all | solution.py:612
  50.9 23.9 %collective-permute-start.21 = (bf16[64,2048]{1,0:T(8,128)(2,1)S(1)}, bf16[64,2048]{1,0:T(8,128)(2,1)S(1)}, u32[]{:S(2)}, u32[]{:S(2)}) collective-permute-start(bf16[64,2048]{1,0:T(8,128)(2,1)S(1)} %constant_dynamic-slice_fusion.2.refs_16_), channel_id=1, source_target_pairs={{0,4},{2,6},{4,0},{6,2},{8,12},{10,14},{12,8},{14,10},{16,20},{18,... | collective-permute-start | bytes 786440 | tf_op jit(solution)/shard_map/ppermute | solution.py:479
  52.4 22.4 %collective-permute-start.19 = (bf16[64,2048]{1,0:T(8,128)(2,1)S(1)}, bf16[64,2048]{1,0:T(8,128)(2,1)S(1)}, u32[]{:S(2)}, u32[]{:S(2)}) collective-permute-start(bf16[64,2048]{1,0:T(8,128)(2,1)S(1)} %constant_dynamic-slice_fusion.2.refs_16_), channel_id=1, source_target_pairs={{0,2},{2,0},{4,6},{6,4},{8,10},{10,8},{12,14},{14,12},{16,18},{18,... | collective-permute-start | bytes 786440 | tf_op jit(solution)/shard_map/ppermute | solution.py:479
  53.0 23.9 %collective-permute-start.18 = (bf16[64,2048]{1,0:T(8,128)(2,1)S(1)}, bf16[64,2048]{1,0:T(8,128)(2,1)S(1)}, u32[]{:S(2)}, u32[]{:S(2)}) collective-permute-start(bf16[64,2048]{1,0:T(8,128)(2,1)S(1)} %constant_dynamic-slice_fusion.2.refs_16_), channel_id=1, source_target_pairs={{0,1},{1,0},{2,3},{3,2},{4,5},{5,4},{6,7},{7,6},{8,9},{9,8},{10,11... | collective-permute-start | bytes 786440 | tf_op jit(solution)/shard_map/ppermute | solution.py:482
  53.0 24.6 %collective-permute-start.7 = (bf16[64,2048]{1,0:T(8,128)(2,1)S(1)}, bf16[64,2048]{1,0:T(8,128)(2,1)S(1)}, u32[]{:S(2)}, u32[]{:S(2)}) collective-permute-start(bf16[64,2048]{1,0:T(8,128)(2,1)S(1)} %multiply_convert_fusion.1.refs_1_.refs_0_), channel_id=1, source_target_pairs={{0,1},{1,0},{2,3},{3,2},{4,5},{5,4},{6,7},{7,6},{8,9},{9,8},{10,11... | collective-permute-start | bytes 786440 | tf_op jit(solution)/shard_map/ppermute | solution.py:482
  53.5 27.2 %collective-permute-start.1 = (bf16[64,2048]{1,0:T(8,128)(2,1)S(1)}, bf16[64,2048]{1,0:T(8,128)(2,1)S(1)}, u32[]{:S(2)}, u32[]{:S(2)}) collective-permute-start(bf16[64,2048]{1,0:T(8,128)(2,1)S(1)} %multiply_convert_fusion.1.refs_1_.refs_0_), channel_id=1, source_target_pairs={{0,4},{2,6},{4,0},{6,2},{8,12},{10,14},{12,8},{14,10},{16,20},{18,... | collective-permute-start | bytes 786440 | tf_op jit(solution)/shard_map/ppermute | solution.py:479
  74.8 26.3 %collective-permute-start = (bf16[64,2048]{1,0:T(8,128)(2,1)S(1)}, bf16[64,2048]{1,0:T(8,128)(2,1)S(1)}, u32[]{:S(2)}, u32[]{:S(2)}) collective-permute-start(bf16[64,2048]{1,0:T(8,128)(2,1)S(1)} %multiply_convert_fusion.1.refs_1_.refs_0_), channel_id=1, source_target_pairs={{0,2},{2,0},{4,6},{6,4},{8,10},{10,8},{12,14},{14,12},{16,18},{18,... | collective-permute-start | bytes 786440 | tf_op jit(solution)/shard_map/ppermute | solution.py:479
  74.8 29.9 %collective-permute-start.23 = (bf16[64,2048]{1,0:T(8,128)(2,1)S(1)}, bf16[64,2048]{1,0:T(8,128)(2,1)}, u32[]{:S(2)}, u32[]{:S(2)}) collective-permute-start(bf16[64,2048]{1,0:T(8,128)(2,1)S(1)} %collective-permute-done.21.refs_18_), channel_id=1, source_target_pairs={{0,2},{2,0},{4,6},{6,4},{8,10},{10,8},{12,14},{14,12},{16,18},{18,... | collective-permute-start | bytes 786440 | tf_op jit(solution)/shard_map/ppermute | solution.py:479
  76.8 27.9 %collective-permute-start.22 = (bf16[64,2048]{1,0:T(8,128)(2,1)S(1)}, bf16[64,2048]{1,0:T(8,128)(2,1)S(1)}, u32[]{:S(2)}, u32[]{:S(2)}) collective-permute-start(bf16[64,2048]{1,0:T(8,128)(2,1)S(1)} %collective-permute-done.21.refs_18_), channel_id=1, source_target_pairs={{0,1},{1,0},{2,3},{3,2},{4,5},{5,4},{6,7},{7,6},{8,9},{9,8},{10,11... | collective-permute-start | bytes 786440 | tf_op jit(solution)/shard_map/ppermute | solution.py:482
  78.3 26.5 %collective-permute-start.20 = (bf16[64,2048]{1,0:T(8,128)(2,1)S(1)}, bf16[64,2048]{1,0:T(8,128)(2,1)S(1)}, u32[]{:S(2)}, u32[]{:S(2)}) collective-permute-start(bf16[64,2048]{1,0:T(8,128)(2,1)S(1)} %collective-permute-done.19.refs_17_), channel_id=1, source_target_pairs={{0,1},{1,0},{2,3},{3,2},{4,5},{5,4},{6,7},{7,6},{8,9},{9,8},{10,11... | collective-permute-start | bytes 786440 | tf_op jit(solution)/shard_map/ppermute | solution.py:482
  80.7 27.4 %collective-permute-start.27 = (bf16[64,2048]{1,0:T(8,128)(2,1)}, bf16[64,2048]{1,0:T(8,128)(2,1)}, u32[]{:S(2)}, u32[]{:S(2)}) collective-permute-start(bf16[64,2048]{1,0:T(8,128)(2,1)} %collective-permute-done.15.refs_20_), channel_id=1, source_target_pairs={{0,4},{2,6},{4,0},{6,2},{8,12},{10,14},{12,8},{14,10},{16,20},{18,... | collective-permute-start | bytes 786440 | tf_op jit(solution)/shard_map/ppermute | solution.py:479
  169.2 69.2 %all-to-all-start.2 = ((bf16[16,704,128]{2,1,0:T(8,128)(2,1)}), bf16[16,704,128]{2,1,0:T(8,128)(2,1)}, u32[]{:S(2)}, u32[]{:S(2)}) async-start(bf16[16,704,128]{2,1,0:T(8,128)(2,1)} %bitcast.139), calls=%async_computation.2 | async-start | bytes 5767168 | tf_op jit(solution)/shard_map/all_to_all | solution.py:656
  175.3 115.7 %all-gather.6.cloned.1.call-start = ((), (), s32[]{:S(2)}) async-start(), calls=%async_computation.8 | async-start | bytes 2162688 | tf_op jit(solution)/shard_map/all_gather | solution.py:529
  202.5 38.0 %collective-permute-start.36 = (bf16[64,2048]{1,0:T(8,128)(2,1)S(1)}, bf16[64,2048]{1,0:T(8,128)(2,1)S(1)}, u32[]{:S(2)}, u32[]{:S(2)}) collective-permute-start(bf16[64,2048]{1,0:T(8,128)(2,1)S(1)} %get-tuple-element.121), channel_id=1, source_target_pairs={{0,4},{2,6},{4,0},{6,2},{8,12},{10,14},{12,8},{14,10},{16,20},{18,... | collective-permute-start | bytes 786440 | tf_op jit(solution)/shard_map/ppermute | solution.py:479
  203.1 37.4 %collective-permute-start.34 = (bf16[64,2048]{1,0:T(8,128)(2,1)S(1)}, bf16[64,2048]{1,0:T(8,128)(2,1)S(1)}, u32[]{:S(2)}, u32[]{:S(2)}) collective-permute-start(bf16[64,2048]{1,0:T(8,128)(2,1)S(1)} %get-tuple-element.122), channel_id=1, source_target_pairs={{0,2},{2,0},{4,6},{6,4},{8,10},{10,8},{12,14},{14,12},{16,18},{18,... | collective-permute-start | bytes 786440 | tf_op jit(solution)/shard_map/ppermute | solution.py:479
  250.1 185.5 %all-gather.4.cloned.1.call-start = ((), (), s32[]{:S(2)}) async-start(), calls=%async_computation.6 | async-start | bytes 6488064 | tf_op jit(solution)/shard_map/all_gather | solution.py:529
  441.0 94.3 %all-to-all-start.3 = ((bf16[16,688,128]{2,1,0:T(8,128)(2,1)}), bf16[16,688,128]{2,1,0:T(8,128)(2,1)S(1)}, u32[]{:S(2)}, u32[]{:S(2)}) async-start(bf16[16,688,128]{2,1,0:T(8,128)(2,1)} %bitcast.30.refs_3_), calls=%async_computation.4 | async-start | bytes 5636096 | tf_op jit(solution)/shard_map/all_to_all | solution.py:735
  448.2 129.8 %reduce-scatter.2.cloned.1.call-start = ((), (), s32[]{:S(2)}) async-start(), calls=%async_computation.7 | async-start | bytes 2359296 | tf_op jit(solution)/shard_map/reduce_scatter | solution.py:756
  468.9 42.9 %collective-permute-start.84 = (bf16[64,2048]{1,0:T(8,128)(2,1)S(1)}, bf16[64,2048]{1,0:T(8,128)(2,1)S(1)}, u32[]{:S(2)}, u32[]{:S(2)}) collective-permute-start(bf16[64,2048]{1,0:T(8,128)(2,1)S(1)} %get-tuple-element.110), channel_id=1, source_target_pairs={{0,2},{2,0},{4,6},{6,4},{8,10},{10,8},{12,14},{14,12},{16,18},{18,... | collective-permute-start | bytes 786440 | tf_op jit(solution)/shard_map/ppermute | solution.py:479
  469.5 46.5 %collective-permute-start.86 = (bf16[64,2048]{1,0:T(8,128)(2,1)S(1)}, bf16[64,2048]{1,0:T(8,128)(2,1)S(1)}, u32[]{:S(2)}, u32[]{:S(2)}) collective-permute-start(bf16[64,2048]{1,0:T(8,128)(2,1)S(1)} %get-tuple-element.109), channel_id=1, source_target_pairs={{0,4},{2,6},{4,0},{6,2},{8,12},{10,14},{12,8},{14,10},{16,20},{18,... | collective-permute-start | bytes 786440 | tf_op jit(solution)/shard_map/ppermute | solution.py:479
  514.0 42.9 %collective-permute-start.83 = (bf16[64,2048]{1,0:T(8,128)(2,1)}, bf16[64,2048]{1,0:T(8,128)(2,1)}, u32[]{:S(2)}, u32[]{:S(2)}) collective-permute-start(bf16[64,2048]{1,0:T(8,128)(2,1)} %get-tuple-element.107), channel_id=1, source_target_pairs={{0,2},{2,0},{4,6},{6,4},{8,10},{10,8},{12,14},{14,12},{16,18},{18,... | collective-permute-start | bytes 786440 | tf_op jit(solution)/shard_map/ppermute | solution.py:479
  516.0 40.9 %collective-permute-start.85 = (bf16[64,2048]{1,0:T(8,128)(2,1)}, bf16[64,2048]{1,0:T(8,128)(2,1)}, u32[]{:S(2)}, u32[]{:S(2)}) collective-permute-start(bf16[64,2048]{1,0:T(8,128)(2,1)} %get-tuple-element.111), channel_id=1, source_target_pairs={{0,4},{2,6},{4,0},{6,2},{8,12},{10,14},{12,8},{14,10},{16,20},{18,... | collective-permute-start | bytes 786440 | tf_op jit(solution)/shard_map/ppermute | solution.py:479
  535.3 50.8 %all-to-all-start.4 = ((bf16[8,1056,128]{2,1,0:T(8,128)(2,1)}), bf16[8,1056,128]{2,1,0:T(8,128)(2,1)}, u32[]{:S(2)}, u32[]{:S(2)}) async-start(bf16[8,1056,128]{2,1,0:T(8,128)(2,1)} %copy-done.4), calls=%async_computation.5 | async-start | bytes 4325376 | tf_op jit(solution)/shard_map/all_to_all | solution.py:526
  (177 other events, 1872.8 us)
Sparse Core Ops, SparseCore 0:
  250.3 40.6 all-gather.5
  328.6 106.9 all-gather.3
  465.0 112.9 reduce-scatter.1

commit v3 on v2

--- a/solution.py
+++ b/solution.py
@@ -16,7 +16,7 @@
 HIGH = lax.Precision.HIGHEST
 F32 = jnp.float32
 BF16 = jnp.bfloat16
-VMEM_LIMIT = 48 * 1024 * 1024
+MIB = 1024 * 1024
 
 
 def mul(a, b, ca, cb, precision=HIGH):
@@ -259,27 +259,26 @@
 
 
 def mix_blocks_kernel(mix, out_weight, out):
-    groups, heads, depth, _ = out.shape
+    heads, depth, _ = out.shape
     for m in range(heads):
         cols = slice(m * HEAD_DIM, (m + 1) * HEAD_DIM)
-        turned = out_weight[cols, :].astype(F32).T.astype(BF16)
-        for g in range(groups):
-            for j in range(4):
-                out[g, m, :, j * HEAD_DIM : (j + 1) * HEAD_DIM] = mix[j, :, cols]
-            out[g, m, :, 4 * HEAD_DIM :] = turned
-
-
-def up_blocks_kernel(up, out, turned):
+        for j in range(4):
+            out[m, :, j * HEAD_DIM : (j + 1) * HEAD_DIM] = mix[j, :, cols]
+        out[m, :, 4 * HEAD_DIM :] = out_weight[cols, :].astype(F32).T.astype(BF16)
+
+
+def feed_blocks_kernel(up, down, out, turned):
     _, _, units = up.shape
-    groups, heads, rows, _ = out.shape
-    rows = rows // 2
+    heads = out.shape[0]
+    rows = units // heads
     for j in range(2):
         for t in range(units // 128):
             block = up[j, :, t * 128 : (t + 1) * 128].astype(F32)
             turned[t * 128 : (t + 1) * 128, :] = block.T.astype(BF16)
-        for g in range(groups):
-            for m in range(heads):
-                out[g, m, j * rows : (j + 1) * rows, :] = turned[m * rows : (m + 1) * rows, :]
+        for m in range(heads):
+            out[m, j * rows : (j + 1) * rows, :] = turned[m * rows : (m + 1) * rows, :]
+    for m in range(heads):
+        out[m, 2 * rows :, :] = down[m * rows : (m + 1) * rows, :]
 
 
 def project_kernel(ids, *refs, members):
@@ -298,13 +297,13 @@
 
 def feed_kernel(*refs, members):
     own, other, cot_own, cot_other = (refs[i * members : (i + 1) * members] for i in range(4))
-    up, down, turned, inner_out, mine, away, weights = refs[4 * members :]
+    feed, turned, inner_out, mine, away, weights = refs[4 * members :]
     half, width = own[0].shape
-    units = down.shape[2]
+    units = feed.shape[2] // 3
     wide = turned.shape[0] // 3
     for j in range(3):
         weights[j * wide + units : (j + 1) * wide, :] = jnp.zeros((wide - units, width), BF16)
-        fill_columns(weights, *((up, 0), (up, units), (down, 0))[j], j * wide, units)
+        fill_columns(weights, feed, j * units, j * wide, units)
     for k in range(2):
         for b in range(0, members, STEP):
             x = rows_of((own, other)[k], b)
@@ -329,57 +328,57 @@
             )
 
 
-def block_kernel(ids, inner, down, mine, away, weights):
+def block_kernel(inner, feed, mine, away, weights):
     members, half, width = mine.shape
-    units, wide = down.shape[2], inner.shape[1]
+    units, wide = feed.shape[2] // 3, inner.shape[1]
     weights[units:, :] = jnp.zeros((wide - units, width), BF16)
-    fill_columns(weights, down, 0, 0, units)
+    fill_columns(weights, feed, 2 * units, 0, units)
     for k in range(2):
         for b in range(0, members, STEP):
             at = (k * members + b) * half
-            result = mul(inner[at : at + STEP * half, :], weights[...], 1, 0, None).astype(BF16)
-            for i in range(STEP):
-                (mine, away)[k][ids[0] ^ (b + i)] = result[i * half : (i + 1) * half]
-
-
-def store_shards(out, at, first, result):
-    depth = out.shape[3]
-    for i in range(result.shape[1] // depth):
-        part = result[:, i * depth : (i + 1) * depth].astype(BF16)
-        out[(at + i) // out.shape[1], (at + i) % out.shape[1], first : first + part.shape[0], :] = part
-
-
-def product_into(out, first, turned, spans, own, other, members):
+            result = mul(inner[at : at + STEP * half, :], weights[...], 1, 0, None)
+            (mine, away)[k][b : b + STEP] = result.astype(BF16).reshape(STEP, half, width)
+
+
+def product_into(ids, out, first, turned, spans, own, other, members, got=None):
     rows = turned.shape[1] // 2
-    width = out.shape[0] * out.shape[1] * out.shape[3]
+    shards, _, depth = out.shape
     low, high = spans[0][0], spans[-1][1]
-    for at in range(0, width, 256):
-        cols = slice(at, at + 256)
+    for at in range(0, shards * depth, 256):
+        cols = pl.ds(pl.multiple_of(ids[2] * (shards * depth) + at, 128), 256)
         result = mul(turned[low:high, :rows], rows_of(own, 0, members, cols), 1, 0, None)
         result += mul(turned[low:high, rows:], rows_of(other, 0, members, cols), 1, 0, None)
         to = first
         for start, stop in spans:
-            store_shards(out, at // out.shape[3], to, result[start - low : stop - low])
+            here = slice(to, to + stop - start)
+            for i in range(256 // depth):
+                part = result[start - low : stop - low, i * depth : (i + 1) * depth]
+                if got is not None:
+                    part = part + got[ids[3], at // depth + i, here, :].astype(F32)
+                out[at // depth + i, here, :] = part.astype(BF16)
             to += stop - start
 
 
-def feed_grad_kernel(*refs, members):
+def feed_grad_kernel(ids, *refs, members):
     own, other, cot_own, cot_other = (refs[i * members : (i + 1) * members] for i in range(4))
-    turned, out = refs[4 * members :]
-    units, wide = out.shape[2] // 3, turned.shape[0] // 3
-    product_into(out, 0, turned, [(0, units), (wide, wide + units)], own, other, members)
-    product_into(out, 2 * units, turned, [(2 * wide, 2 * wide + units)], cot_own, cot_other, members)
-
-
-def mix_grad_kernel(*refs, members):
+    turned, *got, out = refs[4 * members :]
+    got = got[0] if got else None
+    units, wide = out.shape[1] // 3, turned.shape[0] // 3
+    product_into(ids, out, 0, turned, [(0, units), (wide, wide + units)], own, other, members, got)
+    product_into(ids, out, 2 * units, turned, [(2 * wide, 2 * wide + units)], cot_own, cot_other, members, got)
+
+
+def mix_grad_kernel(ids, *refs, members):
     own, other, branch_own, branch_other = (refs[i * members : (i + 1) * members] for i in range(4))
-    turned, turned_gated, sums, out = refs[4 * members :]
-    groups, heads, rows, _ = out.shape
-    for g in range(groups):
-        for m in range(heads):
-            out[g, m, 5 * HEAD_DIM :, :] = sums[...]
-    product_into(out, 0, turned, [(0, 4 * HEAD_DIM)], own, other, members)
-    product_into(out, 4 * HEAD_DIM, turned_gated, [(0, HEAD_DIM)], branch_own, branch_other, members)
+    turned, turned_gated, sums, *got, out = refs[4 * members :]
+    got = got[0] if got else None
+    for m in range(out.shape[0]):
+        total = sums[...]
+        if got is not None:
+            total = total + got[ids[3], m, 5 * HEAD_DIM :, :].astype(F32)
+        out[m, 5 * HEAD_DIM :, :] = total.astype(BF16)
+    product_into(ids, out, 0, turned, [(0, 4 * HEAD_DIM)], own, other, members, got)
+    product_into(ids, out, 4 * HEAD_DIM, turned_gated, [(0, HEAD_DIM)], branch_own, branch_other, members, got)
 
 
 def project_back_kernel(ids, *refs, members):
@@ -404,14 +403,11 @@
             result = mul(x, weights[:, : 4 * HEAD_DIM], 1, 1, None)
             normed = rows_of((own, other)[k], b + 1 - STEP).astype(F32)
             grad_norm = grad_norm + jnp.sum(result * normed, axis=0, keepdims=True)
-            (mine_out, away_out)[k][b + 1 - STEP : b + 1] = result.astype(BF16).reshape(STEP, half, width)
+            for i in range(STEP):
+                to = ids[0] ^ (b + 1 - STEP + i)
+                (mine_out, away_out)[k][to] = result[i * half : (i + 1) * half].astype(BF16)
             parts = []
     norm_out[...] = jnp.broadcast_to(grad_norm / norm_gain[...], norm_out.shape)
-
-
-def add_kernel(ids, blocks, got, out):
-    for m in range(out.shape[0]):
-        out[m] = (blocks[ids[0], m].astype(F32) + got[ids[1], m].astype(F32)).astype(BF16)
 
 
 def mix_total_kernel(got, mix_out, out_out):
@@ -442,7 +438,7 @@
         down_out[i * units : (i + 1) * units, :] = got[i, 2 * units :, :].astype(F32)
 
 
-def call(kernel, outs, args, scratch=(), ids=None, behind=(), us=5):
+def call(kernel, outs, args, scratch=(), ids=None, behind=(), us=5, mib=20):
     specs = [pl.BlockSpec(memory_space=pltpu.VMEM)] * len(args)
     if ids is not None:
         specs = [pl.BlockSpec(memory_space=pltpu.SMEM)] + specs
@@ -458,7 +454,7 @@
         in_specs=specs + [pl.BlockSpec(memory_space=pl.ANY)] * len(behind),
         out_specs=[pl.BlockSpec(memory_space=pltpu.VMEM)] * len(outs),
         scratch_shapes=list(scratch),
-        compiler_params=pltpu.CompilerParams(vmem_limit_bytes=VMEM_LIMIT),
+        compiler_params=pltpu.CompilerParams(vmem_limit_bytes=mib * MIB),
         cost_estimate=pl.CostEstimate(flops=0, bytes_accessed=us * 3000000, transcendentals=0),
     )(*args, *behind)
 
@@ -528,19 +524,20 @@
     def all_groups(self, value):
         return lax.all_gather(value, "seq", axis_index_groups=self.columns)
 
-    def over_groups(self, blocks, behind):
-        if self.count == 2:
-            away = lax.dynamic_index_in_dim(blocks, 1 - self.index, 0, False)
-            (total,) = call(
-                add_kernel,
-                [(away.shape, BF16)],
-                (blocks, self.all_groups(away)),
-                (),
-                jnp.stack([self.index, 1 - self.index]).astype(jnp.int32),
-                behind,
-            )
-            return total
-        return lax.psum_scatter(blocks, "seq", axis_index_groups=self.columns)
+    def away(self, kernel, rows, depth, args, us):
+        count = 1 if self.count == 2 else self.count
+        ids = jnp.stack([self.member, self.core, (1 - self.index) * (count == 1), 0 * self.core]).astype(jnp.int32)
+        (out,) = call(kernel, [((count * self.size, rows, depth), BF16)], args, (), ids, us=us, mib=28)
+        if count == 1:
+            return self.all_groups(out)
+        out = out.reshape(count, self.size, rows, depth)
+        return lax.psum_scatter(out, "seq", axis_index_groups=self.columns)
+
+    def over_groups(self, kernel, args, got, behind, us):
+        if self.count != 2:
+            return got
+        ids = jnp.stack([self.member, self.core, self.index, 1 - self.index]).astype(jnp.int32)
+        return call(kernel, [(got.shape[1:], BF16)], (*args, got), (), ids, behind, us, 28)[0]
 
 
 def inverse_of(rows):
@@ -552,6 +549,16 @@
     dot_term = jnp.mean(scaled * rows, axis=-1, keepdims=True)
     grad_rows = inverse * scaled - rows * (inverse * inverse * inverse) * dot_term
     return grad_rows, jnp.sum(grad * rows * inverse, axis=0)
+
+
+def together(steps, *args):
+    shapes = jax.eval_shape(steps, *args)
+    always = lax.axis_index("seq") < 2 * lax.axis_size("seq")
+
+    def never(*_):
+        return jax.tree.map(lambda leaf: jnp.zeros(leaf.shape, leaf.dtype), shapes)
+
+    return lax.cond(always, steps, never, *args)
 
 
 def after(value, *earlier):
@@ -593,168 +600,191 @@
     gap = own_head(decay_gap).reshape(1, HEAD_DIM)
     gain = own_head(group_gain).reshape(1, HEAD_DIM)
 
+    everything = jnp.stack([member, core, 0 * core, 0 * core]).astype(jnp.int32)
+    square = ((HEAD_DIM, HEAD_DIM), F32)
+    all_rows = ((heads, half, width), BF16)
+
+    def many(n, dtype=F32):
+        return ((length, n * HEAD_DIM), dtype)
+
     token_rows = tokens.astype(F32)
     inverse1 = inverse_of(token_rows)
     half_tokens = my_half(token_rows)
     half_inverse1 = my_half(inverse1)
     cot_half = my_half(cotangent)
-    down_here = group.spread(down_weight.reshape(heads, units, depth))
-    normed1, normed1_other = group.gather((half_tokens * half_inverse1 * norm1_gain).astype(BF16))
-    cot, cot_other = group.gather(cot_half)
     (mix_blocks,) = call(
-        mix_blocks_kernel,
-        [((groups, heads, depth, 5 * HEAD_DIM), BF16)],
-        (mix_weight, out_weight),
-        (),
-        None,
-        (normed1[5], cot[5], down_here),
-    )
-    mix_own = lax.all_to_all(mix_blocks.reshape(peers, depth, 5 * HEAD_DIM), "seq", 0, 0, tiled=True)
-    mix_own = mix_own.reshape(width, 5 * HEAD_DIM)
-    (up_blocks,) = call(
-        up_blocks_kernel,
-        [((groups, heads, 2 * units, depth), BF16)],
-        (up_pair,),
-        [pltpu.VMEM((heads * units, depth), BF16)],
-        None,
-        (mix_blocks,),
-        3,
-    )
-    down_own = group.all_groups(down_here)
-    projected, tail = call(
-        functools.partial(project_kernel, members=heads),
-        [((length, 4 * HEAD_DIM), BF16), ((16, 3 * HEAD_DIM), BF16)],
-        (*normed1, *normed1_other, mix_own),
-        (),
-        ids,
-    )
-    halo = group.shift(tail, 1)
-
-    def many(n, dtype=F32):
-        return ((length, n * HEAD_DIM), dtype)
-
-    square = ((HEAD_DIM, HEAD_DIM), F32)
-    all_rows = ((heads, half, width), BF16)
-    conv, query, key, totals, states, mixed_here, last = call(
-        forward_kernel,
-        [
-            many(3),
-            many(1),
-            many(1),
-            ((count, HEAD_DIM), F32),
-            ((count, HEAD_DIM, HEAD_DIM), F32),
-            many(1),
-            ((HEAD_DIM + PAD, HEAD_DIM), F32),
-        ],
-        (projected, halo, taps, gap),
-        [pltpu.VMEM((length + 16, 3 * HEAD_DIM), F32)],
-        None,
-        cot_other,
-    )
-    own_decay = last[HEAD_DIM : HEAD_DIM + 1]
-    carry = group.carry(last[:HEAD_DIM], own_decay, 1)
-    up_own = lax.all_to_all(
-        after(up_blocks.reshape(peers, 2 * units, depth), carry), "seq", 0, 0, tiled=True
-    )
-    up_own = up_own.reshape(groups, heads, 2 * units, depth)
-    mixed, states, turned_gated, mine, away = call(
-        gate_kernel,
-        [many(1), ((count, HEAD_DIM, HEAD_DIM), F32), ((HEAD_DIM, length), BF16), all_rows, all_rows],
-        (mixed_here, query, totals, states, carry, projected, gain, mix_own),
-        [pltpu.VMEM((length, HEAD_DIM), BF16)],
-        ids,
-    )
-    hidden = half_tokens + group.scatter(mine, away, up_own)
-    inverse2 = inverse_of(hidden)
-    normed2, normed2_other = group.gather((hidden * inverse2 * norm2_gain).astype(BF16))
-
+        mix_blocks_kernel, [((heads, depth, 5 * HEAD_DIM), BF16)], (mix_weight, out_weight), us=2
+    )
+    mix_all = group.all_groups(mix_blocks)
+
+    def start_steps(rows, blocks, up, down):
+        own, other = group.gather(rows)
+        (feed_blocks,) = call(
+            feed_blocks_kernel,
+            [((heads, 3 * units, depth), BF16)],
+            (up, down),
+            [pltpu.VMEM((heads * units, depth), BF16)],
+            us=3,
+        )
+        here = group.spread(after(blocks, *other))
+        feed = group.spread(after(feed_blocks, here))
+        return own, other, feed, here
+
+    normed1, normed1_other, feed_here, mix_here = together(
+        start_steps,
+        after((half_tokens * half_inverse1 * norm1_gain).astype(BF16), mix_blocks),
+        mix_blocks,
+        up_pair,
+        down_weight,
+    )
+    feed_own = group.all_groups(feed_here)
+
+    def forward_steps(mix_all, mix_here, normed1, normed1_other):
+        if groups == 2:
+            far = group.spread(lax.dynamic_index_in_dim(mix_all, 1 - group.index, 0, False))
+            mix_own = jnp.where(group.index == 0, jnp.stack([mix_here, far]), jnp.stack([far, mix_here]))
+        else:
+            mix_own = jnp.moveaxis(group.spread(jnp.moveaxis(mix_all, 0, 1)), 0, 1)
+        mix_own = mix_own.reshape(width, 5 * HEAD_DIM)
+        projected, tail = call(
+            functools.partial(project_kernel, members=heads),
+            [((length, 4 * HEAD_DIM), BF16), ((16, 3 * HEAD_DIM), BF16)],
+            (*normed1, *normed1_other, mix_own),
+            (),
+            ids,
+        )
+        halo = group.shift(tail, 1)
+        conv, query, key, totals, states, mixed_here, last = call(
+            forward_kernel,
+            [
+                many(3),
+                many(1),
+                many(1),
+                ((count, HEAD_DIM), F32),
+                ((count, HEAD_DIM, HEAD_DIM), F32),
+                many(1),
+                ((HEAD_DIM + PAD, HEAD_DIM), F32),
+            ],
+            (projected, halo, taps, gap),
+            [pltpu.VMEM((length + 16, 3 * HEAD_DIM), F32)],
+        )
+        cot, cot_other = group.gather(after(cot_half, halo))
+        own_decay = last[HEAD_DIM : HEAD_DIM + 1]
+        carry = group.carry(last[:HEAD_DIM], own_decay, 1)
+        mixed, states, turned_gated, mine, away = call(
+            gate_kernel,
+            [many(1), ((count, HEAD_DIM, HEAD_DIM), F32), ((HEAD_DIM, length), BF16), all_rows, all_rows],
+            (mixed_here, query, totals, states, carry, projected, gain, mix_own),
+            [pltpu.VMEM((length, HEAD_DIM), BF16)],
+            ids,
+            tuple(cot),
+        )
+        hidden = half_tokens + group.scatter(mine, away)
+        inverse2 = inverse_of(hidden)
+        normed2, normed2_other = group.gather((hidden * inverse2 * norm2_gain).astype(BF16))
+        decays = jnp.exp(jnp.concatenate([totals[1:] - totals[:-1], jnp.log(own_decay) - totals[-1:]], axis=0))
+        kept = (mix_own, projected, halo, conv, query, key, states, mixed, own_decay, decays)
+        return kept, (normed2, normed2_other, cot, cot_other), (turned_gated, hidden, inverse2)
+
+    kept, feed_rows, (turned_gated, hidden, inverse2) = together(
+        forward_steps, mix_all, mix_here, normed1, normed1_other
+    )
+    feed_rows = tuple(block for blocks in feed_rows for block in blocks)
     turned, inner, mine, away = call(
         functools.partial(feed_kernel, members=heads),
         [((3 * wide, length), BF16), ((length, wide), BF16), all_rows, all_rows],
-        (*normed2, *normed2_other, *cot, *cot_other, up_own, down_own),
+        (*feed_rows, feed_own),
         [pltpu.VMEM((3 * wide, width), BF16)],
         us=17,
-    )
-    (grad_feed,) = call(
-        functools.partial(feed_grad_kernel, members=heads),
-        [((groups, heads, 3 * units, depth), BF16)],
-        (*normed2, *normed2_other, *cot, *cot_other, turned),
-        us=10,
-    )
-    grad_normed2 = group.scatter(mine, away, grad_feed)
-    grad_hidden_norm, grad_norm2 = norm_back(hidden, inverse2, norm2_gain, grad_normed2)
-    grad_hidden = cot_half.astype(F32) + grad_hidden_norm
-    branch, branch_other = group.gather(grad_hidden.astype(BF16))
-
-    decays = jnp.exp(jnp.concatenate([totals[1:] - totals[:-1], jnp.log(own_decay) - totals[-1:]], axis=0))
-    grad_mixed, grad_gate_rows, grad_group, start_grad = call(
-        functools.partial(gate_back_kernel, members=heads),
-        [many(1), many(1, BF16), ((PAD, HEAD_DIM), F32), square],
-        (*branch, *branch_other, mix_own, mixed, projected, gain, query, decays),
-        [pltpu.VMEM((length, HEAD_DIM), F32)],
-        ids,
-    )
-    back_carry = group.carry(start_grad, own_decay, -1)
-    grad_rows3, grad_tail, edge, small = call(
-        backward_kernel,
-        [many(3, BF16), ((16, 3 * HEAD_DIM), F32), ((PAD, 3 * HEAD_DIM), F32), ((16, HEAD_DIM), F32)],
-        (grad_mixed, conv, query, key, states, back_carry, halo, projected, taps, gap),
-        [
-            pltpu.VMEM((length + 16, 3 * HEAD_DIM), F32),
-            pltpu.VMEM((length + 2 * PAD, 3 * HEAD_DIM), F32),
-        ],
-    )
-    later = group.shift(edge, -1)
-    turned_mix, mine, away, grad_norm1 = call(
-        functools.partial(project_back_kernel, members=heads),
-        [((4 * HEAD_DIM, length), BF16), all_rows, all_rows, ((PAD, width), F32)],
-        (
-            *normed1,
-            *normed1_other,
-            grad_rows3,
-            grad_tail,
-            later,
-            grad_gate_rows,
-            mix_own,
-            norm1_gain.reshape(1, width),
-        ),
-        [pltpu.VMEM((length, 4 * HEAD_DIM), BF16)],
-        ids,
-    )
-    sums = jnp.concatenate([small[:13].reshape(-1), grad_group[0], grad_norm1[0], grad_norm2]).astype(BF16)
-    extra = -(-sums.shape[0] // (16 * depth)) * 16
-    sums = jnp.pad(sums, (0, extra * depth - sums.shape[0])).reshape(extra, depth)
-    (grad_mix,) = call(
-        functools.partial(mix_grad_kernel, members=heads),
-        [((groups, heads, 5 * HEAD_DIM + extra, depth), BF16)],
-        (*normed1, *normed1_other, *branch, *branch_other, turned_mix, turned_gated, sums),
-        us=7,
-    )
-    feed_total = group.over_groups(grad_feed, (grad_mix,))
-    grad_mix = after(grad_mix.reshape(peers, 5 * HEAD_DIM + extra, depth), feed_total)
-    mix_got = lax.all_to_all(grad_mix, "seq", 0, 0, tiled=True)
-    grad_normed1 = group.scatter(mine, after(away, grad_mix))
+        mib=38,
+    )
+    feed_grad = functools.partial(feed_grad_kernel, members=heads)
+    feed_args = (*feed_rows, turned)
+    feed_away = group.away(feed_grad, 3 * units, depth, feed_args, 5)
+
+    def backward_steps(mine, away, kept, hidden, inverse2, normed1, normed1_other, turned_gated):
+        mix_own, projected, halo, conv, query, key, states, mixed, own_decay, decays = kept
+        grad_normed2 = group.scatter(mine, away)
+        grad_hidden_norm, grad_norm2 = norm_back(hidden, inverse2, norm2_gain, grad_normed2)
+        grad_hidden = cot_half.astype(F32) + grad_hidden_norm
+        branch, branch_other = group.gather(grad_hidden.astype(BF16))
+        grad_mixed, grad_gate_rows, grad_group, start_grad = call(
+            functools.partial(gate_back_kernel, members=heads),
+            [many(1), many(1, BF16), ((PAD, HEAD_DIM), F32), square],
+            (*branch, *branch_other, mix_own, mixed, projected, gain, query, decays),
+            [pltpu.VMEM((length, HEAD_DIM), F32)],
+            ids,
+        )
+        back_carry = group.carry(start_grad, own_decay, -1)
+        grad_rows3, grad_tail, edge, small = call(
+            backward_kernel,
+            [many(3, BF16), ((16, 3 * HEAD_DIM), F32), ((PAD, 3 * HEAD_DIM), F32), ((16, HEAD_DIM), F32)],
+            (grad_mixed, conv, query, key, states, back_carry, halo, projected, taps, gap),
+            [
+                pltpu.VMEM((length + 16, 3 * HEAD_DIM), F32),
+                pltpu.VMEM((length + 2 * PAD, 3 * HEAD_DIM), F32),
+            ],
+            us=8,
+        )
+        later = group.shift(edge, -1)
+        turned_mix, mine, away, grad_norm1 = call(
+            functools.partial(project_back_kernel, members=heads),
+            [((4 * HEAD_DIM, length), BF16), all_rows, all_rows, ((PAD, width), F32)],
+            (
+                *normed1,
+                *normed1_other,
+                grad_rows3,
+                grad_tail,
+                later,
+                grad_gate_rows,
+                mix_own,
+                norm1_gain.reshape(1, width),
+            ),
+            [pltpu.VMEM((length, 4 * HEAD_DIM), BF16)],
+            ids,
+            us=7,
+            mib=28,
+        )
+        sums = jnp.concatenate([small[:13].reshape(-1), grad_group[0], grad_norm1[0], grad_norm2]).astype(BF16)
+        sums = jnp.pad(sums, (0, extra * depth - sums.shape[0])).reshape(extra, depth)
+        (grad_mix,) = call(
+            functools.partial(mix_grad_kernel, members=heads),
+            [((peers, 5 * HEAD_DIM + extra, depth), BF16)],
+            (*normed1, *normed1_other, *branch, *branch_other, turned_mix, turned_gated, sums),
+            (),
+            everything,
+            us=7,
+            mib=28,
+        )
+        both = (mine.astype(F32) + group.other_core(away).astype(F32)).astype(BF16)
+        return grad_hidden, grad_mix, both
+
+    extra = -(-(14 * HEAD_DIM + 2 * width) // (16 * depth)) * 16
+    grad_hidden, grad_mix, both = together(
+        backward_steps, mine, away, kept, hidden, inverse2, normed1, normed1_other, turned_gated
+    )
+    grad_normed1 = lax.psum_scatter(both, "seq", axis_index_groups=group.lists).astype(F32)
+    mix_got = lax.all_to_all(after(grad_mix, feed_away), "seq", 0, 0, tiled=True)
+    (block_mine, block_away) = call(
+        block_kernel, [all_rows, all_rows], (inner, feed_own), [pltpu.VMEM((wide, width), BF16)], None, (grad_mix,)
+    )
+    block_half = hidden + group.scatter(block_mine, block_away)
+    feed_total = group.over_groups(feed_grad, feed_args, feed_away, (grad_mix,), 8)
     feed_got = group.spread(after(feed_total, mix_got))
     mix_total, out_total = call(
         mix_total_kernel,
         [((4, depth, heads * HEAD_DIM), F32), ((heads * HEAD_DIM, depth), F32)],
         (mix_got.reshape(groups, heads, 5 * HEAD_DIM + extra, depth),),
+        us=4,
     )
     grad_rows1 = norm_back(half_tokens, half_inverse1, norm1_gain, grad_normed1)[0]
     grad_tokens = grad_hidden + grad_rows1
-
     up_total, down_total = call(
         feed_total_kernel,
         [((2, depth, heads * units), F32), ((heads * units, depth), F32)],
         (feed_got,),
         [pltpu.VMEM((heads * units, depth), F32)],
     )
-    (block_mine, block_away) = call(
-        block_kernel, [all_rows, all_rows], (inner, down_own), [pltpu.VMEM((wide, width), BF16)], ids, (grad_mix,)
-    )
-    block = (block_mine.astype(F32) + group.other_core(block_away).astype(F32)).astype(BF16)
-    block_half = hidden + lax.psum_scatter(block, "seq", axis_index_groups=group.lists).astype(F32)
-
     def both_halves(rows):
         other = group.other_core(rows)
         return jnp.where(core == 0, jnp.concatenate([rows, other], 0), jnp.concatenate([other, rows], 0))

time: 609 us -> 585 us (0.961)
  local copies, waits for them, and re-layouts: 54.4 us -> 24.2 us
  starting transfers between devices: 106 us -> 119 us
    all_to_all x2 -> x4, waiting for transfers between devices: 0.01 us -> 95.4 us  [spread(): lax.all_to_all(blocks, 'seq', 0, 0, axis_index_groups=self.lists, tiled=T...]
    ppermute x49, waiting for transfers between devices: 236 us -> 160 us  [swap(): lax.ppermute(value, 'seq', [(s, s ^ bits) for s in range(self.peers)])]
    unnamed x200 -> x44, local copies, waits for them, and re-layouts: 44.3 us -> 16.4 us
    ppermute x49, starting transfers between devices: 48.2 us -> 72.1 us  [swap(): lax.ppermute(value, 'seq', [(s, s ^ bits) for s in range(self.peers)])]
    all_to_all x3 -> x1, waiting for transfers between devices: 23.6 us -> 0.01 us  [shards(): lax.all_to_all(after(grad_mix, feed_away), 'seq', 0, 0, tiled=True)]
    all_to_all x3 -> x1, starting transfers between devices: 19.2 us -> 6.99 us  [shards(): lax.all_to_all(after(grad_mix, feed_away), 'seq', 0, 0, tiled=True)]
    all_to_all x2 -> x4, starting transfers between devices: 10.4 us -> 22.4 us  [spread(): lax.all_to_all(blocks, 'seq', 0, 0, axis_index_groups=self.lists, tiled=T...]
    all_gather x2 -> x3, starting transfers between devices: 11.2 us -> 0.12 us  [all_groups(): return lax.all_gather(value, 'seq', axis_index_groups=self.columns)]
  transfers between devices with their start and end apart: 101 -> 102, of which waited for: 45 -> 52; matrix products, arithmetic and copies ran while one was open for 8% -> 7% of each run, Pallas kernels for 9% -> 10%
where the time goes in v3:
time: 585 us; the launch traced here: 574 us
  waiting for transfers between devices  296 us (51%)
  starting transfers between devices  119 us (20%)
  Pallas kernels  85.6 us (15%)
  other arithmetic  34.7 us (6%)
  local copies, waits for them, and re-layouts  24.2 us (4%)
  between operations  14.2 us (2%)
    ppermute x49, waiting for transfers between devices, swap(): lax.ppermute(value, 'seq', [(s, s ^ bits) for s in range(self.peers)])  160 us
    all_to_all x4, waiting for transfers between devices, spread(): lax.all_to_all(blocks, 'seq', 0, 0, axis_index_groups=self.lists, tiled=T...  95.4 us
    pallas_call x15, Pallas kernels, call(): pl.pallas_call(body, out_shape=[jax.ShapeDtypeStruct(s, d) for s, d in ou...  85.6 us
    ppermute x49, starting transfers between devices, swap(): lax.ppermute(value, 'seq', [(s, s ^ bits) for s in range(self.peers)])  72.1 us
    all_to_all x4, starting transfers between devices, spread(): lax.all_to_all(blocks, 'seq', 0, 0, axis_index_groups=self.lists, tiled=T...  22.4 us
    ppermute x40, waiting for transfers between devices, other_core(): return lax.ppermute(value, 'head', [(0, 1), (1, 0)])  18.9 us
    ppermute x4, waiting for transfers between devices, shift(): return lax.ppermute(value, 'seq', pairs)  16.8 us
    unnamed x44, local copies, waits for them, and re-layouts  16.4 us
  transfers between devices with their start and end apart: 102, of which 52 were waited for; matrix products, arithmetic and copies ran while one was open for 7% of the time, Pallas kernels for 10%

profile of v3, /device:TPU:18, one launch (start us, length us, event | category | flops | bytes accessed | tf_op | source)
XLA Modules:
  0.0 573.6 jit_solution(6602242030309981637)
XLA Ops:
  12.3 105.7 %conditional.3 = (bf16[64,2048]{1,0:T(8,128)(2,1)S(1)}, bf16[64,2048]{1,0:T(8,128)(2,1)}, bf16[64,2048]{1,0:T(8,128)(2,1)}, bf16[64,2048]{1,0:T(8,128)(2,1)}, bf...) conditional(s32[]{:T(128)} %convert_element_type.398, () %tuple.39, ...), branch_computations={%region_1.0_spmd, %region_2.0_spmd} | conditional | bytes 48257208 | solution.py:561
  46.6 38.7 %all-to-all-done = bf16[8,128,640]{2,1,0:T(8,128)(2,1)} async-done(((bf16[8,128,640]{2,1,0:T(8,128)(2,1)}), bf16[8,128,640]{2,1,0:T(8,128)(2,1)}, u32[]{:S(2)}, u32[]{:S(2)}) %all-to-all-start) | async-done | bytes 1310752 | tf_op jit(solution)/shard_map/cond/branch_1_fun/all_to_all | solution.py:522
  85.2 6.2 %all-to-all-start.1 = ((bf16[8,1056,128]{2,1,0:T(8,128)(2,1)}), bf16[8,1056,128]{2,1,0:T(8,128)(2,1)}, u32[]{:S(2)}, u32[]{:S(2)}) async-start(bf16[8,1056,128]{2,1,0:T(8,128)(2,1)} %branch_1_fun.8), calls=%async_computation.1 | async-start | bytes 4325376 | tf_op jit(solution)/shard_map/cond/branch_1_fun/all_to_all | solution.py:522
  91.5 26.5 %all-to-all-done.1 = bf16[8,1056,128]{2,1,0:T(8,128)(2,1)} async-done(((bf16[8,1056,128]{2,1,0:T(8,128)(2,1)}), bf16[8,1056,128]{2,1,0:T(8,128)(2,1)}, u32[]{:S(2)}, u32[]{:S(2)}) %all-to-all-start.1) | async-done | bytes 2162720 | tf_op jit(solution)/shard_map/cond/branch_1_fun/all_to_all | solution.py:522
  120.5 157.7 %conditional.4 = (bf16[2048,640]{1,0:T(8,128)(2,1)S(1)}, bf16[1024,512]{1,0:T(8,128)(2,1)}, bf16[16,384]{1,0:T(8,128)(2,1)S(1)}, f32[1024,384]{1,0:T(8,128)}, f3...) conditional(s32[]{:T(128)} %convert_element_type.398, () %tuple.38, ...), branch_computations={%region_3.0_spmd, %region_4.6_spmd} | conditional | flops 10618949 | bytes 152527808 | solution.py:561
  127.5 30.2 %all-to-all-done.2 = bf16[8,128,640]{2,1,0:T(8,128)(2,1)} async-done(((bf16[8,128,640]{2,1,0:T(8,128)(2,1)}), bf16[8,128,640]{2,1,0:T(8,128)(2,1)}, u32[]{:S(2)}, u32[]{:S(2)}) %all-to-all-start.2) | async-done | bytes 1310752 | tf_op jit(solution)/shard_map/cond/branch_1_fun/all_to_all | solution.py:522
  175.1 12.3 %collective-permute-done.20.refs_13_ = bf16[64,2048]{1,0:T(8,128)(2,1)} collective-permute-done((bf16[64,2048]{1,0:T(8,128)(2,1)S(1)}, bf16[64,2048]{1,0:T(8,128)(2,1)}, u32[]{:S(2)}, u32[]{:S(2)}) %collective-permute-start.20) | collective-permute-done | bytes 262176 | tf_op jit(solution)/shard_map/cond/branch_1_fun/ppermute | solution.py:475
  198.4 7.2 %branch_1_fun.10 = (f32[1024,384]{1,0:T(8,128)}, f32[1024,128]{1,0:T(8,128)S(1)}, f32[1024,128]{1,0:T(8,128)}, f32[8,128]{1,0:T(8,128)S(1)}, f32[8,128,128]{2,1,...) custom-call(bf16[1024,512]{1,0:T(8,128)(2,1)} %get-tuple-element.526.refs_0_.refs_6_, ...), custom_call_target="tpu_custom_call" | custom-call | bytes 15000000 | tf_op jit(solution)/shard_map/cond/branch_1_fun/pallas_call | solution.py:451
  254.1 6.0 %collective-permute-done.35 = bf16[64,2048]{1,0:T(8,128)(2,1)} collective-permute-done((bf16[64,2048]{1,0:T(8,128)(2,1)}, bf16[64,2048]{1,0:T(8,128)(2,1)}, u32[]{:S(2)}, u32[]{:S(2)}) %collective-permute-start.35) | collective-permute-done | bytes 262176 | tf_op jit(solution)/shard_map/cond/branch_1_fun/ppermute | solution.py:475
  263.2 6.4 %collective-permute-done.36 = bf16[64,2048]{1,0:T(8,128)(2,1)} collective-permute-done((bf16[64,2048]{1,0:T(8,128)(2,1)}, bf16[64,2048]{1,0:T(8,128)(2,1)}, u32[]{:S(2)}, u32[]{:S(2)}) %collective-permute-start.36) | collective-permute-done | bytes 262176 | tf_op jit(solution)/shard_map/cond/branch_1_fun/ppermute | solution.py:475
  280.6 16.2 %shard_map.205 = (bf16[1152,1024]{1,0:T(8,128)(2,1)S(1)}, bf16[1024,384]{1,0:T(8,128)(2,1)S(1)}, bf16[8,64,2048]{2,1,0:T(8,128)(2,1)}, bf16[8,64,2048]{2,1,0:T(8,128)(2,1)}) custom-call(bf16[64,2048]{1,0:T(8,128)(2,1)} %get-tuple-element.342.refs_0_.refs_1_, bf16[64,2048]{1,0:T(8,128)(2,1)} %get-tuple-element.343.refs_1_.refs_2_, ...), custom_call_target="tpu_custom_call" | custom-call | bytes 51000000 | tf_op jit(solution)/shard_map/pallas_call | solution.py:451
  297.7 7.2 %shard_map.207 = bf16[8,1056,128]{2,1,0:T(8,128)(2,1)} custom-call(s32[4]{0:T(128)S(1)} %pad_add_fusion.3.refs_0_, bf16[64,2048]{1,0:T(8,128)(2,1)} %get-tuple-element.342.refs_0_.refs_1_, bf16[64,2048]{1,0:T(8,128)(2,1)} %get-tuple-element.343.refs_1_.refs_2_, bf16[64,2048]{1,0:T(8,128)(2,1)} %get-tuple-element.344.refs_2_.refs_3_, ...), custom_call_target="tpu_custom_call" | custom-call | bytes 15000000 | tf_op jit(solution)/shard_map/pallas_call | solution.py:451
  307.4 110.1 %conditional.5 = (f32[64,2048]{1,0:T(8,128)}, bf16[16,688,128]{2,1,0:T(8,128)(2,1)}, bf16[8,64,2048]{2,1,0:T(8,128)(2,1)}) conditional(s32[]{:T(128)} %convert_element_type.398, () %tuple.43, (bf16[64,2048]{1,0:T(8,128)(2,1)S(1)}, f32[64,1]{0,1:T(1,128)S(1)}, bf16[8,64,2048]{2,1,0:T(8,128)(2,1)}, bf16[8,64,2048]{2,1,0:T(8,128)(2,1)}, ...), branch_computations={%region_6.7_spmd, %region_7.10_spmd} | conditional | flops 12006528 | bytes 159499968 | solution.py:561
  336.3 10.0 %collective-permute-done.62 = bf16[64,2048]{1,0:T(8,128)(2,1)S(1)} collective-permute-done((bf16[64,2048]{1,0:T(8,128)(2,1)S(1)}, bf16[64,2048]{1,0:T(8,128)(2,1)S(1)}, u32[]{:S(2)}, u32[]{:S(2)}) %collective-permute-start.62) | collective-permute-done | bytes 262176 | tf_op jit(solution)/shard_map/cond/branch_1_fun/ppermute | solution.py:475
  351.0 11.2 %collective-permute-done.66.refs_5_.refs_21_ = bf16[64,2048]{1,0:T(8,128)(2,1)S(1)} collective-permute-done((bf16[64,2048]{1,0:T(8,128)(2,1)S(1)}, bf16[64,2048]{1,0:T(8,128)(2,1)S(1)}, u32[]{:S(2)}, u32[]{:S(2)}) %collective-permute-start.66) | collective-permute-done | bytes 262176 | tf_op jit(solution)/shard_map/cond/branch_1_fun/ppermute | solution.py:475
  387.6 10.4 %branch_1_fun.13 = (bf16[1024,384]{1,0:T(8,128)(2,1)S(1)}, f32[16,384]{1,0:T(8,128)S(1)}, f32[8,384]{1,0:T(8,128)S(1)}, f32[16,128]{1,0:T(8,128)S(1)}) custom-call(f32[1024,128]{1,0:T(8,128)S(1)} %get-tuple-element.213.refs_0_, f32[1024,384]{1,0:T(8,128)} %get-tuple-element.214.refs_1_, f32[1024,128]{1,0:T(8,128)S(1)} %copy-done.16, ...), custom_call_target="tpu_custom_call" | custom-call | bytes 24000000 | tf_op jit(solution)/shard_map/cond/branch_1_fun/pallas_call | solution.py:451
  409.4 5.9 %branch_1_fun.15 = bf16[16,688,128]{2,1,0:T(8,128)(2,1)} custom-call(s32[4]{0:T(128)S(1)} %get-tuple-element.189.refs_0_, bf16[64,2048]{1,0:T(8,128)(2,1)S(1)} %get-tuple-element.190.refs_1_, bf16[64,2048]{1,0:T(8,128)(2,1)S(1)} %copy-done.26, bf16[64,2048]{1,0:T(8,128)(2,1)S(1)} %copy-done.29, bf16[64,2048]{1,0:T(8,128)(2,1)S(1)} %copy-done.32, ...), custom_call_target="tpu_custom_call" | custom-call | bytes 21000000 | tf_op jit(solution)/shard_map/cond/branch_1_fun/pallas_call | solution.py:451
  417.5 7.0 %all-to-all-start.3 = ((bf16[16,688,128]{2,1,0:T(8,128)(2,1)}), bf16[16,688,128]{2,1,0:T(8,128)(2,1)S(1)}, u32[]{:S(2)}, u32[]{:S(2)}) async-start(bf16[16,688,128]{2,1,0:T(8,128)(2,1)} %get-tuple-element.395.refs_2_.refs_35_), calls=%async_computation.4 | async-start | bytes 5636096 | tf_op jit(solution)/shard_map/all_to_all | solution.py:767
  442.8 12.2 %collective-permute-done.83 = bf16[64,2048]{1,0:T(8,128)(2,1)S(1)} collective-permute-done((bf16[64,2048]{1,0:T(8,128)(2,1)S(1)}, bf16[64,2048]{1,0:T(8,128)(2,1)S(1)}, u32[]{:S(2)}, u32[]{:S(2)}) %collective-permute-start.83) | collective-permute-done | bytes 262176 | tf_op jit(solution)/shard_map/ppermute | solution.py:475
  464.5 27.2 %collective-permute-start.84 = (bf16[64,2048]{1,0:T(8,128)(2,1)}, bf16[64,2048]{1,0:T(8,128)(2,1)}, u32[]{:S(2)}, u32[]{:S(2)}) collective-permute-start(bf16[64,2048]{1,0:T(8,128)(2,1)} %get-tuple-element.435), channel_id=1, source_target_pairs={{0,4},{2,6},{4,0},{6,2},{8,12},{10,14},{12,8},{14,10},{16,20},{18,... | collective-permute-start | bytes 786440 | tf_op jit(solution)/shard_map/ppermute | solution.py:475
  494.0 5.8 %shard_map.209 = bf16[8,1056,128]{2,1,0:T(8,128)(2,1)S(1)} custom-call(s32[4]{0:T(128)S(1)} %pad_add_fusion.4.refs_0_, bf16[64,2048]{1,0:T(8,128)(2,1)} %get-tuple-element.342.refs_0_.refs_1_, bf16[64,2048]{1,0:T(8,128)(2,1)} %get-tuple-element.343.refs_1_.refs_2_, bf16[64,2048]{1,0:T(8,128)(2,1)} %get-tuple-element.344.refs_2_.refs_3_, ...), custom_call_target="tpu_custom_call" | custom-call | bytes 24000000 | tf_op jit(solution)/shard_map/pallas_call | solution.py:451
  501.3 6.5 %all-to-all-start.4 = ((bf16[8,1056,128]{2,1,0:T(8,128)(2,1)}), bf16[8,1056,128]{2,1,0:T(8,128)(2,1)}, u32[]{:S(2)}, u32[]{:S(2)}) async-start(bf16[8,1056,128]{2,1,0:T(8,128)(2,1)} %copy-done.6), calls=%async_computation.5 | async-start | bytes 4325376 | tf_op jit(solution)/shard_map/all_to_all | solution.py:522
  510.7 17.4 %collective-permute-done.82 = bf16[64,2048]{1,0:T(8,128)(2,1)} collective-permute-done((bf16[64,2048]{1,0:T(8,128)(2,1)}, bf16[64,2048]{1,0:T(8,128)(2,1)}, u32[]{:S(2)}, u32[]{:S(2)}) %collective-permute-start.82) | collective-permute-done | bytes 262176 | tf_op jit(solution)/shard_map/ppermute | solution.py:475
  528.1 10.8 %collective-permute-done.88 = bf16[64,2048]{1,0:T(8,128)(2,1)S(1)} collective-permute-done((bf16[64,2048]{1,0:T(8,128)(2,1)S(1)}, bf16[64,2048]{1,0:T(8,128)(2,1)S(1)}, u32[]{:S(2)}, u32[]{:S(2)}) %collective-permute-start.88) | collective-permute-done | bytes 262176 | tf_op jit(solution)/shard_map/ppermute | solution.py:475
  (393 shorter events, 277.3 us)
Async XLA Ops:
  7.2 113.3 %all-gather.7.cloned.1.call-start = ((), (), s32[]{:S(2)}) async-start(), calls=%async_computation.7 | async-start | bytes 3932160 | tf_op jit(solution)/shard_map/all_gather | solution.py:525
  10.8 267.4 %all-gather.9.cloned.1.call-start = ((), (), s32[]{:S(2)}) async-start(), calls=%async_computation.8 | async-start | bytes 6488064 | tf_op jit(solution)/shard_map/all_gather | solution.py:525
  37.7 47.6 %all-to-all-start = ((bf16[8,128,640]{2,1,0:T(8,128)(2,1)}), bf16[8,128,640]{2,1,0:T(8,128)(2,1)}, u32[]{:S(2)}, u32[]{:S(2)}) async-start(bf16[8,128,640]{2,1,0:T(8,128)(2,1)} %get-tuple-element.140), calls=%async_computation | async-start | bytes 2621440 | tf_op jit(solution)/shard_map/cond/branch_1_fun/all_to_all | solution.py:522
  85.2 32.8 %all-to-all-start.1 = ((bf16[8,1056,128]{2,1,0:T(8,128)(2,1)}), bf16[8,1056,128]{2,1,0:T(8,128)(2,1)}, u32[]{:S(2)}, u32[]{:S(2)}) async-start(bf16[8,1056,128]{2,1,0:T(8,128)(2,1)} %branch_1_fun.8), calls=%async_computation.1 | async-start | bytes 4325376 | tf_op jit(solution)/shard_map/cond/branch_1_fun/all_to_all | solution.py:522
  118.1 299.4 %all-gather.11.cloned.1.call-start = ((), (), s32[]{:S(2)}) async-start(), calls=%async_computation.9 | async-start | bytes 6488064 | tf_op jit(solution)/shard_map/all_gather | solution.py:525
  123.0 34.6 %all-to-all-start.2 = ((bf16[8,128,640]{2,1,0:T(8,128)(2,1)}), bf16[8,128,640]{2,1,0:T(8,128)(2,1)}, u32[]{:S(2)}, u32[]{:S(2)}) async-start(bf16[8,128,640]{2,1,0:T(8,128)(2,1)} %dynamic-slice_bitcast_fusion), calls=%async_computation.2 | async-start | bytes 2621440 | tf_op jit(solution)/shard_map/cond/branch_1_fun/all_to_all | solution.py:522
  173.7 17.2 %collective-permute-start.18 = (bf16[64,2048]{1,0:T(8,128)(2,1)S(1)}, bf16[64,2048]{1,0:T(8,128)(2,1)}, u32[]{:S(2)}, u32[]{:S(2)}) collective-permute-start(bf16[64,2048]{1,0:T(8,128)(2,1)S(1)} %copy-done.55), channel_id=1, source_target_pairs={{0,4},{2,6},{4,0},{6,2},{8,12},{10,14},{12,8},{14,10},{16,20},{18,... | collective-permute-start | bytes 786440 | tf_op jit(solution)/shard_map/cond/branch_1_fun/ppermute | solution.py:475
  187.9 24.8 %collective-permute-start.17 = (bf16[64,2048]{1,0:T(8,128)(2,1)S(1)}, bf16[64,2048]{1,0:T(8,128)(2,1)}, u32[]{:S(2)}, u32[]{:S(2)}) collective-permute-start(bf16[64,2048]{1,0:T(8,128)(2,1)S(1)} %copy-done.55), channel_id=1, source_target_pairs={{0,2},{2,0},{4,6},{6,4},{8,10},{10,8},{12,14},{14,12},{16,18},{18,... | collective-permute-start | bytes 786440 | tf_op jit(solution)/shard_map/cond/branch_1_fun/ppermute | solution.py:475
  189.4 23.4 %collective-permute-start.22 = (bf16[64,2048]{1,0:T(8,128)(2,1)}, bf16[64,2048]{1,0:T(8,128)(2,1)}, u32[]{:S(2)}, u32[]{:S(2)}) collective-permute-start(bf16[64,2048]{1,0:T(8,128)(2,1)} %collective-permute-done.20.refs_13_), channel_id=1, source_target_pairs={{0,4},{2,6},{4,0},{6,2},{8,12},{10,14},{12,8},{14,10},{16,20},{18,... | collective-permute-start | bytes 786440 | tf_op jit(solution)/shard_map/cond/branch_1_fun/ppermute | solution.py:475
  190.9 21.9 %collective-permute-start.19 = (bf16[64,2048]{1,0:T(8,128)(2,1)}, bf16[64,2048]{1,0:T(8,128)(2,1)}, u32[]{:S(2)}, u32[]{:S(2)}) collective-permute-start(bf16[64,2048]{1,0:T(8,128)(2,1)} %collective-permute-done.18.refs_11_), channel_id=1, source_target_pairs={{0,2},{2,0},{4,6},{6,4},{8,10},{10,8},{12,14},{14,12},{16,18},{18,... | collective-permute-start | bytes 786440 | tf_op jit(solution)/shard_map/cond/branch_1_fun/ppermute | solution.py:475
  196.9 15.8 %collective-permute-start.23 = (bf16[64,2048]{1,0:T(8,128)(2,1)}, bf16[64,2048]{1,0:T(8,128)(2,1)}, u32[]{:S(2)}, u32[]{:S(2)}) collective-permute-start(bf16[64,2048]{1,0:T(8,128)(2,1)} %collective-permute-done.21.refs_14_), channel_id=1, source_target_pairs={{0,4},{2,6},{4,0},{6,2},{8,12},{10,14},{12,8},{14,10},{16,20},{18,... | collective-permute-start | bytes 786440 | tf_op jit(solution)/shard_map/cond/branch_1_fun/ppermute | solution.py:475
  223.0 14.2 %collective-permute-start.28 = (bf16[64,2048]{1,0:T(8,128)(2,1)S(1)}, bf16[64,2048]{1,0:T(8,128)(2,1)S(1)}, u32[]{:S(2)}, u32[]{:S(2)}) collective-permute-start(bf16[64,2048]{1,0:T(8,128)(2,1)S(1)} %get-tuple-element.419), channel_id=1, source_target_pairs={{0,4},{2,6},{4,0},{6,2},{8,12},{10,14},{12,8},{14,10},{16,20},{18,... | collective-permute-start | bytes 786440 | tf_op jit(solution)/shard_map/cond/branch_1_fun/ppermute | solution.py:475
  315.5 14.2 %collective-permute-start.59 = (bf16[64,2048]{1,0:T(8,128)(2,1)S(1)}, bf16[64,2048]{1,0:T(8,128)(2,1)S(1)}, u32[]{:S(2)}, u32[]{:S(2)}) collective-permute-start(bf16[64,2048]{1,0:T(8,128)(2,1)S(1)} %get-tuple-element.427), channel_id=1, source_target_pairs={{0,4},{2,6},{4,0},{6,2},{8,12},{10,14},{12,8},{14,10},{16,20},{18,... | collective-permute-start | bytes 786440 | tf_op jit(solution)/shard_map/cond/branch_1_fun/ppermute | solution.py:475
  350.4 14.4 %collective-permute-start.63 = (bf16[64,2048]{1,0:T(8,128)(2,1)S(1)}, bf16[64,2048]{1,0:T(8,128)(2,1)S(1)}, u32[]{:S(2)}, u32[]{:S(2)}) collective-permute-start(bf16[64,2048]{1,0:T(8,128)(2,1)S(1)} %get-tuple-element.410.refs_1_.refs_17_), channel_id=1, source_target_pairs={{0,2},{2,0},{4,6},{6,4},{8,10},{10,8},{12,14},{14,12},{16,18},{18,... | collective-permute-start | bytes 786440 | tf_op jit(solution)/shard_map/cond/branch_1_fun/ppermute | solution.py:475
  417.5 83.8 %all-to-all-start.3 = ((bf16[16,688,128]{2,1,0:T(8,128)(2,1)}), bf16[16,688,128]{2,1,0:T(8,128)(2,1)S(1)}, u32[]{:S(2)}, u32[]{:S(2)}) async-start(bf16[16,688,128]{2,1,0:T(8,128)(2,1)} %get-tuple-element.395.refs_2_.refs_35_), calls=%async_computation.4 | async-start | bytes 5636096 | tf_op jit(solution)/shard_map/all_to_all | solution.py:767
  424.5 121.5 %reduce-scatter.2.cloned.1.call-start = ((), (), s32[]{:S(2)}) async-start(), calls=%async_computation.6 | async-start | bytes 2359296 | tf_op jit(solution)/shard_map/reduce_scatter | solution.py:766
  440.2 14.8 %collective-permute-start.83 = (bf16[64,2048]{1,0:T(8,128)(2,1)S(1)}, bf16[64,2048]{1,0:T(8,128)(2,1)S(1)}, u32[]{:S(2)}, u32[]{:S(2)}) collective-permute-start(bf16[64,2048]{1,0:T(8,128)(2,1)S(1)} %get-tuple-element.434), channel_id=1, source_target_pairs={{0,2},{2,0},{4,6},{6,4},{8,10},{10,8},{12,14},{14,12},{16,18},{18,... | collective-permute-start | bytes 786440 | tf_op jit(solution)/shard_map/ppermute | solution.py:475
  440.8 19.4 %collective-permute-start.86 = (bf16[64,2048]{1,0:T(8,128)(2,1)S(1)}, bf16[64,2048]{1,0:T(8,128)(2,1)S(1)}, u32[]{:S(2)}, u32[]{:S(2)}) collective-permute-start(bf16[64,2048]{1,0:T(8,128)(2,1)S(1)} %get-tuple-element.432), channel_id=1, source_target_pairs={{0,4},{2,6},{4,0},{6,2},{8,12},{10,14},{12,8},{14,10},{16,20},{18,... | collective-permute-start | bytes 786440 | tf_op jit(solution)/shard_map/ppermute | solution.py:475
  442.3 65.5 %collective-permute-start.85 = (bf16[64,2048]{1,0:T(8,128)(2,1)}, bf16[64,2048]{1,0:T(8,128)(2,1)}, u32[]{:S(2)}, u32[]{:S(2)}) collective-permute-start(bf16[64,2048]{1,0:T(8,128)(2,1)} %get-tuple-element.433), channel_id=1, source_target_pairs={{0,4},{2,6},{4,0},{6,2},{8,12},{10,14},{12,8},{14,10},{16,20},{18,... | collective-permute-start | bytes 786440 | tf_op jit(solution)/shard_map/ppermute | solution.py:475
  462.4 45.3 %collective-permute-start.87 = (bf16[64,2048]{1,0:T(8,128)(2,1)}, bf16[64,2048]{1,0:T(8,128)(2,1)}, u32[]{:S(2)}, u32[]{:S(2)}) collective-permute-start(bf16[64,2048]{1,0:T(8,128)(2,1)} %get-tuple-element.436), channel_id=1, source_target_pairs={{0,2},{2,0},{4,6},{6,4},{8,10},{10,8},{12,14},{14,12},{16,18},{18,... | collective-permute-start | bytes 786440 | tf_op jit(solution)/shard_map/ppermute | solution.py:475
  462.5 65.6 %collective-permute-start.82 = (bf16[64,2048]{1,0:T(8,128)(2,1)}, bf16[64,2048]{1,0:T(8,128)(2,1)}, u32[]{:S(2)}, u32[]{:S(2)}) collective-permute-start(bf16[64,2048]{1,0:T(8,128)(2,1)} %get-tuple-element.431), channel_id=1, source_target_pairs={{0,2},{2,0},{4,6},{6,4},{8,10},{10,8},{12,14},{14,12},{16,18},{18,... | collective-permute-start | bytes 786440 | tf_op jit(solution)/shard_map/ppermute | solution.py:475
  464.5 63.6 %collective-permute-start.84 = (bf16[64,2048]{1,0:T(8,128)(2,1)}, bf16[64,2048]{1,0:T(8,128)(2,1)}, u32[]{:S(2)}, u32[]{:S(2)}) collective-permute-start(bf16[64,2048]{1,0:T(8,128)(2,1)} %get-tuple-element.435), channel_id=1, source_target_pairs={{0,4},{2,6},{4,0},{6,2},{8,12},{10,14},{12,8},{14,10},{16,20},{18,... | collective-permute-start | bytes 786440 | tf_op jit(solution)/shard_map/ppermute | solution.py:475
  501.3 61.5 %all-to-all-start.4 = ((bf16[8,1056,128]{2,1,0:T(8,128)(2,1)}), bf16[8,1056,128]{2,1,0:T(8,128)(2,1)}, u32[]{:S(2)}, u32[]{:S(2)}) async-start(bf16[8,1056,128]{2,1,0:T(8,128)(2,1)} %copy-done.6), calls=%async_computation.5 | async-start | bytes 4325376 | tf_op jit(solution)/shard_map/all_to_all | solution.py:522
  509.1 29.7 %collective-permute-start.88 = (bf16[64,2048]{1,0:T(8,128)(2,1)S(1)}, bf16[64,2048]{1,0:T(8,128)(2,1)S(1)}, u32[]{:S(2)}, u32[]{:S(2)}) collective-permute-start(bf16[64,2048]{1,0:T(8,128)(2,1)S(1)} %fusion.40), channel_id=1, source_target_pairs={{0,8},{2,10},{4,12},{6,14},{8,0},{10,2},{12,4},{14,6},{16,24},{18,... | collective-permute-start | bytes 786440 | tf_op jit(solution)/shard_map/ppermute | solution.py:475
  (142 other events, 1550.6 us)
Sparse Core Ops, SparseCore 0:
  10.9 66.0 all-gather.6
  118.2 102.7 all-gather.8
  306.5 105.0 all-gather.10
  433.3 112.6 reduce-scatter.1

commit v4 on v3

--- a/solution.py
+++ b/solution.py
@@ -259,12 +259,14 @@
 
 
 def mix_blocks_kernel(mix, out_weight, out):
-    heads, depth, _ = out.shape
+    groups, heads, depth, _ = out.shape
     for m in range(heads):
         cols = slice(m * HEAD_DIM, (m + 1) * HEAD_DIM)
-        for j in range(4):
-            out[m, :, j * HEAD_DIM : (j + 1) * HEAD_DIM] = mix[j, :, cols]
-        out[m, :, 4 * HEAD_DIM :] = out_weight[cols, :].astype(F32).T.astype(BF16)
+        turned = out_weight[cols, :].astype(F32).T.astype(BF16)
+        for g in range(groups):
+            for j in range(4):
+                out[g, m, :, j * HEAD_DIM : (j + 1) * HEAD_DIM] = mix[j, :, cols]
+            out[g, m, :, 4 * HEAD_DIM :] = turned
 
 
 def feed_blocks_kernel(up, down, out, turned):
@@ -500,10 +502,7 @@
         own = [got[bits] for bits in range(self.size)]
         return own, [self.other_core(block) for block in own]
 
-    def scatter(self, mine, away, meanwhile=None):
-        other = self.other_core(away)
-        part = [mine[b].astype(F32) + other[b].astype(F32) for b in range(self.size)]
-
+    def over_members(self, part, before_last=()):
         def add(to, source, bits):
             part[to] = part[to] + self.swap(part[source].astype(BF16), bits).astype(F32)
 
@@ -511,12 +510,15 @@
         add(2, 3, 1)
         add(4, 6, 2)
         add(0, 1, 1)
-        if meanwhile is not None:
-            part[5] = after(part[5], meanwhile)
         add(4, 5, 1)
         add(0, 2, 2)
+        part[4] = after(part[4], *before_last)
         add(0, 4, 4)
         return part[0]
+
+    def scatter(self, mine, other, before_last=()):
+        part = [mine[b].astype(F32) + other[b].astype(F32) for b in range(self.size)]
+        return self.over_members(part, before_last)
 
     def spread(self, blocks):
         return lax.all_to_all(blocks, "seq", 0, 0, axis_index_groups=self.lists, tiled=True)
@@ -612,13 +614,14 @@
     half_tokens = my_half(token_rows)
     half_inverse1 = my_half(inverse1)
     cot_half = my_half(cotangent)
-    (mix_blocks,) = call(
-        mix_blocks_kernel, [((heads, depth, 5 * HEAD_DIM), BF16)], (mix_weight, out_weight), us=2
-    )
-    mix_all = group.all_groups(mix_blocks)
-
-    def start_steps(rows, blocks, up, down):
+
+    def start_steps(rows, mix_weight, out_weight, up, down):
         own, other = group.gather(rows)
+        (mix_blocks,) = call(
+            mix_blocks_kernel, [((groups, heads, depth, 5 * HEAD_DIM), BF16)], (mix_weight, out_weight), us=2
+        )
+        mix_blocks = after(mix_blocks.reshape(peers, depth, 5 * HEAD_DIM), *other)
+        mix_own = lax.all_to_all(mix_blocks, "seq", 0, 0, tiled=True).reshape(width, 5 * HEAD_DIM)
         (feed_blocks,) = call(
             feed_blocks_kernel,
             [((heads, 3 * units, depth), BF16)],
@@ -626,30 +629,11 @@
             [pltpu.VMEM((heads * units, depth), BF16)],
             us=3,
         )
-        here = group.spread(after(blocks, *other))
-        feed = group.spread(after(feed_blocks, here))
-        return own, other, feed, here
-
-    normed1, normed1_other, feed_here, mix_here = together(
-        start_steps,
-        after((half_tokens * half_inverse1 * norm1_gain).astype(BF16), mix_blocks),
-        mix_blocks,
-        up_pair,
-        down_weight,
-    )
-    feed_own = group.all_groups(feed_here)
-
-    def forward_steps(mix_all, mix_here, normed1, normed1_other):
-        if groups == 2:
-            far = group.spread(lax.dynamic_index_in_dim(mix_all, 1 - group.index, 0, False))
-            mix_own = jnp.where(group.index == 0, jnp.stack([mix_here, far]), jnp.stack([far, mix_here]))
-        else:
-            mix_own = jnp.moveaxis(group.spread(jnp.moveaxis(mix_all, 0, 1)), 0, 1)
-        mix_own = mix_own.reshape(width, 5 * HEAD_DIM)
+        feed = group.spread(after(feed_blocks, mix_own))
         projected, tail = call(
             functools.partial(project_kernel, members=heads),
             [((length, 4 * HEAD_DIM), BF16), ((16, 3 * HEAD_DIM), BF16)],
-            (*normed1, *normed1_other, mix_own),
+            (*own, *other, mix_own),
             (),
             ids,
         )
@@ -668,28 +652,46 @@
             (projected, halo, taps, gap),
             [pltpu.VMEM((length + 16, 3 * HEAD_DIM), F32)],
         )
-        cot, cot_other = group.gather(after(cot_half, halo))
         own_decay = last[HEAD_DIM : HEAD_DIM + 1]
         carry = group.carry(last[:HEAD_DIM], own_decay, 1)
+        decays = jnp.exp(jnp.concatenate([totals[1:] - totals[:-1], jnp.log(own_decay) - totals[-1:]], axis=0))
+        kept = (mix_own, projected, halo, conv, query, key)
+        return own, other, feed, kept, (own_decay, decays), (mixed_here, totals, states, carry)
+
+    normed1, normed1_other, feed_here, kept, decay_rows, here = together(
+        start_steps,
+        (half_tokens * half_inverse1 * norm1_gain).astype(BF16),
+        mix_weight,
+        out_weight,
+        up_pair,
+        down_weight,
+    )
+    feed_own = group.all_groups(feed_here)
+
+    def both_halves(rows):
+        other = group.other_core(rows)
+        return jnp.where(core == 0, jnp.concatenate([rows, other], 0), jnp.concatenate([other, rows], 0))
+
+    def forward_steps(kept, here, cot_half):
+        mix_own, projected, _, _, query, _ = kept
+        mixed_here, totals, states, carry = here
+        cot, cot_other = group.gather(cot_half)
         mixed, states, turned_gated, mine, away = call(
             gate_kernel,
             [many(1), ((count, HEAD_DIM, HEAD_DIM), F32), ((HEAD_DIM, length), BF16), all_rows, all_rows],
             (mixed_here, query, totals, states, carry, projected, gain, mix_own),
             [pltpu.VMEM((length, HEAD_DIM), BF16)],
             ids,
-            tuple(cot),
-        )
-        hidden = half_tokens + group.scatter(mine, away)
+        )
+        hidden = half_tokens + group.scatter(mine, group.other_core(away))
         inverse2 = inverse_of(hidden)
         normed2, normed2_other = group.gather((hidden * inverse2 * norm2_gain).astype(BF16))
-        decays = jnp.exp(jnp.concatenate([totals[1:] - totals[:-1], jnp.log(own_decay) - totals[-1:]], axis=0))
-        kept = (mix_own, projected, halo, conv, query, key, states, mixed, own_decay, decays)
-        return kept, (normed2, normed2_other, cot, cot_other), (turned_gated, hidden, inverse2)
-
-    kept, feed_rows, (turned_gated, hidden, inverse2) = together(
-        forward_steps, mix_all, mix_here, normed1, normed1_other
-    )
-    feed_rows = tuple(block for blocks in feed_rows for block in blocks)
+        return (states, mixed), (*normed2, *normed2_other, *cot, *cot_other), (turned_gated, hidden, inverse2, both_halves(inverse2))
+
+    mixed_rows, feed_rows, (turned_gated, hidden, inverse2, inverse2_all) = together(
+        forward_steps, kept, here, cot_half
+    )
+    kept = (*kept, *mixed_rows, *decay_rows)
     turned, inner, mine, away = call(
         functools.partial(feed_kernel, members=heads),
         [((3 * wide, length), BF16), ((length, wide), BF16), all_rows, all_rows],
@@ -700,11 +702,12 @@
     )
     feed_grad = functools.partial(feed_grad_kernel, members=heads)
     feed_args = (*feed_rows, turned)
-    feed_away = group.away(feed_grad, 3 * units, depth, feed_args, 5)
-
-    def backward_steps(mine, away, kept, hidden, inverse2, normed1, normed1_other, turned_gated):
+    other = group.other_core(away)
+    feed_away = group.away(feed_grad, 3 * units, depth, feed_args, 7)
+
+    def backward_steps(mine, other, kept, hidden, inverse2, normed1, normed1_other, turned_gated):
         mix_own, projected, halo, conv, query, key, states, mixed, own_decay, decays = kept
-        grad_normed2 = group.scatter(mine, away)
+        grad_normed2 = group.scatter(mine, other)
         grad_hidden_norm, grad_norm2 = norm_back(hidden, inverse2, norm2_gain, grad_normed2)
         grad_hidden = cot_half.astype(F32) + grad_hidden_norm
         branch, branch_other = group.gather(grad_hidden.astype(BF16))
@@ -761,15 +764,14 @@
 
     extra = -(-(14 * HEAD_DIM + 2 * width) // (16 * depth)) * 16
     grad_hidden, grad_mix, both = together(
-        backward_steps, mine, away, kept, hidden, inverse2, normed1, normed1_other, turned_gated
-    )
-    grad_normed1 = lax.psum_scatter(both, "seq", axis_index_groups=group.lists).astype(F32)
+        backward_steps, mine, other, kept, hidden, inverse2, normed1, normed1_other, turned_gated
+    )
+    grad_normed1 = lax.psum_scatter(both, "seq", axis_index_groups=group.lists)
     mix_got = lax.all_to_all(after(grad_mix, feed_away), "seq", 0, 0, tiled=True)
+    feed_total = group.over_groups(feed_grad, feed_args, feed_away, (grad_mix,), 8)
     (block_mine, block_away) = call(
-        block_kernel, [all_rows, all_rows], (inner, feed_own), [pltpu.VMEM((wide, width), BF16)], None, (grad_mix,)
-    )
-    block_half = hidden + group.scatter(block_mine, block_away)
-    feed_total = group.over_groups(feed_grad, feed_args, feed_away, (grad_mix,), 8)
+        block_kernel, [all_rows, all_rows], (inner, feed_own), [pltpu.VMEM((wide, width), BF16)], None, (feed_total,)
+    )
     feed_got = group.spread(after(feed_total, mix_got))
     mix_total, out_total = call(
         mix_total_kernel,
@@ -777,6 +779,14 @@
         (mix_got.reshape(groups, heads, 5 * HEAD_DIM + extra, depth),),
         us=4,
     )
+    sums = mix_got[:, 5 * HEAD_DIM :].reshape(groups, heads, -1).astype(F32).sum(0)
+    own_sums = sums[:, : 14 * HEAD_DIM].reshape(heads, 14, HEAD_DIM).transpose(1, 0, 2).reshape(14, heads * HEAD_DIM)
+    norms = sums[:, 14 * HEAD_DIM : 14 * HEAD_DIM + 2 * width].sum(0).reshape(2, width)
+    norms = norms + group.other_core(norms)
+    block_half = hidden + group.scatter(
+        block_mine, group.other_core(block_away), (mix_total, out_total, own_sums, norms)
+    )
+    grad_normed1 = after(grad_normed1, block_half).astype(F32)
     grad_rows1 = norm_back(half_tokens, half_inverse1, norm1_gain, grad_normed1)[0]
     grad_tokens = grad_hidden + grad_rows1
     up_total, down_total = call(
@@ -785,19 +795,10 @@
         (feed_got,),
         [pltpu.VMEM((heads * units, depth), F32)],
     )
-    def both_halves(rows):
-        other = group.other_core(rows)
-        return jnp.where(core == 0, jnp.concatenate([rows, other], 0), jnp.concatenate([other, rows], 0))
-
     block_out = both_halves(block_half)
     grad_tokens = both_halves(grad_tokens)
-    inverse2 = both_halves(inverse2)
-
-    sums = mix_got[:, 5 * HEAD_DIM :].reshape(groups, heads, -1).astype(F32).sum(0)
-    own_sums = sums[:, : 14 * HEAD_DIM].reshape(heads, 14, HEAD_DIM).transpose(1, 0, 2).reshape(14, heads * HEAD_DIM)
-    norms = sums[:, 14 * HEAD_DIM : 14 * HEAD_DIM + 2 * width].sum(0).reshape(2, width)
-    norms = norms + group.other_core(norms)
-    inverse_rms = jnp.stack([inverse1[:, 0], inverse2[:, 0]])
+
+    inverse_rms = jnp.stack([inverse1[:, 0], inverse2_all[:, 0]])
     return (
         block_out,
         grad_tokens,

time: 585 us -> 573 us (0.979)
  starting transfers between devices: 119 us -> 91.6 us
  waiting for transfers between devices: 296 us -> 313 us
  local copies, waits for them, and re-layouts: 24.2 us -> 17.4 us
  Pallas kernels: 85.6 us -> 92.2 us
    all_to_all x4 -> x2, waiting for transfers between devices: 95.4 us -> 0.01 us  [spread(): lax.all_to_all(blocks, 'seq', 0, 0, axis_index_groups=self.lists, tiled=T...]
    all_to_all x0 -> x1, waiting for transfers between devices: none -> 56.9 us  [start_steps(): lax.all_to_all(mix_blocks, 'seq', 0, 0, tiled=True)]
    all_to_all x1, waiting for transfers between devices: 0.01 us -> 42.1 us  [shards(): lax.all_to_all(after(grad_mix, feed_away), 'seq', 0, 0, tiled=True)]
    ppermute x49, starting transfers between devices: 72.1 us -> 49.9 us  [swap(): lax.ppermute(value, 'seq', [(s, s ^ bits) for s in range(self.peers)])]
    all_to_all x4 -> x2, starting transfers between devices: 22.4 us -> 8.9 us  [spread(): lax.all_to_all(blocks, 'seq', 0, 0, axis_index_groups=self.lists, tiled=T...]
    ppermute x4, waiting for transfers between devices: 16.8 us -> 30.2 us  [shift(): return lax.ppermute(value, 'seq', pairs)]
    all_gather x3 -> x2, waiting for transfers between devices: 0.02 us -> 10.1 us  [all_groups(): return lax.all_gather(value, 'seq', axis_index_groups=self.columns)]
    all_to_all x0 -> x1, starting transfers between devices: none -> 7.23 us  [start_steps(): lax.all_to_all(mix_blocks, 'seq', 0, 0, tiled=True)]
  transfers between devices with their start and end apart: 102 -> 100, of which waited for: 52 -> 41; matrix products, arithmetic and copies ran while one was open for 7% -> 6% of each run, Pallas kernels for 10% -> 12%
where the time goes in v4:
time: 573 us; the launch traced here: 564 us
  waiting for transfers between devices  313 us (55%)
  Pallas kernels  92.2 us (16%)
  starting transfers between devices  91.6 us (16%)
  other arithmetic  34.3 us (6%)
  local copies, waits for them, and re-layouts  17.4 us (3%)
  between operations  14.6 us (3%)
    ppermute x49, waiting for transfers between devices, swap(): lax.ppermute(value, 'seq', [(s, s ^ bits) for s in range(self.peers)])  158 us
    pallas_call x15, Pallas kernels, call(): pl.pallas_call(body, out_shape=[jax.ShapeDtypeStruct(s, d) for s, d in ou...  92.2 us
    all_to_all x1, waiting for transfers between devices, start_steps(): lax.all_to_all(mix_blocks, 'seq', 0, 0, tiled=True)  56.9 us
    ppermute x49, starting transfers between devices, swap(): lax.ppermute(value, 'seq', [(s, s ^ bits) for s in range(self.peers)])  49.9 us
    all_to_all x1, waiting for transfers between devices, shards(): lax.all_to_all(after(grad_mix, feed_away), 'seq', 0, 0, tiled=True)  42.1 us
    ppermute x4, waiting for transfers between devices, shift(): return lax.ppermute(value, 'seq', pairs)  30.2 us
    ppermute x40, waiting for transfers between devices, other_core(): return lax.ppermute(value, 'head', [(0, 1), (1, 0)])  15.9 us
  transfers between devices with their start and end apart: 100, of which 41 were waited for; matrix products, arithmetic and copies ran while one was open for 6% of the time, Pallas kernels for 12%

profile of v4, /device:TPU:18, one launch (start us, length us, event | category | flops | bytes accessed | tf_op | source)
XLA Modules:
  0.0 563.5 jit_solution(4400765699793668583)
XLA Ops:
  11.5 141.5 %conditional.3 = (bf16[64,2048]{1,0:T(8,128)(2,1)S(1)}, bf16[64,2048]{1,0:T(8,128)(2,1)}, bf16[64,2048]{1,0:T(8,128)(2,1)}, bf16[64,2048]{1,0:T(8,128)(2,1)}, bf...) conditional(s32[]{:T(128)} %convert_element_type.395, () %tuple.42, ...), branch_computations={%region_1.0_spmd, %region_2.0_spmd} | conditional | flops 2048 | bytes 78952744 | solution.py:563
  39.2 7.2 %all-to-all-start = ((bf16[16,128,640]{2,1,0:T(8,128)(2,1)}), bf16[16,128,640]{2,1,0:T(8,128)(2,1)}, u32[]{:S(2)}, u32[]{:S(2)}) async-start(bf16[16,128,640]{2,1,0:T(8,128)(2,1)} %bitcast), calls=%async_computation | async-start | bytes 5242880 | tf_op jit(solution)/shard_map/cond/branch_1_fun/all_to_all | solution.py:624
  49.8 56.9 %all-to-all-done = bf16[16,128,640]{2,1,0:T(8,128)(2,1)} async-done(((bf16[16,128,640]{2,1,0:T(8,128)(2,1)}), bf16[16,128,640]{2,1,0:T(8,128)(2,1)}, u32[]{:S(2)}, u32[]{:S(2)}) %all-to-all-start) | async-done | bytes 2621472 | tf_op jit(solution)/shard_map/cond/branch_1_fun/all_to_all | solution.py:624
  111.0 6.3 %branch_1_fun.11 = (bf16[1024,512]{1,0:T(8,128)(2,1)}, bf16[16,384]{1,0:T(8,128)(2,1)S(1)}) custom-call(s32[2]{0:T(128)S(1)} %get-tuple-element.126.refs_0_, bf16[64,2048]{1,0:T(8,128)(2,1)S(1)} %get-tuple-element.457.refs_1_, bf16[64,2048]{1,0:T(8,128)(2,1)} %collective-permute-done.refs_2_, bf16[64,2048]{1,0:T(8,128)(2,1)} %collective-permute-done.1.refs_3_, ...), custom_call_target="tpu_custom_call" | custom-call | bytes 15000000 | tf_op jit(solution)/shard_map/cond/branch_1_fun/pallas_call | solution.py:453
  118.6 19.9 %collective-permute-done.15.refs_1_ = bf16[16,384]{1,0:T(8,128)(2,1)} collective-permute-done((bf16[16,384]{1,0:T(8,128)(2,1)S(1)}, bf16[16,384]{1,0:T(8,128)(2,1)}, u32[]{:S(2)}, u32[]{:S(2)}) %collective-permute-start.15) | collective-permute-done | bytes 12320 | tf_op jit(solution)/shard_map/cond/branch_1_fun/ppermute | solution.py:485
  138.5 7.3 %branch_1_fun.12 = (f32[1024,384]{1,0:T(8,128)}, f32[1024,128]{1,0:T(8,128)S(1)}, f32[1024,128]{1,0:T(8,128)}, f32[8,128]{1,0:T(8,128)}, f32[8,128,128]{2,1,0:T(...) custom-call(bf16[1024,512]{1,0:T(8,128)(2,1)} %get-tuple-element.475.refs_0_, ...), custom_call_target="tpu_custom_call" | custom-call | bytes 15000000 | tf_op jit(solution)/shard_map/cond/branch_1_fun/pallas_call | solution.py:453
  154.4 90.4 %conditional.4 = (f32[8,128,128]{2,1,0:T(8,128)S(1)}, f32[1024,128]{1,0:T(8,128)S(1)}, bf16[64,2048]{1,0:T(8,128)(2,1)}, bf16[64,2048]{1,0:T(8,128)(2,1)}, bf16[...) conditional(s32[]{:T(128)} %convert_element_type.395, () %tuple.41, ...), branch_computations={%region_3.0_spmd, %region_4.6_spmd} | conditional | flops 6685377 | bytes 72423696 | solution.py:563
  166.6 6.2 %collective-permute-done.44 = bf16[64,2048]{1,0:T(8,128)(2,1)S(1)} collective-permute-done((bf16[64,2048]{1,0:T(8,128)(2,1)S(1)}, bf16[64,2048]{1,0:T(8,128)(2,1)S(1)}, u32[]{:S(2)}, u32[]{:S(2)}) %collective-permute-start.44) | collective-permute-done | bytes 262176 | tf_op jit(solution)/shard_map/cond/branch_1_fun/ppermute | solution.py:477
  183.5 7.4 %collective-permute-done.68 = bf16[64,2048]{1,0:T(8,128)(2,1)} collective-permute-done((bf16[64,2048]{1,0:T(8,128)(2,1)S(1)}, bf16[64,2048]{1,0:T(8,128)(2,1)}, u32[]{:S(2)}, u32[]{:S(2)}) %collective-permute-start.68) | collective-permute-done | bytes 262176 | tf_op jit(solution)/shard_map/cond/branch_1_fun/ppermute | solution.py:477
  194.4 6.5 %collective-permute-done.49 = bf16[64,2048]{1,0:T(8,128)(2,1)S(1)} collective-permute-done((bf16[64,2048]{1,0:T(8,128)(2,1)S(1)}, bf16[64,2048]{1,0:T(8,128)(2,1)S(1)}, u32[]{:S(2)}, u32[]{:S(2)}) %collective-permute-start.49) | collective-permute-done | bytes 262176 | tf_op jit(solution)/shard_map/cond/branch_1_fun/ppermute | solution.py:477
  215.9 10.0 %collective-permute-done.53 = bf16[64,2048]{1,0:T(8,128)(2,1)} collective-permute-done((bf16[64,2048]{1,0:T(8,128)(2,1)}, bf16[64,2048]{1,0:T(8,128)(2,1)}, u32[]{:S(2)}, u32[]{:S(2)}) %collective-permute-start.53) | collective-permute-done | bytes 262176 | tf_op jit(solution)/shard_map/cond/branch_1_fun/ppermute | solution.py:477
  245.6 10.1 %all-gather.5.cloned.1.call-done = bf16[16,1056,128]{2,1,0:T(8,128)(2,1)} async-done(((bf16[8,1056,128]{2,1,0:T(8,128)(2,1)}), bf16[16,1056,128]{2,1,0:T(8,128)(2,1)}) %all-gather.5.cloned.1.call-update) | async-done | bytes 4325392 | tf_op jit(solution)/shard_map/all_gather | solution.py:527
  257.9 15.5 %shard_map.206 = (bf16[1152,1024]{1,0:T(8,128)(2,1)S(1)}, bf16[1024,384]{1,0:T(8,128)(2,1)S(1)}, bf16[8,64,2048]{2,1,0:T(8,128)(2,1)}, bf16[8,64,2048]{2,1,0:T(8,128)(2,1)S(1)}) custom-call(bf16[64,2048]{1,0:T(8,128)(2,1)} %get-tuple-element.309.refs_0_.refs_1_, bf16[64,2048]{1,0:T(8,128)(2,1)} %get-tuple-element.310.refs_1_.refs_2_, ...), custom_call_target="tpu_custom_call" | custom-call | bytes 51000000 | tf_op jit(solution)/shard_map/pallas_call | solution.py:453
  274.3 7.1 %shard_map.207 = bf16[8,1056,128]{2,1,0:T(8,128)(2,1)} custom-call(s32[4]{0:T(128)S(1)} %pad_add_fusion.3.refs_0_, bf16[64,2048]{1,0:T(8,128)(2,1)} %get-tuple-element.309.refs_0_.refs_1_, bf16[64,2048]{1,0:T(8,128)(2,1)} %get-tuple-element.310.refs_1_.refs_2_, bf16[64,2048]{1,0:T(8,128)(2,1)} %get-tuple-element.311.refs_2_.refs_3_, ...), custom_call_target="tpu_custom_call" | custom-call | bytes 21000000 | tf_op jit(solution)/shard_map/pallas_call | solution.py:453
  287.1 109.0 %conditional.5 = (f32[64,2048]{1,0:T(8,128)}, bf16[16,688,128]{2,1,0:T(8,128)(2,1)}, bf16[8,64,2048]{2,1,0:T(8,128)(2,1)}) conditional(s32[]{:T(128)} %convert_element_type.395, () %tuple.45, (bf16[64,2048]{1,0:T(8,128)(2,1)}, f32[64,1]{0,1:T(1,128)}, bf16[8,64,2048]{2,1,0:T(8,128)(2,1)}, bf16[8,64,2048]{2,1,0:T(8,128)(2,1)S(1)}, ...), branch_computations={%region_6.7_spmd, %region_7.10_spmd} | conditional | flops 12006528 | bytes 153208320 | solution.py:563
  311.4 10.1 %collective-permute-done.23 = bf16[64,2048]{1,0:T(8,128)(2,1)S(1)} collective-permute-done((bf16[64,2048]{1,0:T(8,128)(2,1)S(1)}, bf16[64,2048]{1,0:T(8,128)(2,1)S(1)}, u32[]{:S(2)}, u32[]{:S(2)}) %collective-permute-start.23) | collective-permute-done | bytes 262176 | tf_op jit(solution)/shard_map/cond/branch_1_fun/ppermute | solution.py:477
  328.0 9.6 %collective-permute-done.27.refs_5_.refs_21_ = bf16[64,2048]{1,0:T(8,128)(2,1)S(1)} collective-permute-done((bf16[64,2048]{1,0:T(8,128)(2,1)S(1)}, bf16[64,2048]{1,0:T(8,128)(2,1)S(1)}, u32[]{:S(2)}, u32[]{:S(2)}) %collective-permute-start.27) | collective-permute-done | bytes 262176 | tf_op jit(solution)/shard_map/cond/branch_1_fun/ppermute | solution.py:477
  365.1 9.5 %branch_1_fun.15 = (bf16[1024,384]{1,0:T(8,128)(2,1)S(1)}, f32[16,384]{1,0:T(8,128)S(1)}, f32[8,384]{1,0:T(8,128)S(1)}, f32[16,128]{1,0:T(8,128)S(1)}) custom-call(f32[1024,128]{1,0:T(8,128)S(1)} %get-tuple-element.186.refs_0_, f32[1024,384]{1,0:T(8,128)S(1)} %copy-done.9, f32[1024,128]{1,0:T(8,128)S(1)} %get-tuple-element.184.refs_21_.refs_2_, ...), custom_call_target="tpu_custom_call" | custom-call | bytes 24000000 | tf_op jit(solution)/shard_map/cond/branch_1_fun/pallas_call | solution.py:453
  387.4 6.6 %branch_1_fun.17 = bf16[16,688,128]{2,1,0:T(8,128)(2,1)} custom-call(s32[4]{0:T(128)S(1)} %get-tuple-element.162.refs_0_, bf16[64,2048]{1,0:T(8,128)(2,1)S(1)} %get-tuple-element.163.refs_1_, bf16[64,2048]{1,0:T(8,128)(2,1)} %get-tuple-element.164.refs_2_, bf16[64,2048]{1,0:T(8,128)(2,1)} %get-tuple-element.165.refs_3_, ...), custom_call_target="tpu_custom_call" | custom-call | bytes 21000000 | tf_op jit(solution)/shard_map/cond/branch_1_fun/pallas_call | solution.py:453
  396.1 7.9 %all-to-all-start.2 = ((bf16[16,688,128]{2,1,0:T(8,128)(2,1)}), bf16[16,688,128]{2,1,0:T(8,128)(2,1)S(1)}, u32[]{:S(2)}, u32[]{:S(2)}) async-start(bf16[16,688,128]{2,1,0:T(8,128)(2,1)} %get-tuple-element.373.refs_35_), calls=%async_computation.2 | async-start | bytes 5636096 | tf_op jit(solution)/shard_map/all_to_all | solution.py:770
  408.1 7.5 %shard_map.208.refs_2_ = bf16[8,1056,128]{2,1,0:T(8,128)(2,1)} custom-call(s32[4]{0:T(128)S(1)} %pad_add_fusion.1.refs_0_, bf16[64,2048]{1,0:T(8,128)(2,1)} %get-tuple-element.309.refs_0_.refs_1_, bf16[64,2048]{1,0:T(8,128)(2,1)} %get-tuple-element.310.refs_1_.refs_2_, bf16[64,2048]{1,0:T(8,128)(2,1)} %get-tuple-element.311.refs_2_.refs_3_, ...), custom_call_target="tpu_custom_call" | custom-call | bytes 24000000 | tf_op jit(solution)/shard_map/pallas_call | solution.py:453
  432.0 42.1 %all-to-all-done.2 = bf16[16,688,128]{2,1,0:T(8,128)(2,1)S(1)} async-done(((bf16[16,688,128]{2,1,0:T(8,128)(2,1)}), bf16[16,688,128]{2,1,0:T(8,128)(2,1)S(1)}, u32[]{:S(2)}, u32[]{:S(2)}) %all-to-all-start.2) | async-done | bytes 2818080 | tf_op jit(solution)/shard_map/all_to_all | solution.py:770
  487.5 43.7 %collective-permute-done.88 = bf16[64,2048]{1,0:T(8,128)(2,1)} collective-permute-done((bf16[64,2048]{1,0:T(8,128)(2,1)}, bf16[64,2048]{1,0:T(8,128)(2,1)}, u32[]{:S(2)}, u32[]{:S(2)}) %collective-permute-start.88) | collective-permute-done | bytes 262176 | tf_op jit(solution)/shard_map/ppermute | solution.py:477
  536.8 7.0 %collective-permute-done.90 = bf16[64,2048]{1,0:T(8,128)(2,1)S(1)} collective-permute-done((bf16[64,2048]{1,0:T(8,128)(2,1)}, bf16[64,2048]{1,0:T(8,128)(2,1)S(1)}, u32[]{:S(2)}, u32[]{:S(2)}) %collective-permute-start.90) | collective-permute-done | bytes 262176 | tf_op jit(solution)/shard_map/ppermute | solution.py:477
  (319 shorter events, 244.0 us)
Async XLA Ops:
  7.2 248.5 %all-gather.5.cloned.1.call-start = ((), (), s32[]{:S(2)}) async-start(), calls=%async_computation.6 | async-start | bytes 6488064 | tf_op jit(solution)/shard_map/all_gather | solution.py:527
  39.2 67.6 %all-to-all-start = ((bf16[16,128,640]{2,1,0:T(8,128)(2,1)}), bf16[16,128,640]{2,1,0:T(8,128)(2,1)}, u32[]{:S(2)}, u32[]{:S(2)}) async-start(bf16[16,128,640]{2,1,0:T(8,128)(2,1)} %bitcast), calls=%async_computation | async-start | bytes 5242880 | tf_op jit(solution)/shard_map/cond/branch_1_fun/all_to_all | solution.py:624
  106.7 46.3 %all-to-all-start.1 = ((bf16[8,1056,128]{2,1,0:T(8,128)(2,1)}), bf16[8,1056,128]{2,1,0:T(8,128)(2,1)}, u32[]{:S(2)}, u32[]{:S(2)}) async-start(bf16[8,1056,128]{2,1,0:T(8,128)(2,1)} %branch_1_fun.9), calls=%async_computation.1 | async-start | bytes 4325376 | tf_op jit(solution)/shard_map/cond/branch_1_fun/all_to_all | solution.py:524
  117.3 21.2 %collective-permute-start.15 = (bf16[16,384]{1,0:T(8,128)(2,1)S(1)}, bf16[16,384]{1,0:T(8,128)(2,1)}, u32[]{:S(2)}, u32[]{:S(2)}) collective-permute-start(bf16[16,384]{1,0:T(8,128)(2,1)S(1)} %get-tuple-element.128), channel_id=1, source_target_pairs={{0,16},{2,18},{4,20},{6,22},{8,24},{10,26},{12,28},{14,30},{1,17},... | collective-permute-start | bytes 36872 | tf_op jit(solution)/shard_map/cond/branch_1_fun/ppermute | solution.py:485
  153.0 243.1 %all-gather.7.cloned.1.call-start = ((), (), s32[]{:S(2)}) async-start(), calls=%async_computation.7 | async-start | bytes 6488064 | tf_op jit(solution)/shard_map/all_gather | solution.py:527
  176.0 14.9 %collective-permute-start.68 = (bf16[64,2048]{1,0:T(8,128)(2,1)S(1)}, bf16[64,2048]{1,0:T(8,128)(2,1)}, u32[]{:S(2)}, u32[]{:S(2)}) collective-permute-start(bf16[64,2048]{1,0:T(8,128)(2,1)S(1)} %get-tuple-element.541), channel_id=1, source_target_pairs={{0,8},{2,10},{4,12},{6,14},{8,0},{10,2},{12,4},{14,6},{16,24},{18,... | collective-permute-start | bytes 786440 | tf_op jit(solution)/shard_map/cond/branch_1_fun/ppermute | solution.py:477
  176.0 14.9 %collective-permute-start.66 = (bf16[64,2048]{1,0:T(8,128)(2,1)S(1)}, bf16[64,2048]{1,0:T(8,128)(2,1)}, u32[]{:S(2)}, u32[]{:S(2)}) collective-permute-start(bf16[64,2048]{1,0:T(8,128)(2,1)S(1)} %get-tuple-element.541), channel_id=1, source_target_pairs={{0,4},{2,6},{4,0},{6,2},{8,12},{10,14},{12,8},{14,10},{16,20},{18,... | collective-permute-start | bytes 786440 | tf_op jit(solution)/shard_map/cond/branch_1_fun/ppermute | solution.py:477
  183.4 17.5 %collective-permute-start.49 = (bf16[64,2048]{1,0:T(8,128)(2,1)S(1)}, bf16[64,2048]{1,0:T(8,128)(2,1)S(1)}, u32[]{:S(2)}, u32[]{:S(2)}) collective-permute-start(bf16[64,2048]{1,0:T(8,128)(2,1)S(1)} %fusion.1), channel_id=1, source_target_pairs={{0,8},{2,10},{4,12},{6,14},{8,0},{10,2},{12,4},{14,6},{16,24},{18,... | collective-permute-start | bytes 786440 | tf_op jit(solution)/shard_map/cond/branch_1_fun/ppermute | solution.py:477
  191.0 14.1 %collective-permute-start.69 = (bf16[64,2048]{1,0:T(8,128)(2,1)}, bf16[64,2048]{1,0:T(8,128)(2,1)}, u32[]{:S(2)}, u32[]{:S(2)}) collective-permute-start(bf16[64,2048]{1,0:T(8,128)(2,1)} %collective-permute-done.68), channel_id=1, source_target_pairs={{0,2},{2,0},{4,6},{6,4},{8,10},{10,8},{12,14},{14,12},{16,18},{18,... | collective-permute-start | bytes 786440 | tf_op jit(solution)/shard_map/cond/branch_1_fun/ppermute | solution.py:477
  211.0 14.9 %collective-permute-start.53 = (bf16[64,2048]{1,0:T(8,128)(2,1)}, bf16[64,2048]{1,0:T(8,128)(2,1)}, u32[]{:S(2)}, u32[]{:S(2)}) collective-permute-start(bf16[64,2048]{1,0:T(8,128)(2,1)} %multiply_convert_fusion), channel_id=1, source_target_pairs={{0,8},{2,10},{4,12},{6,14},{8,0},{10,2},{12,4},{14,6},{16,24},{18,... | collective-permute-start | bytes 786440 | tf_op jit(solution)/shard_map/cond/branch_1_fun/ppermute | solution.py:477
  215.6 14.4 %collective-permute-start.50 = (bf16[64,2048]{1,0:T(8,128)(2,1)}, bf16[64,2048]{1,0:T(8,128)(2,1)}, u32[]{:S(2)}, u32[]{:S(2)}) collective-permute-start(bf16[64,2048]{1,0:T(8,128)(2,1)} %multiply_convert_fusion), channel_id=1, source_target_pairs={{0,2},{2,0},{4,6},{6,4},{8,10},{10,8},{12,14},{14,12},{16,18},{18,... | collective-permute-start | bytes 786440 | tf_op jit(solution)/shard_map/cond/branch_1_fun/ppermute | solution.py:477
  215.6 14.4 %collective-permute-start.57 = (bf16[64,2048]{1,0:T(8,128)(2,1)}, bf16[64,2048]{1,0:T(8,128)(2,1)}, u32[]{:S(2)}, u32[]{:S(2)}) collective-permute-start(bf16[64,2048]{1,0:T(8,128)(2,1)} %multiply_convert_fusion), channel_id=1, source_target_pairs={{0,1},{1,0},{2,3},{3,2},{4,5},{5,4},{6,7},{7,6},{8,9},{9,8},{10,11... | collective-permute-start | bytes 786440 | tf_op jit(solution)/shard_map/cond/branch_1_fun/ppermute | solution.py:480
  325.1 13.9 %collective-permute-start.25 = (bf16[64,2048]{1,0:T(8,128)(2,1)S(1)}, bf16[64,2048]{1,0:T(8,128)(2,1)S(1)}, u32[]{:S(2)}, u32[]{:S(2)}) collective-permute-start(bf16[64,2048]{1,0:T(8,128)(2,1)S(1)} %get-tuple-element.396.refs_1_.refs_17_), channel_id=1, source_target_pairs={{0,4},{2,6},{4,0},{6,2},{8,12},{10,14},{12,8},{14,10},{16,20},{18,... | collective-permute-start | bytes 786440 | tf_op jit(solution)/shard_map/cond/branch_1_fun/ppermute | solution.py:477
  326.6 14.5 %collective-permute-start.24 = (bf16[64,2048]{1,0:T(8,128)(2,1)S(1)}, bf16[64,2048]{1,0:T(8,128)(2,1)S(1)}, u32[]{:S(2)}, u32[]{:S(2)}) collective-permute-start(bf16[64,2048]{1,0:T(8,128)(2,1)S(1)} %get-tuple-element.396.refs_1_.refs_17_), channel_id=1, source_target_pairs={{0,2},{2,0},{4,6},{6,4},{8,10},{10,8},{12,14},{14,12},{16,18},{18,... | collective-permute-start | bytes 786440 | tf_op jit(solution)/shard_map/cond/branch_1_fun/ppermute | solution.py:477
  396.1 78.0 %all-to-all-start.2 = ((bf16[16,688,128]{2,1,0:T(8,128)(2,1)}), bf16[16,688,128]{2,1,0:T(8,128)(2,1)S(1)}, u32[]{:S(2)}, u32[]{:S(2)}) async-start(bf16[16,688,128]{2,1,0:T(8,128)(2,1)} %get-tuple-element.373.refs_35_), calls=%async_computation.2 | async-start | bytes 5636096 | tf_op jit(solution)/shard_map/all_to_all | solution.py:770
  404.1 141.3 %reduce-scatter.2.cloned.1.call-start = ((), (), s32[]{:S(2)}) async-start(), calls=%async_computation.5 | async-start | bytes 2359296 | tf_op jit(solution)/shard_map/reduce_scatter | solution.py:769
  428.0 50.7 %collective-permute-start.84 = (bf16[64,2048]{1,0:T(8,128)(2,1)}, bf16[64,2048]{1,0:T(8,128)(2,1)}, u32[]{:S(2)}, u32[]{:S(2)}) collective-permute-start(bf16[64,2048]{1,0:T(8,128)(2,1)} %get-tuple-element.418), channel_id=1, source_target_pairs={{0,2},{2,0},{4,6},{6,4},{8,10},{10,8},{12,14},{14,12},{16,18},{18,... | collective-permute-start | bytes 786440 | tf_op jit(solution)/shard_map/ppermute | solution.py:477
  428.5 50.2 %collective-permute-start.87 = (bf16[64,2048]{1,0:T(8,128)(2,1)}, bf16[64,2048]{1,0:T(8,128)(2,1)}, u32[]{:S(2)}, u32[]{:S(2)}) collective-permute-start(bf16[64,2048]{1,0:T(8,128)(2,1)} %get-tuple-element.416), channel_id=1, source_target_pairs={{0,4},{2,6},{4,0},{6,2},{8,12},{10,14},{12,8},{14,10},{16,20},{18,... | collective-permute-start | bytes 786440 | tf_op jit(solution)/shard_map/ppermute | solution.py:477
  430.0 57.5 %collective-permute-start.86 = (bf16[64,2048]{1,0:T(8,128)(2,1)}, bf16[64,2048]{1,0:T(8,128)(2,1)}, u32[]{:S(2)}, u32[]{:S(2)}) collective-permute-start(bf16[64,2048]{1,0:T(8,128)(2,1)} %get-tuple-element.417), channel_id=1, source_target_pairs={{0,4},{2,6},{4,0},{6,2},{8,12},{10,14},{12,8},{14,10},{16,20},{18,... | collective-permute-start | bytes 786440 | tf_op jit(solution)/shard_map/ppermute | solution.py:477
  430.6 106.3 %collective-permute-start.83 = (bf16[64,2048]{1,0:T(8,128)(2,1)}, bf16[64,2048]{1,0:T(8,128)(2,1)}, u32[]{:S(2)}, u32[]{:S(2)}) collective-permute-start(bf16[64,2048]{1,0:T(8,128)(2,1)} %get-tuple-element.415), channel_id=1, source_target_pairs={{0,2},{2,0},{4,6},{6,4},{8,10},{10,8},{12,14},{14,12},{16,18},{18,... | collective-permute-start | bytes 786440 | tf_op jit(solution)/shard_map/ppermute | solution.py:477
  474.1 78.3 %all-to-all-start.3 = ((bf16[8,1056,128]{2,1,0:T(8,128)(2,1)}), bf16[8,1056,128]{2,1,0:T(8,128)(2,1)}, u32[]{:S(2)}, u32[]{:S(2)}) async-start(bf16[8,1056,128]{2,1,0:T(8,128)(2,1)} %shard_map.208.refs_2_), calls=%async_computation.4 | async-start | bytes 4325376 | tf_op jit(solution)/shard_map/all_to_all | solution.py:524
  481.1 50.1 %collective-permute-start.88 = (bf16[64,2048]{1,0:T(8,128)(2,1)}, bf16[64,2048]{1,0:T(8,128)(2,1)}, u32[]{:S(2)}, u32[]{:S(2)}) collective-permute-start(bf16[64,2048]{1,0:T(8,128)(2,1)} %get-tuple-element.420), channel_id=1, source_target_pairs={{0,2},{2,0},{4,6},{6,4},{8,10},{10,8},{12,14},{14,12},{16,18},{18,... | collective-permute-start | bytes 786440 | tf_op jit(solution)/shard_map/ppermute | solution.py:477
  481.1 55.7 %collective-permute-start.85 = (bf16[64,2048]{1,0:T(8,128)(2,1)}, bf16[64,2048]{1,0:T(8,128)(2,1)}, u32[]{:S(2)}, u32[]{:S(2)}) collective-permute-start(bf16[64,2048]{1,0:T(8,128)(2,1)} %get-tuple-element.419), channel_id=1, source_target_pairs={{0,4},{2,6},{4,0},{6,2},{8,12},{10,14},{12,8},{14,10},{16,20},{18,... | collective-permute-start | bytes 786440 | tf_op jit(solution)/shard_map/ppermute | solution.py:477
  487.4 47.9 %collective-permute-start.89 = (f32[2,2048]{1,0:T(2,128)S(1)}, f32[2,2048]{1,0:T(2,128)S(1)}, u32[]{:S(2)}, u32[]{:S(2)}) collective-permute-start(f32[2,2048]{1,0:T(2,128)S(1)} %reshape.291), channel_id=1, source_target_pairs={{0,1},{1,0},{2,3},{3,2},{4,5},{5,4},{6,7},{7,6},{8,9},{9,8},{10,11... | collective-permute-start | bytes 49160 | tf_op jit(solution)/shard_map/ppermute | solution.py:480
  (105 other events, 967.2 us)
Sparse Core Ops, SparseCore 0:
  153.2 102.4 all-gather.4
  283.0 107.8 all-gather.6
  421.1 112.1 reduce-scatter.1

commit v5 on v4

--- a/solution.py
+++ b/solution.py
@@ -620,7 +620,7 @@
         (mix_blocks,) = call(
             mix_blocks_kernel, [((groups, heads, depth, 5 * HEAD_DIM), BF16)], (mix_weight, out_weight), us=2
         )
-        mix_blocks = after(mix_blocks.reshape(peers, depth, 5 * HEAD_DIM), *other)
+        mix_blocks = mix_blocks.reshape(peers, depth, 5 * HEAD_DIM)
         mix_own = lax.all_to_all(mix_blocks, "seq", 0, 0, tiled=True).reshape(width, 5 * HEAD_DIM)
         (feed_blocks,) = call(
             feed_blocks_kernel,
@@ -629,7 +629,6 @@
             [pltpu.VMEM((heads * units, depth), BF16)],
             us=3,
         )
-        feed = group.spread(after(feed_blocks, mix_own))
         projected, tail = call(
             functools.partial(project_kernel, members=heads),
             [((length, 4 * HEAD_DIM), BF16), ((16, 3 * HEAD_DIM), BF16)],
@@ -638,6 +637,7 @@
             ids,
         )
         halo = group.shift(tail, 1)
+        feed = group.spread(after(feed_blocks, halo))
         conv, query, key, totals, states, mixed_here, last = call(
             forward_kernel,
             [

time: 573 us -> 556 us (0.970)
  waiting for transfers between devices: 313 us -> 297 us
    all_to_all x1, waiting for transfers between devices: 56.9 us -> 0.01 us  [start_steps(): lax.all_to_all(mix_blocks, 'seq', 0, 0, tiled=True)]
    ppermute x49, waiting for transfers between devices: 158 us -> 200 us  [swap(): lax.ppermute(value, 'seq', [(s, s ^ bits) for s in range(self.peers)])]
  transfers between devices with their start and end apart: 100 -> 100, of which waited for: 41 -> 41; matrix products, arithmetic and copies ran while one was open for 6% -> 7% of each run, Pallas kernels for 12% -> 10%
where the time goes in v5:
time: 556 us; the launch traced here: 547 us
  waiting for transfers between devices  297 us (53%)
  starting transfers between devices  93.6 us (17%)
  Pallas kernels  88 us (16%)
  other arithmetic  34.4 us (6%)
  local copies, waits for them, and re-layouts  18.4 us (3%)
  between operations  14.6 us (3%)
    ppermute x49, waiting for transfers between devices, swap(): lax.ppermute(value, 'seq', [(s, s ^ bits) for s in range(self.peers)])  200 us
    pallas_call x15, Pallas kernels, call(): pl.pallas_call(body, out_shape=[jax.ShapeDtypeStruct(s, d) for s, d in ou...  88 us
    ppermute x49, starting transfers between devices, swap(): lax.ppermute(value, 'seq', [(s, s ^ bits) for s in range(self.peers)])  49.6 us
    all_to_all x1, waiting for transfers between devices, shards(): lax.all_to_all(after(grad_mix, feed_away), 'seq', 0, 0, tiled=True)  42.1 us
    ppermute x4, waiting for transfers between devices, shift(): return lax.ppermute(value, 'seq', pairs)  27.8 us
    ppermute x40, waiting for transfers between devices, other_core(): return lax.ppermute(value, 'head', [(0, 1), (1, 0)])  16.6 us
    unnamed x42, local copies, waits for them, and re-layouts  11.2 us
  transfers between devices with their start and end apart: 100, of which 41 were waited for; matrix products, arithmetic and copies ran while one was open for 7% of the time, Pallas kernels for 10%

profile of v5, /device:TPU:18, one launch (start us, length us, event | category | flops | bytes accessed | tf_op | source)
XLA Modules:
  0.0 546.6 jit_solution(7120222622791574743)
XLA Ops:
  11.5 126.8 %conditional.3 = (bf16[64,2048]{1,0:T(8,128)(2,1)S(1)}, bf16[64,2048]{1,0:T(8,128)(2,1)}, bf16[64,2048]{1,0:T(8,128)(2,1)}, bf16[64,2048]{1,0:T(8,128)(2,1)}, bf...) conditional(s32[]{:T(128)} %convert_element_type.395, () %tuple.41, ...), branch_computations={%region_1.0_spmd, %region_2.0_spmd} | conditional | flops 2048 | bytes 102546208 | solution.py:563
  14.7 7.1 %all-to-all-start = ((bf16[16,128,640]{2,1,0:T(8,128)(2,1)}), bf16[16,128,640]{2,1,0:T(8,128)(2,1)}, u32[]{:S(2)}, u32[]{:S(2)}) async-start(bf16[16,128,640]{2,1,0:T(8,128)(2,1)} %bitcast), calls=%async_computation | async-start | bytes 5242880 | tf_op jit(solution)/shard_map/cond/branch_1_fun/all_to_all | solution.py:624
  25.3 46.2 %collective-permute-done.3.refs_5_ = bf16[64,2048]{1,0:T(8,128)(2,1)S(1)} collective-permute-done((bf16[64,2048]{1,0:T(8,128)(2,1)S(1)}, bf16[64,2048]{1,0:T(8,128)(2,1)S(1)}, u32[]{:S(2)}, u32[]{:S(2)}) %collective-permute-start.3) | collective-permute-done | bytes 262176 | tf_op jit(solution)/shard_map/cond/branch_1_fun/ppermute | solution.py:477
  90.9 5.8 %branch_1_fun.11 = (bf16[1024,512]{1,0:T(8,128)(2,1)}, bf16[16,384]{1,0:T(8,128)(2,1)S(1)}) custom-call(s32[2]{0:T(128)S(1)} %get-tuple-element.122.refs_0_, bf16[64,2048]{1,0:T(8,128)(2,1)} %copy-done.45, bf16[64,2048]{1,0:T(8,128)(2,1)S(1)} %collective-permute-done.refs_2_, bf16[64,2048]{1,0:T(8,128)(2,1)S(1)} %collective-permute-done.1.refs_3_, ...), custom_call_target="tpu_custom_call" | custom-call | bytes 15000000 | tf_op jit(solution)/shard_map/cond/branch_1_fun/pallas_call | solution.py:453
  103.3 6.2 %all-to-all-start.1 = ((bf16[8,1056,128]{2,1,0:T(8,128)(2,1)}), bf16[8,1056,128]{2,1,0:T(8,128)(2,1)}, u32[]{:S(2)}, u32[]{:S(2)}) async-start(bf16[8,1056,128]{2,1,0:T(8,128)(2,1)} %branch_1_fun.9), calls=%async_computation.1 | async-start | bytes 4325376 | tf_op jit(solution)/shard_map/cond/branch_1_fun/all_to_all | solution.py:524
  109.6 7.3 %branch_1_fun.12 = (f32[1024,384]{1,0:T(8,128)}, f32[1024,128]{1,0:T(8,128)S(1)}, f32[1024,128]{1,0:T(8,128)}, f32[8,128]{1,0:T(8,128)}, f32[8,128,128]{2,1,0:T(...) custom-call(bf16[1024,512]{1,0:T(8,128)(2,1)} %get-tuple-element.474.refs_0_, ...), custom_call_target="tpu_custom_call" | custom-call | bytes 15000000 | tf_op jit(solution)/shard_map/cond/branch_1_fun/pallas_call | solution.py:453
  119.7 18.6 %collective-permute-done.16 = f32[128,128]{1,0:T(8,128)} collective-permute-done((f32[128,128]{1,0:T(8,128)S(1)}, f32[128,128]{1,0:T(8,128)}, u32[]{:S(2)}, u32[]{:S(2)}) %collective-permute-start.16) | collective-permute-done | bytes 65568 | tf_op jit(solution)/shard_map/cond/branch_1_fun/ppermute | solution.py:485
  139.7 90.4 %conditional.4 = (f32[8,128,128]{2,1,0:T(8,128)S(1)}, f32[1024,128]{1,0:T(8,128)S(1)}, bf16[64,2048]{1,0:T(8,128)(2,1)}, bf16[64,2048]{1,0:T(8,128)(2,1)}, bf16[...) conditional(s32[]{:T(128)} %convert_element_type.395, () %tuple.40, ...), branch_computations={%region_3.0_spmd, %region_4.6_spmd} | conditional | flops 6685377 | bytes 72423696 | solution.py:563
  151.9 6.2 %collective-permute-done.44 = bf16[64,2048]{1,0:T(8,128)(2,1)S(1)} collective-permute-done((bf16[64,2048]{1,0:T(8,128)(2,1)S(1)}, bf16[64,2048]{1,0:T(8,128)(2,1)S(1)}, u32[]{:S(2)}, u32[]{:S(2)}) %collective-permute-start.44) | collective-permute-done | bytes 262176 | tf_op jit(solution)/shard_map/cond/branch_1_fun/ppermute | solution.py:477
  168.8 7.4 %collective-permute-done.68 = bf16[64,2048]{1,0:T(8,128)(2,1)} collective-permute-done((bf16[64,2048]{1,0:T(8,128)(2,1)S(1)}, bf16[64,2048]{1,0:T(8,128)(2,1)}, u32[]{:S(2)}, u32[]{:S(2)}) %collective-permute-start.68) | collective-permute-done | bytes 262176 | tf_op jit(solution)/shard_map/cond/branch_1_fun/ppermute | solution.py:477
  179.7 6.5 %collective-permute-done.49 = bf16[64,2048]{1,0:T(8,128)(2,1)S(1)} collective-permute-done((bf16[64,2048]{1,0:T(8,128)(2,1)S(1)}, bf16[64,2048]{1,0:T(8,128)(2,1)S(1)}, u32[]{:S(2)}, u32[]{:S(2)}) %collective-permute-start.49) | collective-permute-done | bytes 262176 | tf_op jit(solution)/shard_map/cond/branch_1_fun/ppermute | solution.py:477
  201.2 10.1 %collective-permute-done.53 = bf16[64,2048]{1,0:T(8,128)(2,1)} collective-permute-done((bf16[64,2048]{1,0:T(8,128)(2,1)}, bf16[64,2048]{1,0:T(8,128)(2,1)}, u32[]{:S(2)}, u32[]{:S(2)}) %collective-permute-start.53) | collective-permute-done | bytes 262176 | tf_op jit(solution)/shard_map/cond/branch_1_fun/ppermute | solution.py:477
  230.9 10.0 %all-gather.5.cloned.1.call-done = bf16[16,1056,128]{2,1,0:T(8,128)(2,1)} async-done(((bf16[8,1056,128]{2,1,0:T(8,128)(2,1)}), bf16[16,1056,128]{2,1,0:T(8,128)(2,1)}) %all-gather.5.cloned.1.call-update) | async-done | bytes 4325392 | tf_op jit(solution)/shard_map/all_gather | solution.py:527
  243.2 15.5 %shard_map.206 = (bf16[1152,1024]{1,0:T(8,128)(2,1)S(1)}, bf16[1024,384]{1,0:T(8,128)(2,1)S(1)}, bf16[8,64,2048]{2,1,0:T(8,128)(2,1)}, bf16[8,64,2048]{2,1,0:T(8,128)(2,1)S(1)}) custom-call(bf16[64,2048]{1,0:T(8,128)(2,1)} %get-tuple-element.308.refs_0_.refs_1_, bf16[64,2048]{1,0:T(8,128)(2,1)} %get-tuple-element.309.refs_1_.refs_2_, ...), custom_call_target="tpu_custom_call" | custom-call | bytes 51000000 | tf_op jit(solution)/shard_map/pallas_call | solution.py:453
  259.6 7.2 %shard_map.207 = bf16[8,1056,128]{2,1,0:T(8,128)(2,1)} custom-call(s32[4]{0:T(128)S(1)} %pad_add_fusion.3.refs_0_, bf16[64,2048]{1,0:T(8,128)(2,1)} %get-tuple-element.308.refs_0_.refs_1_, bf16[64,2048]{1,0:T(8,128)(2,1)} %get-tuple-element.309.refs_1_.refs_2_, bf16[64,2048]{1,0:T(8,128)(2,1)} %get-tuple-element.310.refs_2_.refs_3_, ...), custom_call_target="tpu_custom_call" | custom-call | bytes 21000000 | tf_op jit(solution)/shard_map/pallas_call | solution.py:453
  272.4 106.8 %conditional.5 = (f32[64,2048]{1,0:T(8,128)}, bf16[16,688,128]{2,1,0:T(8,128)(2,1)}, bf16[8,64,2048]{2,1,0:T(8,128)(2,1)}) conditional(s32[]{:T(128)} %convert_element_type.395, () %tuple.44, (bf16[64,2048]{1,0:T(8,128)(2,1)}, f32[64,1]{0,1:T(1,128)}, bf16[8,64,2048]{2,1,0:T(8,128)(2,1)}, bf16[8,64,2048]{2,1,0:T(8,128)(2,1)S(1)}, ...), branch_computations={%region_6.7_spmd, %region_7.10_spmd} | conditional | flops 12006528 | bytes 168937408 | solution.py:563
  296.7 10.1 %collective-permute-done.23 = bf16[64,2048]{1,0:T(8,128)(2,1)S(1)} collective-permute-done((bf16[64,2048]{1,0:T(8,128)(2,1)S(1)}, bf16[64,2048]{1,0:T(8,128)(2,1)S(1)}, u32[]{:S(2)}, u32[]{:S(2)}) %collective-permute-start.23) | collective-permute-done | bytes 262176 | tf_op jit(solution)/shard_map/cond/branch_1_fun/ppermute | solution.py:477
  313.3 9.6 %collective-permute-done.27.refs_5_.refs_21_ = bf16[64,2048]{1,0:T(8,128)(2,1)S(1)} collective-permute-done((bf16[64,2048]{1,0:T(8,128)(2,1)S(1)}, bf16[64,2048]{1,0:T(8,128)(2,1)S(1)}, u32[]{:S(2)}, u32[]{:S(2)}) %collective-permute-start.27) | collective-permute-done | bytes 262176 | tf_op jit(solution)/shard_map/cond/branch_1_fun/ppermute | solution.py:477
  350.5 9.7 %branch_1_fun.15 = (bf16[1024,384]{1,0:T(8,128)(2,1)S(1)}, f32[16,384]{1,0:T(8,128)S(1)}, f32[8,384]{1,0:T(8,128)S(1)}, f32[16,128]{1,0:T(8,128)S(1)}) custom-call(f32[1024,128]{1,0:T(8,128)S(1)} %get-tuple-element.185.refs_0_, f32[1024,384]{1,0:T(8,128)S(1)} %copy-done.9, f32[1024,128]{1,0:T(8,128)S(1)} %get-tuple-element.183.refs_21_.refs_2_, ...), custom_call_target="tpu_custom_call" | custom-call | bytes 24000000 | tf_op jit(solution)/shard_map/cond/branch_1_fun/pallas_call | solution.py:453
  379.3 8.0 %all-to-all-start.2 = ((bf16[16,688,128]{2,1,0:T(8,128)(2,1)}), bf16[16,688,128]{2,1,0:T(8,128)(2,1)S(1)}, u32[]{:S(2)}, u32[]{:S(2)}) async-start(bf16[16,688,128]{2,1,0:T(8,128)(2,1)} %get-tuple-element.372.refs_35_), calls=%async_computation.2 | async-start | bytes 5636096 | tf_op jit(solution)/shard_map/all_to_all | solution.py:770
  391.3 7.5 %shard_map.208.refs_2_ = bf16[8,1056,128]{2,1,0:T(8,128)(2,1)} custom-call(s32[4]{0:T(128)S(1)} %pad_add_fusion.1.refs_0_, bf16[64,2048]{1,0:T(8,128)(2,1)} %get-tuple-element.308.refs_0_.refs_1_, bf16[64,2048]{1,0:T(8,128)(2,1)} %get-tuple-element.309.refs_1_.refs_2_, bf16[64,2048]{1,0:T(8,128)(2,1)} %get-tuple-element.310.refs_2_.refs_3_, ...), custom_call_target="tpu_custom_call" | custom-call | bytes 24000000 | tf_op jit(solution)/shard_map/pallas_call | solution.py:453
  415.1 42.1 %all-to-all-done.2 = bf16[16,688,128]{2,1,0:T(8,128)(2,1)S(1)} async-done(((bf16[16,688,128]{2,1,0:T(8,128)(2,1)}), bf16[16,688,128]{2,1,0:T(8,128)(2,1)S(1)}, u32[]{:S(2)}, u32[]{:S(2)}) %all-to-all-start.2) | async-done | bytes 2818080 | tf_op jit(solution)/shard_map/all_to_all | solution.py:770
  470.6 43.7 %collective-permute-done.88 = bf16[64,2048]{1,0:T(8,128)(2,1)} collective-permute-done((bf16[64,2048]{1,0:T(8,128)(2,1)}, bf16[64,2048]{1,0:T(8,128)(2,1)}, u32[]{:S(2)}, u32[]{:S(2)}) %collective-permute-start.88) | collective-permute-done | bytes 262176 | tf_op jit(solution)/shard_map/ppermute | solution.py:477
  519.9 7.0 %collective-permute-done.90 = bf16[64,2048]{1,0:T(8,128)(2,1)S(1)} collective-permute-done((bf16[64,2048]{1,0:T(8,128)(2,1)}, bf16[64,2048]{1,0:T(8,128)(2,1)S(1)}, u32[]{:S(2)}, u32[]{:S(2)}) %collective-permute-start.90) | collective-permute-done | bytes 262176 | tf_op jit(solution)/shard_map/ppermute | solution.py:477
  (385 shorter events, 239.6 us)
Async XLA Ops:
  7.2 233.8 %all-gather.5.cloned.1.call-start = ((), (), s32[]{:S(2)}) async-start(), calls=%async_computation.6 | async-start | bytes 6488064 | tf_op jit(solution)/shard_map/all_gather | solution.py:527
  14.7 76.1 %all-to-all-start = ((bf16[16,128,640]{2,1,0:T(8,128)(2,1)}), bf16[16,128,640]{2,1,0:T(8,128)(2,1)}, u32[]{:S(2)}, u32[]{:S(2)}) async-start(bf16[16,128,640]{2,1,0:T(8,128)(2,1)} %bitcast), calls=%async_computation | async-start | bytes 5242880 | tf_op jit(solution)/shard_map/cond/branch_1_fun/all_to_all | solution.py:624
  21.8 49.7 %collective-permute-start.3 = (bf16[64,2048]{1,0:T(8,128)(2,1)S(1)}, bf16[64,2048]{1,0:T(8,128)(2,1)S(1)}, u32[]{:S(2)}, u32[]{:S(2)}) collective-permute-start(bf16[64,2048]{1,0:T(8,128)(2,1)S(1)} %get-tuple-element.456.refs_1_), channel_id=1, source_target_pairs={{0,8},{2,10},{4,12},{6,14},{8,0},{10,2},{12,4},{14,6},{16,24},{18,... | collective-permute-start | bytes 786440 | tf_op jit(solution)/shard_map/cond/branch_1_fun/ppermute | solution.py:477
  23.3 51.6 %collective-permute-start.1 = (bf16[64,2048]{1,0:T(8,128)(2,1)S(1)}, bf16[64,2048]{1,0:T(8,128)(2,1)S(1)}, u32[]{:S(2)}, u32[]{:S(2)}) collective-permute-start(bf16[64,2048]{1,0:T(8,128)(2,1)S(1)} %get-tuple-element.456.refs_1_), channel_id=1, source_target_pairs={{0,4},{2,6},{4,0},{6,2},{8,12},{10,14},{12,8},{14,10},{16,20},{18,... | collective-permute-start | bytes 786440 | tf_op jit(solution)/shard_map/cond/branch_1_fun/ppermute | solution.py:477
  24.8 50.5 %collective-permute-start = (bf16[64,2048]{1,0:T(8,128)(2,1)S(1)}, bf16[64,2048]{1,0:T(8,128)(2,1)S(1)}, u32[]{:S(2)}, u32[]{:S(2)}) collective-permute-start(bf16[64,2048]{1,0:T(8,128)(2,1)S(1)} %get-tuple-element.456.refs_1_), channel_id=1, source_target_pairs={{0,2},{2,0},{4,6},{6,4},{8,10},{10,8},{12,14},{14,12},{16,18},{18,... | collective-permute-start | bytes 786440 | tf_op jit(solution)/shard_map/cond/branch_1_fun/ppermute | solution.py:477
  25.3 50.0 %collective-permute-start.7 = (bf16[64,2048]{1,0:T(8,128)(2,1)S(1)}, bf16[64,2048]{1,0:T(8,128)(2,1)S(1)}, u32[]{:S(2)}, u32[]{:S(2)}) collective-permute-start(bf16[64,2048]{1,0:T(8,128)(2,1)S(1)} %get-tuple-element.456.refs_1_), channel_id=1, source_target_pairs={{0,1},{1,0},{2,3},{3,2},{4,5},{5,4},{6,7},{7,6},{8,9},{9,8},{10,11... | collective-permute-start | bytes 786440 | tf_op jit(solution)/shard_map/cond/branch_1_fun/ppermute | solution.py:480
  103.3 35.0 %all-to-all-start.1 = ((bf16[8,1056,128]{2,1,0:T(8,128)(2,1)}), bf16[8,1056,128]{2,1,0:T(8,128)(2,1)}, u32[]{:S(2)}, u32[]{:S(2)}) async-start(bf16[8,1056,128]{2,1,0:T(8,128)(2,1)} %branch_1_fun.9), calls=%async_computation.1 | async-start | bytes 4325376 | tf_op jit(solution)/shard_map/cond/branch_1_fun/all_to_all | solution.py:524
  116.9 21.4 %collective-permute-start.16 = (f32[128,128]{1,0:T(8,128)S(1)}, f32[128,128]{1,0:T(8,128)}, u32[]{:S(2)}, u32[]{:S(2)}) collective-permute-start(f32[128,128]{1,0:T(8,128)S(1)} %slice.138), channel_id=1, source_target_pairs={{0,16},{2,18},{4,20},{6,22},{8,24},{10,26},{12,28},{14,30},{1,17},... | collective-permute-start | bytes 196616 | tf_op jit(solution)/shard_map/cond/branch_1_fun/ppermute | solution.py:485
  138.4 240.9 %all-gather.7.cloned.1.call-start = ((), (), s32[]{:S(2)}) async-start(), calls=%async_computation.7 | async-start | bytes 6488064 | tf_op jit(solution)/shard_map/all_gather | solution.py:527
  161.3 14.9 %collective-permute-start.68 = (bf16[64,2048]{1,0:T(8,128)(2,1)S(1)}, bf16[64,2048]{1,0:T(8,128)(2,1)}, u32[]{:S(2)}, u32[]{:S(2)}) collective-permute-start(bf16[64,2048]{1,0:T(8,128)(2,1)S(1)} %get-tuple-element.540), channel_id=1, source_target_pairs={{0,8},{2,10},{4,12},{6,14},{8,0},{10,2},{12,4},{14,6},{16,24},{18,... | collective-permute-start | bytes 786440 | tf_op jit(solution)/shard_map/cond/branch_1_fun/ppermute | solution.py:477
  161.3 14.9 %collective-permute-start.66 = (bf16[64,2048]{1,0:T(8,128)(2,1)S(1)}, bf16[64,2048]{1,0:T(8,128)(2,1)}, u32[]{:S(2)}, u32[]{:S(2)}) collective-permute-start(bf16[64,2048]{1,0:T(8,128)(2,1)S(1)} %get-tuple-element.540), channel_id=1, source_target_pairs={{0,4},{2,6},{4,0},{6,2},{8,12},{10,14},{12,8},{14,10},{16,20},{18,... | collective-permute-start | bytes 786440 | tf_op jit(solution)/shard_map/cond/branch_1_fun/ppermute | solution.py:477
  168.7 17.5 %collective-permute-start.49 = (bf16[64,2048]{1,0:T(8,128)(2,1)S(1)}, bf16[64,2048]{1,0:T(8,128)(2,1)S(1)}, u32[]{:S(2)}, u32[]{:S(2)}) collective-permute-start(bf16[64,2048]{1,0:T(8,128)(2,1)S(1)} %fusion.1), channel_id=1, source_target_pairs={{0,8},{2,10},{4,12},{6,14},{8,0},{10,2},{12,4},{14,6},{16,24},{18,... | collective-permute-start | bytes 786440 | tf_op jit(solution)/shard_map/cond/branch_1_fun/ppermute | solution.py:477
  196.4 14.9 %collective-permute-start.53 = (bf16[64,2048]{1,0:T(8,128)(2,1)}, bf16[64,2048]{1,0:T(8,128)(2,1)}, u32[]{:S(2)}, u32[]{:S(2)}) collective-permute-start(bf16[64,2048]{1,0:T(8,128)(2,1)} %multiply_convert_fusion), channel_id=1, source_target_pairs={{0,8},{2,10},{4,12},{6,14},{8,0},{10,2},{12,4},{14,6},{16,24},{18,... | collective-permute-start | bytes 786440 | tf_op jit(solution)/shard_map/cond/branch_1_fun/ppermute | solution.py:477
  311.8 14.5 %collective-permute-start.24 = (bf16[64,2048]{1,0:T(8,128)(2,1)S(1)}, bf16[64,2048]{1,0:T(8,128)(2,1)S(1)}, u32[]{:S(2)}, u32[]{:S(2)}) collective-permute-start(bf16[64,2048]{1,0:T(8,128)(2,1)S(1)} %get-tuple-element.395.refs_1_.refs_17_), channel_id=1, source_target_pairs={{0,2},{2,0},{4,6},{6,4},{8,10},{10,8},{12,14},{14,12},{16,18},{18,... | collective-permute-start | bytes 786440 | tf_op jit(solution)/shard_map/cond/branch_1_fun/ppermute | solution.py:477
  379.3 77.9 %all-to-all-start.2 = ((bf16[16,688,128]{2,1,0:T(8,128)(2,1)}), bf16[16,688,128]{2,1,0:T(8,128)(2,1)S(1)}, u32[]{:S(2)}, u32[]{:S(2)}) async-start(bf16[16,688,128]{2,1,0:T(8,128)(2,1)} %get-tuple-element.372.refs_35_), calls=%async_computation.2 | async-start | bytes 5636096 | tf_op jit(solution)/shard_map/all_to_all | solution.py:770
  387.2 141.2 %reduce-scatter.2.cloned.1.call-start = ((), (), s32[]{:S(2)}) async-start(), calls=%async_computation.5 | async-start | bytes 2359296 | tf_op jit(solution)/shard_map/reduce_scatter | solution.py:769
  411.1 50.7 %collective-permute-start.84 = (bf16[64,2048]{1,0:T(8,128)(2,1)}, bf16[64,2048]{1,0:T(8,128)(2,1)}, u32[]{:S(2)}, u32[]{:S(2)}) collective-permute-start(bf16[64,2048]{1,0:T(8,128)(2,1)} %get-tuple-element.417), channel_id=1, source_target_pairs={{0,2},{2,0},{4,6},{6,4},{8,10},{10,8},{12,14},{14,12},{16,18},{18,... | collective-permute-start | bytes 786440 | tf_op jit(solution)/shard_map/ppermute | solution.py:477
  411.6 50.2 %collective-permute-start.87 = (bf16[64,2048]{1,0:T(8,128)(2,1)}, bf16[64,2048]{1,0:T(8,128)(2,1)}, u32[]{:S(2)}, u32[]{:S(2)}) collective-permute-start(bf16[64,2048]{1,0:T(8,128)(2,1)} %get-tuple-element.415), channel_id=1, source_target_pairs={{0,4},{2,6},{4,0},{6,2},{8,12},{10,14},{12,8},{14,10},{16,20},{18,... | collective-permute-start | bytes 786440 | tf_op jit(solution)/shard_map/ppermute | solution.py:477
  413.1 57.5 %collective-permute-start.86 = (bf16[64,2048]{1,0:T(8,128)(2,1)}, bf16[64,2048]{1,0:T(8,128)(2,1)}, u32[]{:S(2)}, u32[]{:S(2)}) collective-permute-start(bf16[64,2048]{1,0:T(8,128)(2,1)} %get-tuple-element.416), channel_id=1, source_target_pairs={{0,4},{2,6},{4,0},{6,2},{8,12},{10,14},{12,8},{14,10},{16,20},{18,... | collective-permute-start | bytes 786440 | tf_op jit(solution)/shard_map/ppermute | solution.py:477
  413.6 106.3 %collective-permute-start.83 = (bf16[64,2048]{1,0:T(8,128)(2,1)}, bf16[64,2048]{1,0:T(8,128)(2,1)}, u32[]{:S(2)}, u32[]{:S(2)}) collective-permute-start(bf16[64,2048]{1,0:T(8,128)(2,1)} %get-tuple-element.414), channel_id=1, source_target_pairs={{0,2},{2,0},{4,6},{6,4},{8,10},{10,8},{12,14},{14,12},{16,18},{18,... | collective-permute-start | bytes 786440 | tf_op jit(solution)/shard_map/ppermute | solution.py:477
  457.2 78.3 %all-to-all-start.3 = ((bf16[8,1056,128]{2,1,0:T(8,128)(2,1)}), bf16[8,1056,128]{2,1,0:T(8,128)(2,1)}, u32[]{:S(2)}, u32[]{:S(2)}) async-start(bf16[8,1056,128]{2,1,0:T(8,128)(2,1)} %shard_map.208.refs_2_), calls=%async_computation.4 | async-start | bytes 4325376 | tf_op jit(solution)/shard_map/all_to_all | solution.py:524
  464.2 50.1 %collective-permute-start.88 = (bf16[64,2048]{1,0:T(8,128)(2,1)}, bf16[64,2048]{1,0:T(8,128)(2,1)}, u32[]{:S(2)}, u32[]{:S(2)}) collective-permute-start(bf16[64,2048]{1,0:T(8,128)(2,1)} %get-tuple-element.419), channel_id=1, source_target_pairs={{0,2},{2,0},{4,6},{6,4},{8,10},{10,8},{12,14},{14,12},{16,18},{18,... | collective-permute-start | bytes 786440 | tf_op jit(solution)/shard_map/ppermute | solution.py:477
  464.2 55.7 %collective-permute-start.85 = (bf16[64,2048]{1,0:T(8,128)(2,1)}, bf16[64,2048]{1,0:T(8,128)(2,1)}, u32[]{:S(2)}, u32[]{:S(2)}) collective-permute-start(bf16[64,2048]{1,0:T(8,128)(2,1)} %get-tuple-element.418), channel_id=1, source_target_pairs={{0,4},{2,6},{4,0},{6,2},{8,12},{10,14},{12,8},{14,10},{16,20},{18,... | collective-permute-start | bytes 786440 | tf_op jit(solution)/shard_map/ppermute | solution.py:477
  470.5 47.9 %collective-permute-start.89 = (f32[2,2048]{1,0:T(2,128)S(1)}, f32[2,2048]{1,0:T(2,128)S(1)}, u32[]{:S(2)}, u32[]{:S(2)}) collective-permute-start(f32[2,2048]{1,0:T(2,128)S(1)} %reshape.291), channel_id=1, source_target_pairs={{0,1},{1,0},{2,3},{3,2},{4,5},{5,4},{6,7},{7,6},{8,9},{9,8},{10,11... | collective-permute-start | bytes 49160 | tf_op jit(solution)/shard_map/ppermute | solution.py:480
  (138 other events, 1387.0 us)
Sparse Core Ops, SparseCore 0:
  138.5 102.4 all-gather.4
  268.3 107.8 all-gather.6
  404.2 112.1 reduce-scatter.1

commit v6 on v5

--- a/solution.py
+++ b/solution.py
@@ -772,7 +772,8 @@
     (block_mine, block_away) = call(
         block_kernel, [all_rows, all_rows], (inner, feed_own), [pltpu.VMEM((wide, width), BF16)], None, (feed_total,)
     )
-    feed_got = group.spread(after(feed_total, mix_got))
+    block_half = hidden + group.scatter(block_mine, group.other_core(block_away))
+    feed_got = group.spread(after(feed_total, mix_got, block_half))
     mix_total, out_total = call(
         mix_total_kernel,
         [((4, depth, heads * HEAD_DIM), F32), ((heads * HEAD_DIM, depth), F32)],
@@ -783,9 +784,6 @@
     own_sums = sums[:, : 14 * HEAD_DIM].reshape(heads, 14, HEAD_DIM).transpose(1, 0, 2).reshape(14, heads * HEAD_DIM)
     norms = sums[:, 14 * HEAD_DIM : 14 * HEAD_DIM + 2 * width].sum(0).reshape(2, width)
     norms = norms + group.other_core(norms)
-    block_half = hidden + group.scatter(
-        block_mine, group.other_core(block_away), (mix_total, out_total, own_sums, norms)
-    )
     grad_normed1 = after(grad_normed1, block_half).astype(F32)
     grad_rows1 = norm_back(half_tokens, half_inverse1, norm1_gain, grad_normed1)[0]
     grad_tokens = grad_hidden + grad_rows1

time: 556 us -> 547 us (0.984)
  waiting for transfers between devices: 297 us -> 290 us
    all_to_all x1, waiting for transfers between devices: 42.1 us -> 0.01 us  [shards(): lax.all_to_all(after(grad_mix, feed_away), 'seq', 0, 0, tiled=True)]
    ppermute x49, waiting for transfers between devices: 200 us -> 223 us  [swap(): lax.ppermute(value, 'seq', [(s, s ^ bits) for s in range(self.peers)])]
    all_to_all x2, waiting for transfers between devices: 0.01 us -> 11.4 us  [spread(): lax.all_to_all(blocks, 'seq', 0, 0, axis_index_groups=self.lists, tiled=T...]
    unnamed x42 -> x46, local copies, waits for them, and re-layouts: 11.2 us -> 11.3 us
  transfers between devices with their start and end apart: 100 -> 100, of which waited for: 41 -> 43; matrix products, arithmetic and copies ran while one was open for 7% -> 6% of each run, Pallas kernels for 10% -> 10%
where the time goes in v6:
time: 547 us; the launch traced here: 539 us
  waiting for transfers between devices  290 us (53%)
  starting transfers between devices  94 us (17%)
  Pallas kernels  89 us (16%)
  other arithmetic  34 us (6%)
  local copies, waits for them, and re-layouts  16.6 us (3%)
  between operations  14.5 us (3%)
    ppermute x49, waiting for transfers between devices, swap(): lax.ppermute(value, 'seq', [(s, s ^ bits) for s in range(self.peers)])  223 us
    pallas_call x15, Pallas kernels, call(): pl.pallas_call(body, out_shape=[jax.ShapeDtypeStruct(s, d) for s, d in ou...  89 us
    ppermute x49, starting transfers between devices, swap(): lax.ppermute(value, 'seq', [(s, s ^ bits) for s in range(self.peers)])  49.6 us
    ppermute x4, waiting for transfers between devices, shift(): return lax.ppermute(value, 'seq', pairs)  27.8 us
    ppermute x40, waiting for transfers between devices, other_core(): return lax.ppermute(value, 'head', [(0, 1), (1, 0)])  18.3 us
    all_to_all x2, waiting for transfers between devices, spread(): lax.all_to_all(blocks, 'seq', 0, 0, axis_index_groups=self.lists, tiled=T...  11.4 us
    unnamed x46, local copies, waits for them, and re-layouts  11.3 us
    all_to_all x2, starting transfers between devices, spread(): lax.all_to_all(blocks, 'seq', 0, 0, axis_index_groups=self.lists, tiled=T...  11.1 us
  transfers between devices with their start and end apart: 100, of which 43 were waited for; matrix products, arithmetic and copies ran while one was open for 6% of the time, Pallas kernels for 10%

profile of v6, /device:TPU:18, one launch (start us, length us, event | category | flops | bytes accessed | tf_op | source)
XLA Modules:
  0.0 539.0 jit_solution(14414202762635055024)
XLA Ops:
  12.2 127.1 %conditional.3 = (bf16[64,2048]{1,0:T(8,128)(2,1)S(1)}, bf16[64,2048]{1,0:T(8,128)(2,1)S(1)}, bf16[64,2048]{1,0:T(8,128)(2,1)S(1)}, bf16[64,2048]{1,0:T(8,128)(2...) conditional(s32[]{:T(128)} %convert_element_type.395, () %tuple.39, ...), branch_computations={%region_1.0_spmd, %region_2.0_spmd} | conditional | flops 2048 | bytes 103594808 | solution.py:563
  15.5 7.2 %all-to-all-start = ((bf16[16,128,640]{2,1,0:T(8,128)(2,1)}), bf16[16,128,640]{2,1,0:T(8,128)(2,1)}, u32[]{:S(2)}, u32[]{:S(2)}) async-start(bf16[16,128,640]{2,1,0:T(8,128)(2,1)} %bitcast), calls=%async_computation | async-start | bytes 5242880 | tf_op jit(solution)/shard_map/cond/branch_1_fun/all_to_all | solution.py:624
  26.3 46.1 %collective-permute-done.3.refs_5_ = bf16[64,2048]{1,0:T(8,128)(2,1)S(1)} collective-permute-done((bf16[64,2048]{1,0:T(8,128)(2,1)S(1)}, bf16[64,2048]{1,0:T(8,128)(2,1)S(1)}, u32[]{:S(2)}, u32[]{:S(2)}) %collective-permute-start.3) | collective-permute-done | bytes 262176 | tf_op jit(solution)/shard_map/cond/branch_1_fun/ppermute | solution.py:477
  104.3 6.2 %all-to-all-start.1 = ((bf16[8,1056,128]{2,1,0:T(8,128)(2,1)}), bf16[8,1056,128]{2,1,0:T(8,128)(2,1)}, u32[]{:S(2)}, u32[]{:S(2)}) async-start(bf16[8,1056,128]{2,1,0:T(8,128)(2,1)} %branch_1_fun.9), calls=%async_computation.1 | async-start | bytes 4325376 | tf_op jit(solution)/shard_map/cond/branch_1_fun/all_to_all | solution.py:524
  110.5 7.3 %branch_1_fun.12 = (f32[1024,384]{1,0:T(8,128)}, f32[1024,128]{1,0:T(8,128)S(1)}, f32[1024,128]{1,0:T(8,128)}, f32[8,128]{1,0:T(8,128)}, f32[8,128,128]{2,1,0:T(...) custom-call(bf16[1024,512]{1,0:T(8,128)(2,1)} %get-tuple-element.472.refs_0_, ...), custom_call_target="tpu_custom_call" | custom-call | bytes 15000000 | tf_op jit(solution)/shard_map/cond/branch_1_fun/pallas_call | solution.py:453
  120.6 18.6 %collective-permute-done.16 = f32[128,128]{1,0:T(8,128)} collective-permute-done((f32[128,128]{1,0:T(8,128)S(1)}, f32[128,128]{1,0:T(8,128)}, u32[]{:S(2)}, u32[]{:S(2)}) %collective-permute-start.16) | collective-permute-done | bytes 65568 | tf_op jit(solution)/shard_map/cond/branch_1_fun/ppermute | solution.py:485
  140.6 90.5 %conditional.4 = (f32[8,128,128]{2,1,0:T(8,128)S(1)}, f32[1024,128]{1,0:T(8,128)S(1)}, bf16[64,2048]{1,0:T(8,128)(2,1)}, bf16[64,2048]{1,0:T(8,128)(2,1)}, bf16[...) conditional(s32[]{:T(128)} %convert_element_type.395, () %tuple.38, ...), branch_computations={%region_3.0_spmd, %region_4.6_spmd} | conditional | flops 6685377 | bytes 72423696 | solution.py:563
  153.0 6.2 %collective-permute-done.44 = bf16[64,2048]{1,0:T(8,128)(2,1)S(1)} collective-permute-done((bf16[64,2048]{1,0:T(8,128)(2,1)S(1)}, bf16[64,2048]{1,0:T(8,128)(2,1)S(1)}, u32[]{:S(2)}, u32[]{:S(2)}) %collective-permute-start.44) | collective-permute-done | bytes 262176 | tf_op jit(solution)/shard_map/cond/branch_1_fun/ppermute | solution.py:477
  169.9 7.4 %collective-permute-done.68 = bf16[64,2048]{1,0:T(8,128)(2,1)} collective-permute-done((bf16[64,2048]{1,0:T(8,128)(2,1)S(1)}, bf16[64,2048]{1,0:T(8,128)(2,1)}, u32[]{:S(2)}, u32[]{:S(2)}) %collective-permute-start.68) | collective-permute-done | bytes 262176 | tf_op jit(solution)/shard_map/cond/branch_1_fun/ppermute | solution.py:477
  180.8 6.5 %collective-permute-done.49 = bf16[64,2048]{1,0:T(8,128)(2,1)S(1)} collective-permute-done((bf16[64,2048]{1,0:T(8,128)(2,1)S(1)}, bf16[64,2048]{1,0:T(8,128)(2,1)S(1)}, u32[]{:S(2)}, u32[]{:S(2)}) %collective-permute-start.49) | collective-permute-done | bytes 262176 | tf_op jit(solution)/shard_map/cond/branch_1_fun/ppermute | solution.py:477
  202.3 10.1 %collective-permute-done.53 = bf16[64,2048]{1,0:T(8,128)(2,1)} collective-permute-done((bf16[64,2048]{1,0:T(8,128)(2,1)}, bf16[64,2048]{1,0:T(8,128)(2,1)}, u32[]{:S(2)}, u32[]{:S(2)}) %collective-permute-start.53) | collective-permute-done | bytes 262176 | tf_op jit(solution)/shard_map/cond/branch_1_fun/ppermute | solution.py:477
  232.1 9.8 %all-gather.5.cloned.1.call-done = bf16[16,1056,128]{2,1,0:T(8,128)(2,1)} async-done(((bf16[8,1056,128]{2,1,0:T(8,128)(2,1)}), bf16[16,1056,128]{2,1,0:T(8,128)(2,1)}) %all-gather.5.cloned.1.call-update) | async-done | bytes 4325392 | tf_op jit(solution)/shard_map/all_gather | solution.py:527
  244.1 15.5 %shard_map.206 = (bf16[1152,1024]{1,0:T(8,128)(2,1)S(1)}, bf16[1024,384]{1,0:T(8,128)(2,1)S(1)}, bf16[8,64,2048]{2,1,0:T(8,128)(2,1)}, bf16[8,64,2048]{2,1,0:T(8,128)(2,1)S(1)}) custom-call(bf16[64,2048]{1,0:T(8,128)(2,1)} %get-tuple-element.307.refs_0_.refs_1_, bf16[64,2048]{1,0:T(8,128)(2,1)} %get-tuple-element.308.refs_1_.refs_2_, ...), custom_call_target="tpu_custom_call" | custom-call | bytes 51000000 | tf_op jit(solution)/shard_map/pallas_call | solution.py:453
  260.6 7.2 %shard_map.207 = bf16[8,1056,128]{2,1,0:T(8,128)(2,1)} custom-call(s32[4]{0:T(128)S(1)} %pad_add_fusion.3.refs_0_, bf16[64,2048]{1,0:T(8,128)(2,1)} %get-tuple-element.307.refs_0_.refs_1_, bf16[64,2048]{1,0:T(8,128)(2,1)} %get-tuple-element.308.refs_1_.refs_2_, bf16[64,2048]{1,0:T(8,128)(2,1)} %get-tuple-element.309.refs_2_.refs_3_, ...), custom_call_target="tpu_custom_call" | custom-call | bytes 21000000 | tf_op jit(solution)/shard_map/pallas_call | solution.py:453
  273.4 107.6 %conditional.5 = (f32[64,2048]{1,0:T(8,128)}, bf16[16,688,128]{2,1,0:T(8,128)(2,1)}, bf16[8,64,2048]{2,1,0:T(8,128)(2,1)}) conditional(s32[]{:T(128)} %convert_element_type.395, () %tuple.42, (bf16[64,2048]{1,0:T(8,128)(2,1)}, f32[64,1]{0,1:T(1,128)}, bf16[8,64,2048]{2,1,0:T(8,128)(2,1)}, bf16[8,64,2048]{2,1,0:T(8,128)(2,1)S(1)}, ...), branch_computations={%region_6.7_spmd, %region_7.10_spmd} | conditional | flops 12006528 | bytes 159500096 | solution.py:563
  297.7 10.1 %collective-permute-done.23 = bf16[64,2048]{1,0:T(8,128)(2,1)S(1)} collective-permute-done((bf16[64,2048]{1,0:T(8,128)(2,1)S(1)}, bf16[64,2048]{1,0:T(8,128)(2,1)S(1)}, u32[]{:S(2)}, u32[]{:S(2)}) %collective-permute-start.23) | collective-permute-done | bytes 262176 | tf_op jit(solution)/shard_map/cond/branch_1_fun/ppermute | solution.py:477
  314.2 9.6 %collective-permute-done.27.refs_5_.refs_21_ = bf16[64,2048]{1,0:T(8,128)(2,1)S(1)} collective-permute-done((bf16[64,2048]{1,0:T(8,128)(2,1)S(1)}, bf16[64,2048]{1,0:T(8,128)(2,1)S(1)}, u32[]{:S(2)}, u32[]{:S(2)}) %collective-permute-start.27) | collective-permute-done | bytes 262176 | tf_op jit(solution)/shard_map/cond/branch_1_fun/ppermute | solution.py:477
  351.4 10.1 %branch_1_fun.15 = (bf16[1024,384]{1,0:T(8,128)(2,1)S(1)}, f32[16,384]{1,0:T(8,128)S(1)}, f32[8,384]{1,0:T(8,128)S(1)}, f32[16,128]{1,0:T(8,128)S(1)}) custom-call(f32[1024,128]{1,0:T(8,128)S(1)} %get-tuple-element.185.refs_0_, f32[1024,384]{1,0:T(8,128)} %get-tuple-element.186.refs_1_, f32[1024,128]{1,0:T(8,128)S(1)} %get-tuple-element.183.refs_21_.refs_2_, ...), custom_call_target="tpu_custom_call" | custom-call | bytes 24000000 | tf_op jit(solution)/shard_map/cond/branch_1_fun/pallas_call | solution.py:453
  381.0 8.0 %all-to-all-start.2 = ((bf16[16,688,128]{2,1,0:T(8,128)(2,1)}), bf16[16,688,128]{2,1,0:T(8,128)(2,1)S(1)}, u32[]{:S(2)}, u32[]{:S(2)}) async-start(bf16[16,688,128]{2,1,0:T(8,128)(2,1)} %get-tuple-element.374.refs_35_), calls=%async_computation.3 | async-start | bytes 5636096 | tf_op jit(solution)/shard_map/all_to_all | solution.py:770
  392.9 7.4 %shard_map.208.refs_2_ = bf16[8,1056,128]{2,1,0:T(8,128)(2,1)} custom-call(s32[4]{0:T(128)S(1)} %pad_add_fusion.1.refs_0_, bf16[64,2048]{1,0:T(8,128)(2,1)} %get-tuple-element.307.refs_0_.refs_1_, bf16[64,2048]{1,0:T(8,128)(2,1)} %get-tuple-element.308.refs_1_.refs_2_, bf16[64,2048]{1,0:T(8,128)(2,1)} %get-tuple-element.309.refs_2_.refs_3_, ...), custom_call_target="tpu_custom_call" | custom-call | bytes 24000000 | tf_op jit(solution)/shard_map/pallas_call | solution.py:453
  414.6 41.9 %collective-permute-done.84 = bf16[64,2048]{1,0:T(8,128)(2,1)S(1)} collective-permute-done((bf16[64,2048]{1,0:T(8,128)(2,1)S(1)}, bf16[64,2048]{1,0:T(8,128)(2,1)S(1)}, u32[]{:S(2)}, u32[]{:S(2)}) %collective-permute-start.84) | collective-permute-done | bytes 262176 | tf_op jit(solution)/shard_map/ppermute | solution.py:477
  459.9 16.7 %collective-permute-done.88 = bf16[64,2048]{1,0:T(8,128)(2,1)S(1)} collective-permute-done((bf16[64,2048]{1,0:T(8,128)(2,1)S(1)}, bf16[64,2048]{1,0:T(8,128)(2,1)S(1)}, u32[]{:S(2)}, u32[]{:S(2)}) %collective-permute-start.88) | collective-permute-done | bytes 262176 | tf_op jit(solution)/shard_map/ppermute | solution.py:477
  477.8 14.6 %collective-permute-done.83 = bf16[64,2048]{1,0:T(8,128)(2,1)S(1)} collective-permute-done((bf16[64,2048]{1,0:T(8,128)(2,1)S(1)}, bf16[64,2048]{1,0:T(8,128)(2,1)S(1)}, u32[]{:S(2)}, u32[]{:S(2)}) %collective-permute-start.83) | collective-permute-done | bytes 262176 | tf_op jit(solution)/shard_map/ppermute | solution.py:477
  516.5 11.4 %all-to-all-done.3.refs_0_ = bf16[8,1056,128]{2,1,0:T(8,128)(2,1)} async-done(((bf16[8,1056,128]{2,1,0:T(8,128)(2,1)}), bf16[8,1056,128]{2,1,0:T(8,128)(2,1)}, u32[]{:S(2)}, u32[]{:S(2)}) %all-to-all-start.3) | async-done | bytes 2162720 | tf_op jit(solution)/shard_map/all_to_all | solution.py:524
  (383 shorter events, 245.8 us)
Async XLA Ops:
  7.2 234.7 %all-gather.5.cloned.1.call-start = ((), (), s32[]{:S(2)}) async-start(), calls=%async_computation.6 | async-start | bytes 6488064 | tf_op jit(solution)/shard_map/all_gather | solution.py:527
  15.5 76.3 %all-to-all-start = ((bf16[16,128,640]{2,1,0:T(8,128)(2,1)}), bf16[16,128,640]{2,1,0:T(8,128)(2,1)}, u32[]{:S(2)}, u32[]{:S(2)}) async-start(bf16[16,128,640]{2,1,0:T(8,128)(2,1)} %bitcast), calls=%async_computation | async-start | bytes 5242880 | tf_op jit(solution)/shard_map/cond/branch_1_fun/all_to_all | solution.py:624
  22.7 49.7 %collective-permute-start.3 = (bf16[64,2048]{1,0:T(8,128)(2,1)S(1)}, bf16[64,2048]{1,0:T(8,128)(2,1)S(1)}, u32[]{:S(2)}, u32[]{:S(2)}) collective-permute-start(bf16[64,2048]{1,0:T(8,128)(2,1)S(1)} %copy-done.46), channel_id=1, source_target_pairs={{0,8},{2,10},{4,12},{6,14},{8,0},{10,2},{12,4},{14,6},{16,24},{18,... | collective-permute-start | bytes 786440 | tf_op jit(solution)/shard_map/cond/branch_1_fun/ppermute | solution.py:477
  24.3 51.6 %collective-permute-start.1 = (bf16[64,2048]{1,0:T(8,128)(2,1)S(1)}, bf16[64,2048]{1,0:T(8,128)(2,1)S(1)}, u32[]{:S(2)}, u32[]{:S(2)}) collective-permute-start(bf16[64,2048]{1,0:T(8,128)(2,1)S(1)} %copy-done.46), channel_id=1, source_target_pairs={{0,4},{2,6},{4,0},{6,2},{8,12},{10,14},{12,8},{14,10},{16,20},{18,... | collective-permute-start | bytes 786440 | tf_op jit(solution)/shard_map/cond/branch_1_fun/ppermute | solution.py:477
  25.7 50.5 %collective-permute-start = (bf16[64,2048]{1,0:T(8,128)(2,1)S(1)}, bf16[64,2048]{1,0:T(8,128)(2,1)S(1)}, u32[]{:S(2)}, u32[]{:S(2)}) collective-permute-start(bf16[64,2048]{1,0:T(8,128)(2,1)S(1)} %copy-done.46), channel_id=1, source_target_pairs={{0,2},{2,0},{4,6},{6,4},{8,10},{10,8},{12,14},{14,12},{16,18},{18,... | collective-permute-start | bytes 786440 | tf_op jit(solution)/shard_map/cond/branch_1_fun/ppermute | solution.py:477
  26.3 49.9 %collective-permute-start.7 = (bf16[64,2048]{1,0:T(8,128)(2,1)S(1)}, bf16[64,2048]{1,0:T(8,128)(2,1)S(1)}, u32[]{:S(2)}, u32[]{:S(2)}) collective-permute-start(bf16[64,2048]{1,0:T(8,128)(2,1)S(1)} %copy-done.46), channel_id=1, source_target_pairs={{0,1},{1,0},{2,3},{3,2},{4,5},{5,4},{6,7},{7,6},{8,9},{9,8},{10,11... | collective-permute-start | bytes 786440 | tf_op jit(solution)/shard_map/cond/branch_1_fun/ppermute | solution.py:480
  104.3 35.0 %all-to-all-start.1 = ((bf16[8,1056,128]{2,1,0:T(8,128)(2,1)}), bf16[8,1056,128]{2,1,0:T(8,128)(2,1)}, u32[]{:S(2)}, u32[]{:S(2)}) async-start(bf16[8,1056,128]{2,1,0:T(8,128)(2,1)} %branch_1_fun.9), calls=%async_computation.1 | async-start | bytes 4325376 | tf_op jit(solution)/shard_map/cond/branch_1_fun/all_to_all | solution.py:524
  117.8 21.4 %collective-permute-start.16 = (f32[128,128]{1,0:T(8,128)S(1)}, f32[128,128]{1,0:T(8,128)}, u32[]{:S(2)}, u32[]{:S(2)}) collective-permute-start(f32[128,128]{1,0:T(8,128)S(1)} %slice.138), channel_id=1, source_target_pairs={{0,16},{2,18},{4,20},{6,22},{8,24},{10,26},{12,28},{14,30},{1,17},... | collective-permute-start | bytes 196616 | tf_op jit(solution)/shard_map/cond/branch_1_fun/ppermute | solution.py:485
  139.3 241.6 %all-gather.7.cloned.1.call-start = ((), (), s32[]{:S(2)}) async-start(), calls=%async_computation.7 | async-start | bytes 6488064 | tf_op jit(solution)/shard_map/all_gather | solution.py:527
  162.4 14.9 %collective-permute-start.68 = (bf16[64,2048]{1,0:T(8,128)(2,1)S(1)}, bf16[64,2048]{1,0:T(8,128)(2,1)}, u32[]{:S(2)}, u32[]{:S(2)}) collective-permute-start(bf16[64,2048]{1,0:T(8,128)(2,1)S(1)} %get-tuple-element.538), channel_id=1, source_target_pairs={{0,8},{2,10},{4,12},{6,14},{8,0},{10,2},{12,4},{14,6},{16,24},{18,... | collective-permute-start | bytes 786440 | tf_op jit(solution)/shard_map/cond/branch_1_fun/ppermute | solution.py:477
  162.4 14.9 %collective-permute-start.66 = (bf16[64,2048]{1,0:T(8,128)(2,1)S(1)}, bf16[64,2048]{1,0:T(8,128)(2,1)}, u32[]{:S(2)}, u32[]{:S(2)}) collective-permute-start(bf16[64,2048]{1,0:T(8,128)(2,1)S(1)} %get-tuple-element.538), channel_id=1, source_target_pairs={{0,4},{2,6},{4,0},{6,2},{8,12},{10,14},{12,8},{14,10},{16,20},{18,... | collective-permute-start | bytes 786440 | tf_op jit(solution)/shard_map/cond/branch_1_fun/ppermute | solution.py:477
  169.8 17.5 %collective-permute-start.49 = (bf16[64,2048]{1,0:T(8,128)(2,1)S(1)}, bf16[64,2048]{1,0:T(8,128)(2,1)S(1)}, u32[]{:S(2)}, u32[]{:S(2)}) collective-permute-start(bf16[64,2048]{1,0:T(8,128)(2,1)S(1)} %fusion.1), channel_id=1, source_target_pairs={{0,8},{2,10},{4,12},{6,14},{8,0},{10,2},{12,4},{14,6},{16,24},{18,... | collective-permute-start | bytes 786440 | tf_op jit(solution)/shard_map/cond/branch_1_fun/ppermute | solution.py:477
  197.5 14.9 %collective-permute-start.53 = (bf16[64,2048]{1,0:T(8,128)(2,1)}, bf16[64,2048]{1,0:T(8,128)(2,1)}, u32[]{:S(2)}, u32[]{:S(2)}) collective-permute-start(bf16[64,2048]{1,0:T(8,128)(2,1)} %multiply_convert_fusion), channel_id=1, source_target_pairs={{0,8},{2,10},{4,12},{6,14},{8,0},{10,2},{12,4},{14,6},{16,24},{18,... | collective-permute-start | bytes 786440 | tf_op jit(solution)/shard_map/cond/branch_1_fun/ppermute | solution.py:477
  312.8 14.5 %collective-permute-start.24 = (bf16[64,2048]{1,0:T(8,128)(2,1)S(1)}, bf16[64,2048]{1,0:T(8,128)(2,1)S(1)}, u32[]{:S(2)}, u32[]{:S(2)}) collective-permute-start(bf16[64,2048]{1,0:T(8,128)(2,1)S(1)} %get-tuple-element.393.refs_1_.refs_17_), channel_id=1, source_target_pairs={{0,2},{2,0},{4,6},{6,4},{8,10},{10,8},{12,14},{14,12},{16,18},{18,... | collective-permute-start | bytes 786440 | tf_op jit(solution)/shard_map/cond/branch_1_fun/ppermute | solution.py:477
  381.0 113.6 %all-to-all-start.2 = ((bf16[16,688,128]{2,1,0:T(8,128)(2,1)}), bf16[16,688,128]{2,1,0:T(8,128)(2,1)S(1)}, u32[]{:S(2)}, u32[]{:S(2)}) async-start(bf16[16,688,128]{2,1,0:T(8,128)(2,1)} %get-tuple-element.374.refs_35_), calls=%async_computation.3 | async-start | bytes 5636096 | tf_op jit(solution)/shard_map/all_to_all | solution.py:770
  388.9 110.5 %reduce-scatter.2.cloned.1.call-start = ((), (), s32[]{:S(2)}) async-start(), calls=%async_computation.5 | async-start | bytes 2359296 | tf_op jit(solution)/shard_map/reduce_scatter | solution.py:769
  411.9 44.5 %collective-permute-start.84 = (bf16[64,2048]{1,0:T(8,128)(2,1)S(1)}, bf16[64,2048]{1,0:T(8,128)(2,1)S(1)}, u32[]{:S(2)}, u32[]{:S(2)}) collective-permute-start(bf16[64,2048]{1,0:T(8,128)(2,1)S(1)} %get-tuple-element.415), channel_id=1, source_target_pairs={{0,2},{2,0},{4,6},{6,4},{8,10},{10,8},{12,14},{14,12},{16,18},{18,... | collective-permute-start | bytes 786440 | tf_op jit(solution)/shard_map/ppermute | solution.py:477
  412.5 43.9 %collective-permute-start.87 = (bf16[64,2048]{1,0:T(8,128)(2,1)S(1)}, bf16[64,2048]{1,0:T(8,128)(2,1)S(1)}, u32[]{:S(2)}, u32[]{:S(2)}) collective-permute-start(bf16[64,2048]{1,0:T(8,128)(2,1)S(1)} %get-tuple-element.413), channel_id=1, source_target_pairs={{0,4},{2,6},{4,0},{6,2},{8,12},{10,14},{12,8},{14,10},{16,20},{18,... | collective-permute-start | bytes 786440 | tf_op jit(solution)/shard_map/ppermute | solution.py:477
  414.0 45.9 %collective-permute-start.86 = (bf16[64,2048]{1,0:T(8,128)(2,1)S(1)}, bf16[64,2048]{1,0:T(8,128)(2,1)S(1)}, u32[]{:S(2)}, u32[]{:S(2)}) collective-permute-start(bf16[64,2048]{1,0:T(8,128)(2,1)S(1)} %get-tuple-element.414), channel_id=1, source_target_pairs={{0,4},{2,6},{4,0},{6,2},{8,12},{10,14},{12,8},{14,10},{16,20},{18,... | collective-permute-start | bytes 786440 | tf_op jit(solution)/shard_map/ppermute | solution.py:477
  457.7 19.0 %collective-permute-start.88 = (bf16[64,2048]{1,0:T(8,128)(2,1)S(1)}, bf16[64,2048]{1,0:T(8,128)(2,1)S(1)}, u32[]{:S(2)}, u32[]{:S(2)}) collective-permute-start(bf16[64,2048]{1,0:T(8,128)(2,1)S(1)} %get-tuple-element.417), channel_id=1, source_target_pairs={{0,2},{2,0},{4,6},{6,4},{8,10},{10,8},{12,14},{14,12},{16,18},{18,... | collective-permute-start | bytes 786440 | tf_op jit(solution)/shard_map/ppermute | solution.py:477
  457.8 34.7 %collective-permute-start.83 = (bf16[64,2048]{1,0:T(8,128)(2,1)S(1)}, bf16[64,2048]{1,0:T(8,128)(2,1)S(1)}, u32[]{:S(2)}, u32[]{:S(2)}) collective-permute-start(bf16[64,2048]{1,0:T(8,128)(2,1)S(1)} %get-tuple-element.412), channel_id=1, source_target_pairs={{0,2},{2,0},{4,6},{6,4},{8,10},{10,8},{12,14},{14,12},{16,18},{18,... | collective-permute-start | bytes 786440 | tf_op jit(solution)/shard_map/ppermute | solution.py:477
  459.8 32.7 %collective-permute-start.85 = (bf16[64,2048]{1,0:T(8,128)(2,1)S(1)}, bf16[64,2048]{1,0:T(8,128)(2,1)S(1)}, u32[]{:S(2)}, u32[]{:S(2)}) collective-permute-start(bf16[64,2048]{1,0:T(8,128)(2,1)S(1)} %get-tuple-element.416), channel_id=1, source_target_pairs={{0,4},{2,6},{4,0},{6,2},{8,12},{10,14},{12,8},{14,10},{16,20},{18,... | collective-permute-start | bytes 786440 | tf_op jit(solution)/shard_map/ppermute | solution.py:477
  477.8 14.7 %collective-permute-start.89 = (bf16[64,2048]{1,0:T(8,128)(2,1)S(1)}, bf16[64,2048]{1,0:T(8,128)(2,1)S(1)}, u32[]{:S(2)}, u32[]{:S(2)}) collective-permute-start(bf16[64,2048]{1,0:T(8,128)(2,1)S(1)} %fusion.31), channel_id=1, source_target_pairs={{0,8},{2,10},{4,12},{6,14},{8,0},{10,2},{12,4},{14,6},{16,24},{18,... | collective-permute-start | bytes 786440 | tf_op jit(solution)/shard_map/ppermute | solution.py:477
  494.6 33.3 %all-to-all-start.3 = ((bf16[8,1056,128]{2,1,0:T(8,128)(2,1)}), bf16[8,1056,128]{2,1,0:T(8,128)(2,1)}, u32[]{:S(2)}, u32[]{:S(2)}) async-start(bf16[8,1056,128]{2,1,0:T(8,128)(2,1)} %shard_map.208.refs_2_), calls=%async_computation.4 | async-start | bytes 4325376 | tf_op jit(solution)/shard_map/all_to_all | solution.py:524
  (137 other events, 1593.9 us)
Sparse Core Ops, SparseCore 0:
  139.4 102.4 all-gather.4
  269.3 107.8 all-gather.6
  405.8 89.1 reduce-scatter.1

commit v7 on v6

--- a/solution.py
+++ b/solution.py
@@ -768,10 +768,10 @@
     )
     grad_normed1 = lax.psum_scatter(both, "seq", axis_index_groups=group.lists)
     mix_got = lax.all_to_all(after(grad_mix, feed_away), "seq", 0, 0, tiled=True)
-    feed_total = group.over_groups(feed_grad, feed_args, feed_away, (grad_mix,), 8)
     (block_mine, block_away) = call(
-        block_kernel, [all_rows, all_rows], (inner, feed_own), [pltpu.VMEM((wide, width), BF16)], None, (feed_total,)
-    )
+        block_kernel, [all_rows, all_rows], (inner, feed_own), [pltpu.VMEM((wide, width), BF16)], None, (grad_mix,)
+    )
+    feed_total = group.over_groups(feed_grad, feed_args, feed_away, (block_mine,), 8)
     block_half = hidden + group.scatter(block_mine, group.other_core(block_away))
     feed_got = group.spread(after(feed_total, mix_got, block_half))
     mix_total, out_total = call(

time: 547 us -> 541 us (0.989)
  waiting for transfers between devices: 290 us -> 259 us
  starting transfers between devices: 94 us -> 117 us
    ppermute x49, waiting for transfers between devices: 223 us -> 193 us  [swap(): lax.ppermute(value, 'seq', [(s, s ^ bits) for s in range(self.peers)])]
    ppermute x49, starting transfers between devices: 49.6 us -> 76.1 us  [swap(): lax.ppermute(value, 'seq', [(s, s ^ bits) for s in range(self.peers)])]
  transfers between devices with their start and end apart: 100 -> 100, of which waited for: 43 -> 47; matrix products, arithmetic and copies ran while one was open for 6% -> 6% of each run, Pallas kernels for 10% -> 10%
where the time goes in v7:
time: 541 us; the launch traced here: 532 us
  waiting for transfers between devices  259 us (48%)
  starting transfers between devices  117 us (22%)
  Pallas kernels  87.1 us (16%)
  other arithmetic  34.2 us (6%)
  local copies, waits for them, and re-layouts  19.4 us (4%)
  between operations  14.6 us (3%)
    ppermute x49, waiting for transfers between devices, swap(): lax.ppermute(value, 'seq', [(s, s ^ bits) for s in range(self.peers)])  193 us
    pallas_call x15, Pallas kernels, call(): pl.pallas_call(body, out_shape=[jax.ShapeDtypeStruct(s, d) for s, d in ou...  87.1 us
    ppermute x49, starting transfers between devices, swap(): lax.ppermute(value, 'seq', [(s, s ^ bits) for s in range(self.peers)])  76.1 us
    ppermute x4, waiting for transfers between devices, shift(): return lax.ppermute(value, 'seq', pairs)  27.8 us
    ppermute x40, waiting for transfers between devices, other_core(): return lax.ppermute(value, 'head', [(0, 1), (1, 0)])  18 us
    unnamed x46, local copies, waits for them, and re-layouts  13.8 us
    all_to_all x2, waiting for transfers between devices, spread(): lax.all_to_all(blocks, 'seq', 0, 0, axis_index_groups=self.lists, tiled=T...  11.6 us
    ppermute x4, starting transfers between devices, shift(): return lax.ppermute(value, 'seq', pairs)  10.9 us
  transfers between devices with their start and end apart: 100, of which 47 were waited for; matrix products, arithmetic and copies ran while one was open for 6% of the time, Pallas kernels for 10%

profile of v7, /device:TPU:18, one launch (start us, length us, event | category | flops | bytes accessed | tf_op | source)
XLA Modules:
  0.0 532.1 jit_solution(4387050661937434653)
XLA Ops:
  12.2 128.5 %conditional.3 = (bf16[64,2048]{1,0:T(8,128)(2,1)}, bf16[64,2048]{1,0:T(8,128)(2,1)}, bf16[64,2048]{1,0:T(8,128)(2,1)}, bf16[64,2048]{1,0:T(8,128)(2,1)}, bf16[6...) conditional(s32[]{:T(128)} %convert_element_type.395, () %tuple.39, ...), branch_computations={%region_1.0_spmd, %region_2.0_spmd} | conditional | flops 2048 | bytes 119323368 | solution.py:563
  15.5 7.1 %all-to-all-start = ((bf16[16,128,640]{2,1,0:T(8,128)(2,1)}), bf16[16,128,640]{2,1,0:T(8,128)(2,1)S(1)}, u32[]{:S(2)}, u32[]{:S(2)}) async-start(bf16[16,128,640]{2,1,0:T(8,128)(2,1)} %bitcast), calls=%async_computation | async-start | bytes 5242880 | tf_op jit(solution)/shard_map/cond/branch_1_fun/all_to_all | solution.py:624
  26.0 46.2 %collective-permute-done.3.refs_5_ = bf16[64,2048]{1,0:T(8,128)(2,1)S(1)} collective-permute-done((bf16[64,2048]{1,0:T(8,128)(2,1)S(1)}, bf16[64,2048]{1,0:T(8,128)(2,1)S(1)}, u32[]{:S(2)}, u32[]{:S(2)}) %collective-permute-start.3) | collective-permute-done | bytes 262176 | tf_op jit(solution)/shard_map/cond/branch_1_fun/ppermute | solution.py:477
  92.9 6.4 %branch_1_fun.11 = (bf16[1024,512]{1,0:T(8,128)(2,1)}, bf16[16,384]{1,0:T(8,128)(2,1)S(1)}) custom-call(s32[2]{0:T(128)S(1)} %get-tuple-element.122.refs_0_, bf16[64,2048]{1,0:T(8,128)(2,1)} %copy-done.44, bf16[64,2048]{1,0:T(8,128)(2,1)} %copy-done.40, bf16[64,2048]{1,0:T(8,128)(2,1)} %copy-done.38, bf16[64,2048]{1,0:T(8,128)(2,1)} %copy-done.36, ...), custom_call_target="tpu_custom_call" | custom-call | bytes 15000000 | tf_op jit(solution)/shard_map/cond/branch_1_fun/pallas_call | solution.py:453
  111.7 7.6 %branch_1_fun.12 = (f32[1024,384]{1,0:T(8,128)}, f32[1024,128]{1,0:T(8,128)}, f32[1024,128]{1,0:T(8,128)}, f32[8,128]{1,0:T(8,128)}, f32[8,128,128]{2,1,0:T(8,12...) custom-call(bf16[1024,512]{1,0:T(8,128)(2,1)} %get-tuple-element.472.refs_0_, ...), custom_call_target="tpu_custom_call" | custom-call | bytes 15000000 | tf_op jit(solution)/shard_map/cond/branch_1_fun/pallas_call | solution.py:453
  122.1 18.6 %collective-permute-done.16 = f32[128,128]{1,0:T(8,128)} collective-permute-done((f32[128,128]{1,0:T(8,128)S(1)}, f32[128,128]{1,0:T(8,128)}, u32[]{:S(2)}, u32[]{:S(2)}) %collective-permute-start.16) | collective-permute-done | bytes 65568 | tf_op jit(solution)/shard_map/cond/branch_1_fun/ppermute | solution.py:485
  142.3 92.3 %conditional.4 = (f32[8,128,128]{2,1,0:T(8,128)}, f32[1024,128]{1,0:T(8,128)}, bf16[64,2048]{1,0:T(8,128)(2,1)}, bf16[64,2048]{1,0:T(8,128)(2,1)}, bf16[64,2048]...) conditional(s32[]{:T(128)} %convert_element_type.395, () %tuple.38, ...), branch_computations={%region_3.0_spmd, %region_4.6_spmd} | conditional | flops 6685377 | bytes 74520872 | solution.py:563
  153.9 7.1 %collective-permute-done.47 = bf16[64,2048]{1,0:T(8,128)(2,1)S(1)} collective-permute-done((bf16[64,2048]{1,0:T(8,128)(2,1)S(1)}, bf16[64,2048]{1,0:T(8,128)(2,1)S(1)}, u32[]{:S(2)}, u32[]{:S(2)}) %collective-permute-start.47) | collective-permute-done | bytes 262176 | tf_op jit(solution)/shard_map/cond/branch_1_fun/ppermute | solution.py:477
  179.8 7.7 %collective-permute-done.49 = bf16[64,2048]{1,0:T(8,128)(2,1)S(1)} collective-permute-done((bf16[64,2048]{1,0:T(8,128)(2,1)S(1)}, bf16[64,2048]{1,0:T(8,128)(2,1)S(1)}, u32[]{:S(2)}, u32[]{:S(2)}) %collective-permute-start.49) | collective-permute-done | bytes 262176 | tf_op jit(solution)/shard_map/cond/branch_1_fun/ppermute | solution.py:477
  204.4 10.8 %collective-permute-done.53 = bf16[64,2048]{1,0:T(8,128)(2,1)} collective-permute-done((bf16[64,2048]{1,0:T(8,128)(2,1)}, bf16[64,2048]{1,0:T(8,128)(2,1)}, u32[]{:S(2)}, u32[]{:S(2)}) %collective-permute-start.53) | collective-permute-done | bytes 262176 | tf_op jit(solution)/shard_map/cond/branch_1_fun/ppermute | solution.py:477
  234.7 8.7 %all-gather.5.cloned.1.call-done = bf16[16,1056,128]{2,1,0:T(8,128)(2,1)} async-done(((bf16[8,1056,128]{2,1,0:T(8,128)(2,1)}), bf16[16,1056,128]{2,1,0:T(8,128)(2,1)}) %all-gather.5.cloned.1.call-update) | async-done | bytes 4325392 | tf_op jit(solution)/shard_map/all_gather | solution.py:527
  245.6 15.5 %shard_map.206 = (bf16[1152,1024]{1,0:T(8,128)(2,1)S(1)}, bf16[1024,384]{1,0:T(8,128)(2,1)S(1)}, bf16[8,64,2048]{2,1,0:T(8,128)(2,1)}, bf16[8,64,2048]{2,1,0:T(8,128)(2,1)S(1)}) custom-call(bf16[64,2048]{1,0:T(8,128)(2,1)} %get-tuple-element.307.refs_0_.refs_1_, bf16[64,2048]{1,0:T(8,128)(2,1)} %get-tuple-element.308.refs_1_.refs_2_, ...), custom_call_target="tpu_custom_call" | custom-call | bytes 51000000 | tf_op jit(solution)/shard_map/pallas_call | solution.py:453
  262.0 7.1 %shard_map.208 = bf16[8,1056,128]{2,1,0:T(8,128)(2,1)} custom-call(s32[4]{0:T(128)S(1)} %pad_add_fusion.3.refs_0_, bf16[64,2048]{1,0:T(8,128)(2,1)} %get-tuple-element.307.refs_0_.refs_1_, bf16[64,2048]{1,0:T(8,128)(2,1)} %get-tuple-element.308.refs_1_.refs_2_, bf16[64,2048]{1,0:T(8,128)(2,1)} %get-tuple-element.309.refs_2_.refs_3_, ...), custom_call_target="tpu_custom_call" | custom-call | bytes 21000000 | tf_op jit(solution)/shard_map/pallas_call | solution.py:453
  274.8 109.2 %conditional.5 = (f32[64,2048]{1,0:T(8,128)}, bf16[16,688,128]{2,1,0:T(8,128)(2,1)}, bf16[8,64,2048]{2,1,0:T(8,128)(2,1)}) conditional(s32[]{:T(128)} %convert_element_type.395, () %tuple.42, (bf16[64,2048]{1,0:T(8,128)(2,1)S(1)}, f32[64,1]{0,1:T(1,128)}, bf16[8,64,2048]{2,1,0:T(8,128)(2,1)}, bf16[8,64,2048]{2,1,0:T(8,128)(2,1)S(1)}, ...), branch_computations={%region_6.7_spmd, %region_7.10_spmd} | conditional | flops 12006528 | bytes 157402720 | solution.py:563
  279.2 6.6 %collective-permute-done.21 = bf16[64,2048]{1,0:T(8,128)(2,1)S(1)} collective-permute-done((bf16[64,2048]{1,0:T(8,128)(2,1)S(1)}, bf16[64,2048]{1,0:T(8,128)(2,1)S(1)}, u32[]{:S(2)}, u32[]{:S(2)}) %collective-permute-start.21) | collective-permute-done | bytes 262176 | tf_op jit(solution)/shard_map/cond/branch_1_fun/ppermute | solution.py:477
  299.4 10.4 %collective-permute-done.23 = bf16[64,2048]{1,0:T(8,128)(2,1)S(1)} collective-permute-done((bf16[64,2048]{1,0:T(8,128)(2,1)S(1)}, bf16[64,2048]{1,0:T(8,128)(2,1)S(1)}, u32[]{:S(2)}, u32[]{:S(2)}) %collective-permute-start.23) | collective-permute-done | bytes 262176 | tf_op jit(solution)/shard_map/cond/branch_1_fun/ppermute | solution.py:477
  314.8 11.7 %collective-permute-done.27.refs_5_.refs_21_ = bf16[64,2048]{1,0:T(8,128)(2,1)S(1)} collective-permute-done((bf16[64,2048]{1,0:T(8,128)(2,1)S(1)}, bf16[64,2048]{1,0:T(8,128)(2,1)S(1)}, u32[]{:S(2)}, u32[]{:S(2)}) %collective-permute-start.27) | collective-permute-done | bytes 262176 | tf_op jit(solution)/shard_map/cond/branch_1_fun/ppermute | solution.py:477
  354.3 10.5 %branch_1_fun.15 = (bf16[1024,384]{1,0:T(8,128)(2,1)S(1)}, f32[16,384]{1,0:T(8,128)S(1)}, f32[8,384]{1,0:T(8,128)S(1)}, f32[16,128]{1,0:T(8,128)S(1)}) custom-call(f32[1024,128]{1,0:T(8,128)S(1)} %get-tuple-element.185.refs_0_, f32[1024,384]{1,0:T(8,128)} %get-tuple-element.186.refs_1_, f32[1024,128]{1,0:T(8,128)} %get-tuple-element.183.refs_21_.refs_2_, ...), custom_call_target="tpu_custom_call" | custom-call | bytes 24000000 | tf_op jit(solution)/shard_map/cond/branch_1_fun/pallas_call | solution.py:453
  384.0 7.7 %all-to-all-start.2 = ((bf16[16,688,128]{2,1,0:T(8,128)(2,1)}), bf16[16,688,128]{2,1,0:T(8,128)(2,1)S(1)}, u32[]{:S(2)}, u32[]{:S(2)}) async-start(bf16[16,688,128]{2,1,0:T(8,128)(2,1)} %get-tuple-element.374.refs_2_), calls=%async_computation.3 | async-start | bytes 5636096 | tf_op jit(solution)/shard_map/all_to_all | solution.py:770
  409.3 12.8 %collective-permute-done.87 = bf16[64,2048]{1,0:T(8,128)(2,1)S(1)} collective-permute-done((bf16[64,2048]{1,0:T(8,128)(2,1)S(1)}, bf16[64,2048]{1,0:T(8,128)(2,1)S(1)}, u32[]{:S(2)}, u32[]{:S(2)}) %collective-permute-start.87) | collective-permute-done | bytes 262176 | tf_op jit(solution)/shard_map/ppermute | solution.py:477
  425.7 32.3 %collective-permute-start.85 = (bf16[64,2048]{1,0:T(8,128)(2,1)S(1)}, bf16[64,2048]{1,0:T(8,128)(2,1)S(1)}, u32[]{:S(2)}, u32[]{:S(2)}) collective-permute-start(bf16[64,2048]{1,0:T(8,128)(2,1)S(1)} %get-tuple-element.416), channel_id=1, source_target_pairs={{0,4},{2,6},{4,0},{6,2},{8,12},{10,14},{12,8},{14,10},{16,20},{18,... | collective-permute-start | bytes 786440 | tf_op jit(solution)/shard_map/ppermute | solution.py:477
  458.0 10.9 %collective-permute-done.88 = bf16[64,2048]{1,0:T(8,128)(2,1)S(1)} collective-permute-done((bf16[64,2048]{1,0:T(8,128)(2,1)S(1)}, bf16[64,2048]{1,0:T(8,128)(2,1)S(1)}, u32[]{:S(2)}, u32[]{:S(2)}) %collective-permute-start.88) | collective-permute-done | bytes 262176 | tf_op jit(solution)/shard_map/ppermute | solution.py:477
  479.6 7.5 %collective-permute-done.83 = bf16[64,2048]{1,0:T(8,128)(2,1)S(1)} collective-permute-done((bf16[64,2048]{1,0:T(8,128)(2,1)S(1)}, bf16[64,2048]{1,0:T(8,128)(2,1)S(1)}, u32[]{:S(2)}, u32[]{:S(2)}) %collective-permute-start.83) | collective-permute-done | bytes 262176 | tf_op jit(solution)/shard_map/ppermute | solution.py:477
  509.3 11.6 %all-to-all-done.3.refs_0_ = bf16[8,1056,128]{2,1,0:T(8,128)(2,1)} async-done(((bf16[8,1056,128]{2,1,0:T(8,128)(2,1)}), bf16[8,1056,128]{2,1,0:T(8,128)(2,1)}, u32[]{:S(2)}, u32[]{:S(2)}) %all-to-all-start.3) | async-done | bytes 2162720 | tf_op jit(solution)/shard_map/all_to_all | solution.py:524
  (362 shorter events, 252.0 us)
Async XLA Ops:
  7.2 236.2 %all-gather.5.cloned.1.call-start = ((), (), s32[]{:S(2)}) async-start(), calls=%async_computation.6 | async-start | bytes 6488064 | tf_op jit(solution)/shard_map/all_gather | solution.py:527
  15.5 77.4 %all-to-all-start = ((bf16[16,128,640]{2,1,0:T(8,128)(2,1)}), bf16[16,128,640]{2,1,0:T(8,128)(2,1)S(1)}, u32[]{:S(2)}, u32[]{:S(2)}) async-start(bf16[16,128,640]{2,1,0:T(8,128)(2,1)} %bitcast), calls=%async_computation | async-start | bytes 5242880 | tf_op jit(solution)/shard_map/cond/branch_1_fun/all_to_all | solution.py:624
  22.5 49.7 %collective-permute-start.3 = (bf16[64,2048]{1,0:T(8,128)(2,1)S(1)}, bf16[64,2048]{1,0:T(8,128)(2,1)S(1)}, u32[]{:S(2)}, u32[]{:S(2)}) collective-permute-start(bf16[64,2048]{1,0:T(8,128)(2,1)S(1)} %get-tuple-element.454.refs_1_), channel_id=1, source_target_pairs={{0,8},{2,10},{4,12},{6,14},{8,0},{10,2},{12,4},{14,6},{16,24},{18,... | collective-permute-start | bytes 786440 | tf_op jit(solution)/shard_map/cond/branch_1_fun/ppermute | solution.py:477
  24.0 48.8 %collective-permute-start.7 = (bf16[64,2048]{1,0:T(8,128)(2,1)S(1)}, bf16[64,2048]{1,0:T(8,128)(2,1)S(1)}, u32[]{:S(2)}, u32[]{:S(2)}) collective-permute-start(bf16[64,2048]{1,0:T(8,128)(2,1)S(1)} %get-tuple-element.454.refs_1_), channel_id=1, source_target_pairs={{0,1},{1,0},{2,3},{3,2},{4,5},{5,4},{6,7},{7,6},{8,9},{9,8},{10,11... | collective-permute-start | bytes 786440 | tf_op jit(solution)/shard_map/cond/branch_1_fun/ppermute | solution.py:480
  24.0 51.7 %collective-permute-start.1 = (bf16[64,2048]{1,0:T(8,128)(2,1)S(1)}, bf16[64,2048]{1,0:T(8,128)(2,1)S(1)}, u32[]{:S(2)}, u32[]{:S(2)}) collective-permute-start(bf16[64,2048]{1,0:T(8,128)(2,1)S(1)} %get-tuple-element.454.refs_1_), channel_id=1, source_target_pairs={{0,4},{2,6},{4,0},{6,2},{8,12},{10,14},{12,8},{14,10},{16,20},{18,... | collective-permute-start | bytes 786440 | tf_op jit(solution)/shard_map/cond/branch_1_fun/ppermute | solution.py:477
  25.5 50.5 %collective-permute-start = (bf16[64,2048]{1,0:T(8,128)(2,1)S(1)}, bf16[64,2048]{1,0:T(8,128)(2,1)S(1)}, u32[]{:S(2)}, u32[]{:S(2)}) collective-permute-start(bf16[64,2048]{1,0:T(8,128)(2,1)S(1)} %get-tuple-element.454.refs_1_), channel_id=1, source_target_pairs={{0,2},{2,0},{4,6},{6,4},{8,10},{10,8},{12,14},{14,12},{16,18},{18,... | collective-permute-start | bytes 786440 | tf_op jit(solution)/shard_map/cond/branch_1_fun/ppermute | solution.py:477
  105.9 34.7 %all-to-all-start.1 = ((bf16[8,1056,128]{2,1,0:T(8,128)(2,1)}), bf16[8,1056,128]{2,1,0:T(8,128)(2,1)}, u32[]{:S(2)}, u32[]{:S(2)}) async-start(bf16[8,1056,128]{2,1,0:T(8,128)(2,1)} %branch_1_fun.9), calls=%async_computation.1 | async-start | bytes 4325376 | tf_op jit(solution)/shard_map/cond/branch_1_fun/all_to_all | solution.py:524
  119.3 21.4 %collective-permute-start.16 = (f32[128,128]{1,0:T(8,128)S(1)}, f32[128,128]{1,0:T(8,128)}, u32[]{:S(2)}, u32[]{:S(2)}) collective-permute-start(f32[128,128]{1,0:T(8,128)S(1)} %slice.138), channel_id=1, source_target_pairs={{0,16},{2,18},{4,20},{6,22},{8,24},{10,26},{12,28},{14,30},{1,17},... | collective-permute-start | bytes 196616 | tf_op jit(solution)/shard_map/cond/branch_1_fun/ppermute | solution.py:485
  140.7 243.3 %all-gather.7.cloned.1.call-start = ((), (), s32[]{:S(2)}) async-start(), calls=%async_computation.7 | async-start | bytes 6488064 | tf_op jit(solution)/shard_map/all_gather | solution.py:527
  162.1 15.7 %collective-permute-start.43 = (bf16[64,2048]{1,0:T(8,128)(2,1)S(1)}, bf16[64,2048]{1,0:T(8,128)(2,1)S(1)}, u32[]{:S(2)}, u32[]{:S(2)}) collective-permute-start(bf16[64,2048]{1,0:T(8,128)(2,1)S(1)} %get-tuple-element.400), channel_id=1, source_target_pairs={{0,2},{2,0},{4,6},{6,4},{8,10},{10,8},{12,14},{14,12},{16,18},{18,... | collective-permute-start | bytes 786440 | tf_op jit(solution)/shard_map/cond/branch_1_fun/ppermute | solution.py:477
  163.8 15.9 %collective-permute-start.45 = (bf16[64,2048]{1,0:T(8,128)(2,1)S(1)}, bf16[64,2048]{1,0:T(8,128)(2,1)S(1)}, u32[]{:S(2)}, u32[]{:S(2)}) collective-permute-start(bf16[64,2048]{1,0:T(8,128)(2,1)S(1)} %get-tuple-element.404), channel_id=1, source_target_pairs={{0,4},{2,6},{4,0},{6,2},{8,12},{10,14},{12,8},{14,10},{16,20},{18,... | collective-permute-start | bytes 786440 | tf_op jit(solution)/shard_map/cond/branch_1_fun/ppermute | solution.py:477
  171.2 16.3 %collective-permute-start.49 = (bf16[64,2048]{1,0:T(8,128)(2,1)S(1)}, bf16[64,2048]{1,0:T(8,128)(2,1)S(1)}, u32[]{:S(2)}, u32[]{:S(2)}) collective-permute-start(bf16[64,2048]{1,0:T(8,128)(2,1)S(1)} %fusion.1), channel_id=1, source_target_pairs={{0,8},{2,10},{4,12},{6,14},{8,0},{10,2},{12,4},{14,6},{16,24},{18,... | collective-permute-start | bytes 786440 | tf_op jit(solution)/shard_map/cond/branch_1_fun/ppermute | solution.py:477
  171.2 19.0 %collective-permute-start.72 = (bf16[64,2048]{1,0:T(8,128)(2,1)S(1)}, bf16[64,2048]{1,0:T(8,128)(2,1)}, u32[]{:S(2)}, u32[]{:S(2)}) collective-permute-start(bf16[64,2048]{1,0:T(8,128)(2,1)S(1)} %get-tuple-element.538), channel_id=1, source_target_pairs={{0,1},{1,0},{2,3},{3,2},{4,5},{5,4},{6,7},{7,6},{8,9},{9,8},{10,11... | collective-permute-start | bytes 786440 | tf_op jit(solution)/shard_map/cond/branch_1_fun/ppermute | solution.py:480
  202.6 15.6 %collective-permute-start.57 = (bf16[64,2048]{1,0:T(8,128)(2,1)}, bf16[64,2048]{1,0:T(8,128)(2,1)}, u32[]{:S(2)}, u32[]{:S(2)}) collective-permute-start(bf16[64,2048]{1,0:T(8,128)(2,1)} %multiply_convert_fusion), channel_id=1, source_target_pairs={{0,1},{1,0},{2,3},{3,2},{4,5},{5,4},{6,7},{7,6},{8,9},{9,8},{10,11... | collective-permute-start | bytes 786440 | tf_op jit(solution)/shard_map/cond/branch_1_fun/ppermute | solution.py:480
  203.1 16.1 %collective-permute-start.51 = (bf16[64,2048]{1,0:T(8,128)(2,1)}, bf16[64,2048]{1,0:T(8,128)(2,1)}, u32[]{:S(2)}, u32[]{:S(2)}) collective-permute-start(bf16[64,2048]{1,0:T(8,128)(2,1)} %multiply_convert_fusion), channel_id=1, source_target_pairs={{0,4},{2,6},{4,0},{6,2},{8,12},{10,14},{12,8},{14,10},{16,20},{18,... | collective-permute-start | bytes 786440 | tf_op jit(solution)/shard_map/cond/branch_1_fun/ppermute | solution.py:477
  384.0 105.1 %all-to-all-start.2 = ((bf16[16,688,128]{2,1,0:T(8,128)(2,1)}), bf16[16,688,128]{2,1,0:T(8,128)(2,1)S(1)}, u32[]{:S(2)}, u32[]{:S(2)}) async-start(bf16[16,688,128]{2,1,0:T(8,128)(2,1)} %get-tuple-element.374.refs_2_), calls=%async_computation.3 | async-start | bytes 5636096 | tf_op jit(solution)/shard_map/all_to_all | solution.py:770
  391.7 102.3 %reduce-scatter.2.cloned.1.call-start = ((), (), s32[]{:S(2)}) async-start(), calls=%async_computation.5 | async-start | bytes 2359296 | tf_op jit(solution)/shard_map/reduce_scatter | solution.py:769
  406.6 15.5 %collective-permute-start.87 = (bf16[64,2048]{1,0:T(8,128)(2,1)S(1)}, bf16[64,2048]{1,0:T(8,128)(2,1)S(1)}, u32[]{:S(2)}, u32[]{:S(2)}) collective-permute-start(bf16[64,2048]{1,0:T(8,128)(2,1)S(1)} %get-tuple-element.413), channel_id=1, source_target_pairs={{0,4},{2,6},{4,0},{6,2},{8,12},{10,14},{12,8},{14,10},{16,20},{18,... | collective-permute-start | bytes 786440 | tf_op jit(solution)/shard_map/ppermute | solution.py:477
  408.7 49.3 %collective-permute-start.86 = (bf16[64,2048]{1,0:T(8,128)(2,1)S(1)}, bf16[64,2048]{1,0:T(8,128)(2,1)S(1)}, u32[]{:S(2)}, u32[]{:S(2)}) collective-permute-start(bf16[64,2048]{1,0:T(8,128)(2,1)S(1)} %get-tuple-element.414), channel_id=1, source_target_pairs={{0,4},{2,6},{4,0},{6,2},{8,12},{10,14},{12,8},{14,10},{16,20},{18,... | collective-permute-start | bytes 786440 | tf_op jit(solution)/shard_map/ppermute | solution.py:477
  423.6 45.3 %collective-permute-start.88 = (bf16[64,2048]{1,0:T(8,128)(2,1)S(1)}, bf16[64,2048]{1,0:T(8,128)(2,1)S(1)}, u32[]{:S(2)}, u32[]{:S(2)}) collective-permute-start(bf16[64,2048]{1,0:T(8,128)(2,1)S(1)} %get-tuple-element.417), channel_id=1, source_target_pairs={{0,2},{2,0},{4,6},{6,4},{8,10},{10,8},{12,14},{14,12},{16,18},{18,... | collective-permute-start | bytes 786440 | tf_op jit(solution)/shard_map/ppermute | solution.py:477
  425.2 61.9 %collective-permute-start.83 = (bf16[64,2048]{1,0:T(8,128)(2,1)S(1)}, bf16[64,2048]{1,0:T(8,128)(2,1)S(1)}, u32[]{:S(2)}, u32[]{:S(2)}) collective-permute-start(bf16[64,2048]{1,0:T(8,128)(2,1)S(1)} %get-tuple-element.412), channel_id=1, source_target_pairs={{0,2},{2,0},{4,6},{6,4},{8,10},{10,8},{12,14},{14,12},{16,18},{18,... | collective-permute-start | bytes 786440 | tf_op jit(solution)/shard_map/ppermute | solution.py:477
  425.7 61.4 %collective-permute-start.85 = (bf16[64,2048]{1,0:T(8,128)(2,1)S(1)}, bf16[64,2048]{1,0:T(8,128)(2,1)S(1)}, u32[]{:S(2)}, u32[]{:S(2)}) collective-permute-start(bf16[64,2048]{1,0:T(8,128)(2,1)S(1)} %get-tuple-element.416), channel_id=1, source_target_pairs={{0,4},{2,6},{4,0},{6,2},{8,12},{10,14},{12,8},{14,10},{16,20},{18,... | collective-permute-start | bytes 786440 | tf_op jit(solution)/shard_map/ppermute | solution.py:477
  470.0 17.1 %collective-permute-start.89 = (bf16[64,2048]{1,0:T(8,128)(2,1)S(1)}, bf16[64,2048]{1,0:T(8,128)(2,1)S(1)}, u32[]{:S(2)}, u32[]{:S(2)}) collective-permute-start(bf16[64,2048]{1,0:T(8,128)(2,1)S(1)} %fusion.31), channel_id=1, source_target_pairs={{0,8},{2,10},{4,12},{6,14},{8,0},{10,2},{12,4},{14,6},{16,24},{18,... | collective-permute-start | bytes 786440 | tf_op jit(solution)/shard_map/ppermute | solution.py:477
  489.2 31.7 %all-to-all-start.3 = ((bf16[8,1056,128]{2,1,0:T(8,128)(2,1)}), bf16[8,1056,128]{2,1,0:T(8,128)(2,1)}, u32[]{:S(2)}, u32[]{:S(2)}) async-start(bf16[8,1056,128]{2,1,0:T(8,128)(2,1)} %copy-done.6), calls=%async_computation.4 | async-start | bytes 4325376 | tf_op jit(solution)/shard_map/all_to_all | solution.py:524
  (127 other events, 1404.6 us)
Sparse Core Ops, SparseCore 0:
  140.8 102.5 all-gather.4
  270.7 107.8 all-gather.6
  400.5 91.6 reduce-scatter.1
